TPU v7x, 32 devices: a whole 2x2x4 slice. The times are simulated.
32 devices in a mesh: tile: 16 (over z, y, core), depth: 2 (over x).
Axes of the slice: x: 2, y: 2, z: 4, core: 2. Of those that a mesh axis runs over, the one named last changes fastest.
Arguments:
- objects: float32 [2, 4, 2048, 256], P('depth', None, 'tile'), may hold values from 0.25 to 30, as said below
- observed: float32 [2, 4, 2048, 256], P('depth', None, 'tile'), may hold values from 0.25 to 30, as said below
- pupil_phase: float32 [2, 128, 128], P('depth'), may hold values from -319 to 319
- pupil_amplitude: float32 [2, 128, 128], P('depth'), may hold values from 0.25 to 1.75
Outputs:
- new_objects: float32 [2, 4, 2048, 256], P('depth', None, 'tile')
- new_phase: float32 [2, 128, 128], P('depth')
Inputs may be any that keep to these rules, and one draw needn't show every extreme that they name: `objects`: strictly positive intensities. `observed`: strictly positive intensities.
All inputs are finite; a program needn't handle non-finite values.
Results may differ from a plain program's by a relative error of at most 0.0001.
Values sent between devices are 32-bit elements; how exact they have to be, the bound alone decides.
No kernel may reach another device: no remote copies, remote signals or barrier semaphores. Data moves between devices by JAX's collectives and lax.ppermute only.
A program may use at most 64 MiB of HBM per device.

v0:
```python
import functools
import math

import jax
import jax.numpy as jnp
import ml_dtypes
import numpy as np
from jax import lax
from jax.experimental import pallas as pl
from jax.experimental.pallas import tpu as pltpu
from jax.sharding import PartitionSpec as P

HALF = 64
BACKGROUND = 0.1
STEP_SIZE = 0.3
EPSILON = 1e-06
STACKED = ("row_inverse",)
NEEDED_IN_ORDER = ("pupil_right", "pupil_left", "kernel_right")
VMEM_LIMIT = 32 * 1024 * 1024


def round_up(value, step):
    return -(-value // step) * step


def angles(left, right, length):
    return (2.0 * math.pi / length) * np.outer(left, right)


def halves(matrix):
    high = matrix.astype(np.float32).astype(ml_dtypes.bfloat16)
    low = (matrix - high.astype(np.float64)).astype(np.float32).astype(ml_dtypes.bfloat16)
    return high, low


def row_constants(rows, length):
    freqs = np.arange(length // 2) + 0.5
    theta = angles(freqs, np.arange(length), length)
    forward = np.concatenate([np.cos(theta), -np.sin(theta)], 0)
    inner = theta[:, HALF : HALF + rows]
    inverse = np.concatenate([np.cos(inner).T, -np.sin(inner).T], 1) * (2.0 / length)
    return forward, inverse


def col_constants(cols):
    half = cols // 2
    forward, inverse = [], []
    for parity in range(2):
        theta = angles(np.arange(half), 2 * np.arange(half) + parity, cols)
        c, s = np.cos(theta), np.sin(theta)
        forward.append(np.block([[c, -s], [s, c]]))
        inverse.append(np.block([[c.T, s.T], [-s.T, c.T]]) / cols)
    return forward, inverse


def kernel_constants(length, cols, ker, pad_rows, pad_cols):
    lags = np.arange(ker) - HALF
    theta = angles(np.arange(length // 2) + 0.5, lags, length)
    rows = np.zeros((length, pad_rows))
    rows[: length // 2, :ker] = np.cos(theta)
    rows[length // 2 :, :ker] = -np.sin(theta)
    half = cols // 2
    right = np.zeros((2 * pad_cols, 2 * cols))
    for parity in range(2):
        theta = angles(lags, 2 * np.arange(half) + parity, cols)
        c, s = np.cos(theta), np.sin(theta)
        at = parity * cols
        right[:ker, at : at + half] = c
        right[:ker, at + half : at + cols] = -s
        right[pad_cols : pad_cols + ker, at : at + half] = s
        right[pad_cols : pad_cols + ker, at + half : at + cols] = c
    return rows, right


def pupil_constants(pup, ker, pad_rows, pad_cols):
    theta = angles(np.arange(ker) - HALF, np.arange(pup), ker)
    real, imag = np.cos(theta), -np.sin(theta)
    right = np.zeros((2 * pup, 2 * pad_cols))
    right[:pup, :ker] = real.T
    right[:pup, pad_cols : pad_cols + ker] = imag.T
    right[pup:, :ker] = -imag.T
    right[pup:, pad_cols : pad_cols + ker] = real.T
    left = np.zeros((2 * pad_rows, 2 * pup))
    left[:ker, :pup] = real
    left[:ker, pup:] = -imag
    left[pad_rows : pad_rows + ker, :pup] = imag
    left[pad_rows : pad_rows + ker, pup:] = real
    return left, right


class Joined:
    def __init__(self, left, right):
        self.places, groups = {}, {}
        for name, matrix in right.items():
            high, low = halves(matrix)
            groups.setdefault(matrix.shape[0], []).append((name, np.concatenate([high, high, low], 0)))
        for name, matrix in left.items():
            high, low = halves(matrix)
            held = np.concatenate([high, low], 0) if name in STACKED else np.concatenate([high, low, high], 1)
            groups.setdefault("left", []).append((name, held))
        self.arrays = []
        for kind, members in groups.items():
            at = 0
            for name, block in members:
                rows, cols = block.shape
                start = (at, 0) if kind == "left" else (0, at)
                self.places[name] = (len(self.arrays), *start, rows, cols)
                at += rows if kind == "left" else cols
            blocks = [block for _, block in members]
            if kind == "left":
                width = max(block.shape[1] for block in blocks)
                blocks = [np.pad(block, ((0, 0), (0, width - block.shape[1]))) for block in blocks]
            self.arrays.append(np.concatenate(blocks, 0 if kind == "left" else 1))

    def at(self, *refs):
        return {
            name: refs[which].at[top : top + rows, first : first + cols]
            for name, (which, top, first, rows, cols) in self.places.items()
        }


def dot(left, right):
    return jnp.dot(left, right, preferred_element_type=jnp.float32)


def split(value):
    high = value.astype(jnp.bfloat16)
    low = (value - high.astype(jnp.float32)).astype(jnp.bfloat16)
    return high, low


def left_by(const, value):
    high, low = split(value)
    return dot(const[...], jnp.concatenate([high, high, low], 0))


def left_stacked(const, value):
    high, low = split(value)
    rows = const.shape[0] // 2
    both = dot(const[...], high)
    return both[:rows] + (both[rows:] + dot(const[:rows], low))


def right_by(value, const):
    high, low = split(value)
    return dot(jnp.concatenate([high, low, high], 1), const[...])


def sine_cosine(angle):
    turns = jnp.floor(angle * (2.0 / math.pi) + 0.5)
    rest = angle - turns * 1.5703125
    rest = rest - turns * 4.837512969970703e-4
    rest = rest - turns * 7.54978995489e-8
    square = rest * rest
    sine = rest + rest * square * (
        -1.6666654611e-1 + square * (8.3321608736e-3 + square * -1.9515295891e-4)
    )
    cosine = 1.0 - 0.5 * square + square * square * (
        4.166664568298827e-2 + square * (-1.388731625493765e-3 + square * 2.443315711809948e-5)
    )
    quadrant = turns.astype(jnp.int32) & 3
    swap = (quadrant & 1) == 1
    sine_out = jnp.where(swap, cosine, sine)
    cosine_out = jnp.where(swap, sine, cosine)
    sine_out = jnp.where(quadrant >= 2, -sine_out, sine_out)
    cosine_out = jnp.where((quadrant == 1) | (quadrant == 2), -cosine_out, cosine_out)
    return sine_out, cosine_out


def total(value):
    return jnp.sum(jnp.sum(value, axis=0, keepdims=True), axis=1, keepdims=True)


def weights(amplitude):
    pup = amplitude.shape[0]
    rows = lax.broadcasted_iota(jnp.int32, amplitude.shape, 0).astype(jnp.float32) - (pup - 1) / 2.0
    cols = lax.broadcasted_iota(jnp.int32, amplitude.shape, 1).astype(jnp.float32) - (pup - 1) / 2.0
    return jnp.where(rows * rows + cols * cols <= (pup / 2.0) ** 2, amplitude, 0.0)


def point_spread(phase, amplitude, const, wait_for=lambda name: None):
    weight = weights(amplitude)
    sine, cosine = sine_cosine(phase)
    pupil = jnp.concatenate([weight * cosine, weight * sine], 1)
    wait_for("pupil_right")
    across = right_by(pupil, const["pupil_right"])
    cols = across.shape[1] // 2
    wait_for("pupil_left")
    field = left_by(const["pupil_left"], jnp.concatenate([across[:, :cols], across[:, cols:]], 0))
    rows = field.shape[0] // 2
    intensity = field[:rows] * field[:rows] + field[rows:] * field[rows:]
    norm = 1.0 / total(intensity)
    left = left_by(const["kernel_rows"], intensity)
    freqs = left.shape[0] // 2
    wait_for("kernel_right")
    spectrum = right_by(jnp.concatenate([left[:freqs], left[freqs:]], 1), const["kernel_right"])
    return pupil, field, spectrum * norm, norm


def forward(strips, row_matrix, const):
    sums, differences = [], []
    for strip in strips:
        half = strip.shape[1] // 2
        first, second = strip[:, :half], strip[:, half:]
        mixed = left_by(row_matrix, jnp.concatenate([first + second, first - second], 1))
        freqs = mixed.shape[0] // 2
        sums.append(jnp.concatenate([mixed[:freqs, :half], mixed[freqs:, :half]], 1))
        differences.append(jnp.concatenate([mixed[:freqs, half:], mixed[freqs:, half:]], 1))
    even = [right_by(jnp.concatenate(sums[p : p + 2], 0), const["forward_even"]) for p in range(0, len(sums), 2)]
    odd = [right_by(jnp.concatenate(differences[p : p + 2], 0), const["forward_odd"]) for p in range(0, len(sums), 2)]
    return even, odd


def inverse(even, odd, freqs, const):
    even = [right_by(spectrum, const["inverse_even"]) for spectrum in even]
    odd = [right_by(spectrum, const["inverse_odd"]) for spectrum in odd]
    strips = []
    for sums, differences in zip(even, odd):
        half = sums.shape[1] // 2
        for top in range(0, sums.shape[0], freqs):
            rows = slice(top, top + freqs)
            stacked = jnp.concatenate(
                [
                    jnp.concatenate([sums[rows, :half], differences[rows, :half]], 1),
                    jnp.concatenate([sums[rows, half:], differences[rows, half:]], 1),
                ],
                0,
            )
            mixed = left_stacked(const["row_inverse"], stacked)
            first, second = mixed[:, :half], mixed[:, half:]
            strips.append(jnp.concatenate([first + second, first - second], 1))
    return strips


def times(spectra, other, conjugate):
    half = other.shape[1] // 2
    products = []
    for spectrum in spectra:
        planes = spectrum.shape[0] // other.shape[0]
        real = jnp.concatenate([other[:, :half]] * planes, 0)
        imag = jnp.concatenate([other[:, half:]] * planes, 0)
        left, right = spectrum[:, :half], spectrum[:, half:]
        if conjugate:
            product = [left * real + right * imag, right * real - left * imag]
        else:
            product = [left * real - right * imag, left * imag + right * real]
        products.append(jnp.concatenate(product, 1))
    return products


def cross(firsts, seconds, freqs):
    summed = None
    for first, second in zip(firsts, seconds):
        half = first.shape[1] // 2
        left, right = first[:, :half], first[:, half:]
        real, imag = second[:, :half], second[:, half:]
        both = jnp.concatenate([left * real + right * imag, right * real - left * imag], 1)
        for top in range(0, both.shape[0], freqs):
            summed = both[top : top + freqs] if summed is None else summed + both[top : top + freqs]
    return summed


def is_even():
    return lax.axis_index("tile") % 2 == 0


def edge_rows(top, bottom):
    even = is_even()
    return [pl.multiple_of(jnp.where(even, *choice), 8) for choice in ((top, bottom), (bottom, top))]


def near_kernel(own, chip_out, sem):
    chip, _ = edge_rows(0, own.shape[1] - HALF)
    copy = pltpu.make_async_copy(own.at[:, pl.ds(chip, HALF), :], chip_out, sem)
    copy.start()
    copy.wait()


def first_kernel(
    phase, amplitude, own, observed, *refs, at, places, arrays,
):
    psf_refs, outs = refs[:arrays], refs[arrays + 1 : arrays + 9]
    pupil_out, field_out, spec_out, chip_out, core_out, early_out, late_out, token_out = outs
    psf_outs, (phase_in, amplitude_in, sems) = refs[arrays + 9 : -3], refs[-3:]
    planes, rows, _ = own.shape
    early = early_out.shape[0]
    objects_chip, objects_core = edge_rows(HALF, rows - 2 * HALF)
    observed_chip, observed_core = edge_rows(0, rows - HALF)
    pairs = [
        (phase, phase_in),
        (amplitude, amplitude_in),
        *zip(psf_refs, psf_outs),
        (own.at[:early, pl.ds(observed_core, HALF), :], early_out),
        (own.at[early:, pl.ds(observed_core, HALF), :], late_out),
        (own.at[:, pl.ds(objects_chip, HALF), :], chip_out.at[:planes]),
        (observed.at[:, pl.ds(observed_chip, HALF), :], chip_out.at[planes:]),
        (own.at[:, pl.ds(objects_core, HALF), :], core_out.at[:planes]),
        (observed.at[:, pl.ds(observed_core, HALF), :], core_out.at[planes:]),
    ]
    copies = [pltpu.make_async_copy(source, target, sems.at[i]) for i, (source, target) in enumerate(pairs)]
    for i in (0, 1, *(2 + places[name][0] for name in NEEDED_IN_ORDER), *range(2 + arrays, len(copies))):
        copies[i].start()
    for copy in copies[:2]:
        copy.wait()

    def wait_for(name):
        copies[2 + places[name][0]].wait()

    pupil, field, spectrum, norm = point_spread(phase_in[...], amplitude_in[...], at(*psf_outs), wait_for)
    root = jnp.sqrt(norm)
    pupil_out[...] = pupil * root
    field_out[...] = field * root
    spec_out[...] = spectrum
    token_out[...] = jnp.zeros_like(token_out)
    for copy in copies[2 + arrays :]:
        copy.wait()


def halo_rows(chip, core):
    even = is_even()
    return jnp.where(even, chip, core), jnp.where(even, core, chip)


def gradient_kernel(
    from_chip, early_core, late_core, own, observed, spec, pupil, field, _, *refs, at,
):
    planes, rows, cols = own.shape
    const = at(*refs[:-2])
    keep_out, give_out = refs[-2:]
    freqs = spec.shape[0]
    early = early_core.shape[0]
    strips = []
    for p in range(planes):
        above, below = halo_rows(from_chip[p], early_core[p] if p < early else late_core[p - early])
        strips.append(jnp.concatenate([above, own[p], below], 0))
    even, odd = forward(strips, const["row_forward"], const)
    blurred = inverse(times(even, spec[:, :cols], False), times(odd, spec[:, cols:], False), freqs, const)
    misfit = [1.0 - observed[p] / (blurred[p] + BACKGROUND) for p in range(planes)]
    weighted = misfit[0] * blurred[0]
    for p in range(1, planes):
        weighted = weighted + misfit[p] * blurred[p]
    mean = total(weighted)
    misfit_even, misfit_odd = forward(misfit, const["row_own"], const)
    shared = jnp.concatenate([cross(misfit_even, even, freqs), cross(misfit_odd, odd, freqs)], 1)
    across = right_by(shared, const["lag_right"])
    pad_cols = across.shape[1] // 2
    psf_grad = left_by(const["lag_left"], jnp.concatenate([across[:, :pad_cols], across[:, pad_cols:]], 0))
    far = field[...]
    pad_rows = far.shape[0] // 2
    real, imag = far[:pad_rows], far[pad_rows:]
    centred = 2.0 * (psf_grad - mean)
    back = left_by(const["adjoint_left"], jnp.concatenate([centred * real, centred * imag], 0))
    pup = back.shape[0] // 2
    back = right_by(jnp.concatenate([back[:pup], back[pup:]], 1), const["adjoint_right"])
    near = pupil[...]
    slope = back[:, pup:] * near[:, :pup] - back[:, :pup] * near[:, pup:]
    even_core = is_even()
    keep_out[...] = jnp.where(even_core, slope[: pup // 2], slope[pup // 2 :])
    give_out[...] = jnp.where(even_core, slope[pup // 2 :], slope[: pup // 2])


def square_sums(value):
    rows = value.shape[0]
    squared = value * value
    summed = squared[:8]
    for top in range(8, rows, 8):
        summed = summed + squared[top : top + 8]
    return summed


def squares_kernel(mine, received, *others):
    joined_out = others[-1]
    half = mine[...] + received[...]
    squares = square_sums(half)
    for first, second in zip(others[:-1:2], others[1:-1:2]):
        squares = squares + square_sums(first[...] + second[...])
    joined_out[: half.shape[0]] = half
    joined_out[half.shape[0] :] = squares


def blocks_kernel(from_chip, early_core, late_core, own, far_chip, far_core, _, *refs, at):
    planes = own.shape[0]
    const = at(*refs[:-2])
    even_out, odd_out = refs[-2:]
    early = early_core.shape[0]
    strips = []
    for p in range(planes):
        above, below = halo_rows(from_chip[p], early_core[p] if p < early else late_core[p - early])
        far_above, far_below = halo_rows(far_chip[p], far_core[p])
        strips.append(jnp.concatenate([far_above, above, own[p]], 0))
        strips.append(jnp.concatenate([own[p], below, far_below], 0))
    even, odd = forward(strips, const["row_forward"], const)
    even_out[...] = jnp.concatenate(even, 0)
    odd_out[...] = jnp.concatenate(odd, 0)


def second_kernel(phase, amplitude, mine, theirs, *refs, at, psf_at, arrays, cells, squares_apart):
    if squares_apart:
        squares, *refs = refs
    even, odd, own, observed, far_chip, far_core, *refs = refs
    planes, rows, cols = own.shape
    const = at(*refs[:arrays])
    psf_const = psf_at(*refs[arrays:-2])
    objects_out, phase_out = refs[-2:]
    half = phase.shape[0] // 2
    first, second = halo_rows(mine[:half], theirs[:half])
    slope = jnp.concatenate([first, second], 0)
    summed = squares[...] if squares_apart else mine[half:] + theirs[half:]
    mean_square = total(summed) * (1.0 / cells)
    updated = phase[...] - STEP_SIZE * slope / jnp.sqrt(mean_square + EPSILON)
    phase_out[...] = updated
    _, _, spec, _ = point_spread(updated, amplitude[...], psf_const)
    spec_even, spec_odd = spec[:, :cols], spec[:, cols:]
    freqs = spec.shape[0]
    pairs = range(0, even.shape[0], 2 * freqs)
    light = inverse(
        times([even[top : top + 2 * freqs] for top in pairs], spec_even, False),
        times([odd[top : top + 2 * freqs] for top in pairs], spec_odd, False),
        freqs, const,
    )
    ratios = []
    for p in range(planes):
        above, below = halo_rows(far_chip[planes + p], far_core[planes + p])
        blurred = jnp.concatenate(light[2 * p : 2 * p + 2], 0) + BACKGROUND
        ratios.append(jnp.concatenate([above, observed[p], below], 0) / blurred)
    ratio_even, ratio_odd = forward(ratios, const["row_forward"], const)
    correction = inverse(times(ratio_even, spec_even, True), times(ratio_odd, spec_odd, True), freqs, const)
    for p in range(planes):
        objects_out[p] = own[p] * correction[p]


def call(kernel, out_shapes, args, flops=10**6, spaces=None, scratch=()):
    outs = [
        jax.ShapeDtypeStruct(shape, jnp.float32) if isinstance(shape, tuple) else shape for shape in out_shapes
    ]
    spaces = spaces or {}
    return pl.pallas_call(
        kernel,
        out_shape=outs,
        in_specs=[pl.BlockSpec(memory_space=spaces.get(i, pltpu.VMEM)) for i in range(len(args))],
        out_specs=[pl.BlockSpec(memory_space=pltpu.VMEM)] * len(outs),
        scratch_shapes=scratch,
        compiler_params=pltpu.CompilerParams(vmem_limit_bytes=VMEM_LIMIT),
        cost_estimate=pl.CostEstimate(flops=flops, bytes_accessed=10**5, transcendentals=0),
    )(*args)


def to_next_chip(value):
    count = lax.axis_size("tile")
    return lax.ppermute(value, "tile", [(i, (i + 1 if i % 2 else i - 1) % count) for i in range(count)])


def exchange(value, step):
    return lax.ppermute(value, "tile", [(i, i ^ step) for i in range(lax.axis_size("tile"))])


def across_depth_and_chip(value):
    pairs = [(2 * t + d, 2 * (t ^ 2) + 1 - d) for t in range(lax.axis_size("tile")) for d in range(2)]
    return lax.ppermute(value, ("tile", "depth"), pairs)


def sum_over_depth(value):
    count = lax.axis_size("depth")
    if count & (count - 1):
        return lax.psum(value, "depth")
    for bit in range(count.bit_length() - 1):
        value = value + lax.ppermute(value, "depth", [(i, i ^ (1 << bit)) for i in range(count)])
    return value


def on_device(objects, observed, pupil_phase, pupil_amplitude):
    picture, measured, phase, amplitude = objects[0], observed[0], pupil_phase[0], pupil_amplitude[0]
    planes, rows, cols = picture.shape
    pup = phase.shape[0]
    count = lax.axis_size("tile")
    ker = 2 * HALF + 1
    length = rows + 2 * HALF
    pad_rows, pad_cols = round_up(ker, 16), round_up(ker, 128)
    row_forward, row_inverse = row_constants(rows, length)
    col_forward, col_inverse = col_constants(cols)
    kernel_rows, kernel_right = kernel_constants(length, cols, ker, pad_rows, pad_cols)
    pupil_left, pupil_right = pupil_constants(pup, ker, pad_rows, pad_cols)
    psf_const = Joined(
        {"pupil_left": pupil_left, "kernel_rows": kernel_rows},
        {"pupil_right": pupil_right, "kernel_right": kernel_right},
    )
    block_left = {"row_forward": row_forward, "row_inverse": row_inverse}
    block_right = {
        "forward_even": col_forward[0],
        "forward_odd": col_forward[1],
        "inverse_even": col_inverse[0],
        "inverse_odd": col_inverse[1],
    }
    block_const = Joined(block_left, block_right)
    lag_const = Joined(
        {
            "row_own": row_forward[:, HALF : HALF + rows],
            "lag_left": kernel_rows.T * (2.0 / length),
            "adjoint_left": pupil_left.T,
        },
        {"lag_right": kernel_right.T / cols, "adjoint_right": pupil_right.T},
    )
    psf_arrays, block_arrays, lag_arrays = (
        [jnp.asarray(array) for array in const.arrays] for const in (psf_const, block_const, lag_const)
    )

    def gradient_at(*refs):
        held = len(block_arrays)
        return {**block_const.at(*refs[:held]), **lag_const.at(*refs[held:])}

    in_hbm = [
        pltpu.with_memory_space_constraint(value, pltpu.HBM)
        for value in (phase, amplitude, picture, measured, *psf_arrays)
    ]
    (chip_rows,) = call(
        near_kernel, [(planes, HALF, cols)], in_hbm[2:3], scratch=[pltpu.SemaphoreType.DMA(())], spaces={0: pltpu.HBM}
    )
    from_chip = to_next_chip(chip_rows)
    pupil, field, spec, far_chip, far_core, early_rows, late_rows, token, *psf_arrays = call(
        functools.partial(first_kernel, at=psf_const.at, places=psf_const.places, arrays=len(psf_arrays)),
        [(pup, 2 * pup), (2 * pad_rows, pad_cols), (length // 2, 2 * cols)]
        + [(2 * planes, HALF, cols)] * 2
        + [(planes // 2, HALF, cols), (planes - planes // 2, HALF, cols), (8, 128)]
        + psf_arrays,
        (*in_hbm, chip_rows),
        flops=3 * 10**9,
        spaces={**dict.fromkeys(range(len(in_hbm)), pltpu.HBM), len(in_hbm): pl.ANY},
        scratch=[pltpu.VMEM(phase.shape, jnp.float32)] * 2 + [pltpu.SemaphoreType.DMA((8 + len(psf_arrays),))],
    )
    early_core, late_core, far_core = (exchange(value, 1) for value in (early_rows, late_rows, far_core))
    far_chip, late_core = lax.optimization_barrier((far_chip, late_core))
    far_chip = to_next_chip(far_chip)
    keep, give = call(
        functools.partial(gradient_kernel, at=gradient_at),
        [(pup // 2, pup)] * 2,
        (from_chip, early_core, late_core, picture, measured, spec, pupil, field, token, *block_arrays, *lag_arrays),
        flops=4 * 10**10,
        spaces={8: pl.ANY},
    )
    half = keep + exchange(give, 1)
    bits = list(range(2, count.bit_length() - 1))
    for low, high in zip(bits[::2], bits[1::2]):
        half = half + ((exchange(half, 1 << low) + exchange(half, (1 << low) | (1 << high))) + exchange(half, 1 << high))
    if len(bits) % 2:
        half = half + exchange(half, 1 << bits[-1])
    last_round = [exchange(half, 2)]
    two_strata = lax.axis_size("depth") == 2
    if two_strata:
        last_round += [lax.ppermute(half, "depth", [(0, 1), (1, 0)]), across_depth_and_chip(half)]
    even, odd = call(
        functools.partial(blocks_kernel, at=block_const.at),
        [(planes * length, cols)] * 2,
        (from_chip, early_core, late_core, picture, far_chip, far_core, half, *block_arrays),
        spaces={6: pl.ANY},
    )
    even, *last_round = lax.optimization_barrier((even, *last_round))
    (joined,) = call(squares_kernel, [(pup // 2 + 8, pup)], (half, *last_round))
    other = exchange(joined, 1)
    squares = []
    if not two_strata:
        squares = [sum_over_depth(joined[pup // 2 :] + other[pup // 2 :])]
    new_objects, new_phase = call(
        functools.partial(
            second_kernel,
            at=block_const.at,
            psf_at=psf_const.at,
            arrays=len(block_arrays),
            cells=lax.axis_size("depth") * pup * pup,
            squares_apart=bool(squares),
        ),
        [picture.shape, phase.shape],
        (
            phase, amplitude, joined, other, *squares, even, odd, picture, measured,
            far_chip, far_core, *block_arrays, *psf_arrays,
        ),
    )
    return new_objects[None], new_phase[None]


def solution(mesh):
    return jax.shard_map(
        on_device,
        mesh=mesh,
        in_specs=(
            P("depth", None, "tile", None),
            P("depth", None, "tile", None),
            P("depth", None, None),
            P("depth", None, None),
        ),
        out_specs=(P("depth", None, "tile", None), P("depth", None, None)),
        check_vma=False,
    )
```

profile of v0, /device:TPU:0, one launch (start us, length us, event | category | flops | bytes accessed | tf_op | source)
XLA Modules:
  0.0 38.8 jit_solution(9398129383898953119)
XLA Ops:
  0.6 1.0 %shard_map.122.refs_3_ = f32[4,64,256]{2,1,0:T(8,128)S(1)} custom-call(f32[4,128,256]{2,1,0:T(8,128)} %bitcast.6), custom_call_target="tpu_custom_call" | custom-call | flops 1000000 | bytes 100000 | tf_op jit(solution)/shard_map/pallas_call | solution.py:437
  1.6 5.5 %collective-permute-start = (f32[4,64,256]{2,1,0:T(8,128)S(1)}, f32[4,64,256]{2,1,0:T(8,128)S(1)}, u32[]{:S(2)}, u32[]{:S(2)}) collective-permute-start(f32[4,64,256]{2,1,0:T(8,128)S(1)} %shard_map.122.refs_3_), channel_id=1, source_target_pairs={{0,30},{2,4},{4,2},{6,8},{8,6},{10,12},{12,10},{14,16},{16,14},{18... | collective-permute-start | bytes 786440 | tf_op jit(solution)/shard_map/ppermute | solution.py:450
  7.1 0.0 copy-start
  7.1 0.0 copy-start.1
  7.1 0.0 copy-start.2
  7.1 0.0 copy-start.3
  7.1 0.0 copy-start.6
  7.1 0.0 copy-start.7
  7.2 2.7 %shard_map.123 = (f32[128,256]{1,0:T(8,128)S(1)}, f32[288,256]{1,0:T(8,128)S(1)}, f32[128,512]{1,0:T(8,128)S(1)}, f32[8,64,256]{2,1,0:T(8,128)S(1)}, f32[8,64,25...) custom-call(f32[128,128]{1,0:T(8,128)} %bitcast.14, ...), custom_call_target="tpu_custom_call" | custom-call | flops 3000000000 | bytes 100000 | tf_op jit(solution)/shard_map/pallas_call | solution.py:437
  9.9 0.1 collective-permute-start.2
  10.0 0.5 %collective-permute-start.1 = (f32[2,64,256]{2,1,0:T(8,128)S(1)}, f32[2,64,256]{2,1,0:T(8,128)S(1)}, u32[]{:S(2)}, u32[]{:S(2)}) collective-permute-start(f32[2,64,256]{2,1,0:T(8,128)S(1)} %get-tuple-element.25), channel_id=1, source_target_pairs={{0,2},{2,0},{4,6},{6,4},{8,10},{10,8},{12,14},{14,12},{16,18},{18,... | collective-permute-start | bytes 393224 | tf_op jit(solution)/shard_map/ppermute | solution.py:454
  10.5 0.1 collective-permute-start.8
  10.6 0.8 %collective-permute-done.2.late_core = f32[2,64,256]{2,1,0:T(8,128)S(1)} collective-permute-done((f32[2,64,256]{2,1,0:T(8,128)S(1)}, f32[2,64,256]{2,1,0:T(8,128)S(1)}, u32[]{:S(2)}, u32[]{:S(2)}) %collective-permute-start.2) | collective-permute-done | bytes 131104 | tf_op jit(solution)/shard_map/ppermute | solution.py:454
  11.3 0.4 collective-permute-start.7
  11.7 0.0 collective-permute-done.1.early_core
  11.7 0.0 collective-permute-done.from_chip
  11.7 0.0 copy-done
  11.7 0.0 copy-done.1
  11.7 0.0 copy-done.2
  11.7 0.0 copy-done.3
  11.7 0.0 copy-done.6
  11.7 0.0 copy-done.7
  11.8 3.9 %shard_map.124 = (f32[64,128]{1,0:T(8,128)S(1)}, f32[64,128]{1,0:T(8,128)S(1)}) custom-call(f32[4,64,256]{2,1,0:T(8,128)S(1)} %collective-permute-done.from_chip, f32[2,64,256]{2,1,0:T(8,128)S(1)} %collective-permute-done.1.early_core, f32[2,64,256]{2,1,0:T(8,128)S(1)} %collective-permute-done.2.late_core, f32[4,128,256]{2,1,0:T(8,128)S(1)} %bitcast.8, ...), custom_call_target="tpu_custom_call" | custom-call | flops 40000000000 | bytes 100000 | tf_op jit(solution)/shard_map/pallas_call | solution.py:437
  15.6 0.2 collective-permute-start.3
  15.8 1.1 %collective-permute-done.3 = f32[64,128]{1,0:T(8,128)S(1)} collective-permute-done((f32[64,128]{1,0:T(8,128)S(1)}, f32[64,128]{1,0:T(8,128)S(1)}, u32[]{:S(2)}, u32[]{:S(2)}) %collective-permute-start.3) | collective-permute-done | bytes 32800 | tf_op jit(solution)/shard_map/ppermute | solution.py:454
  16.9 2.2 %collective-permute-start.6 = (f32[64,128]{1,0:T(8,128)S(1)}, f32[64,128]{1,0:T(8,128)S(1)}, u32[]{:S(2)}, u32[]{:S(2)}) collective-permute-start(f32[64,128]{1,0:T(8,128)S(1)} %add.12), channel_id=1, source_target_pairs={{0,16},{2,18},{4,20},{6,22},{8,24},{10,26},{12,28},{14,30},{16,0},... | collective-permute-start | bytes 98312 | tf_op jit(solution)/shard_map/ppermute | solution.py:454
  19.1 1.3 %collective-permute-start.5 = (f32[64,128]{1,0:T(8,128)S(1)}, f32[64,128]{1,0:T(8,128)S(1)}, u32[]{:S(2)}, u32[]{:S(2)}) collective-permute-start(f32[64,128]{1,0:T(8,128)S(1)} %add.12), channel_id=1, source_target_pairs={{0,24},{2,26},{4,28},{6,30},{8,16},{10,18},{12,20},{14,22},{16,8},... | collective-permute-start | bytes 98312 | tf_op jit(solution)/shard_map/ppermute | solution.py:454
  20.4 0.2 collective-permute-start.4
  20.7 1.7 %collective-permute-done.6 = f32[64,128]{1,0:T(8,128)S(1)} collective-permute-done((f32[64,128]{1,0:T(8,128)S(1)}, f32[64,128]{1,0:T(8,128)S(1)}, u32[]{:S(2)}, u32[]{:S(2)}) %collective-permute-start.6) | collective-permute-done | bytes 32800 | tf_op jit(solution)/shard_map/ppermute | solution.py:454
  22.4 2.4 %collective-permute-done.5 = f32[64,128]{1,0:T(8,128)S(1)} collective-permute-done((f32[64,128]{1,0:T(8,128)S(1)}, f32[64,128]{1,0:T(8,128)S(1)}, u32[]{:S(2)}, u32[]{:S(2)}) %collective-permute-start.5) | collective-permute-done | bytes 32800 | tf_op jit(solution)/shard_map/ppermute | solution.py:454
  24.8 0.0 collective-permute-done.4
  24.8 0.0 copy-start.4
  24.8 0.0 copy-start.5
  24.8 3.0 %collective-permute-start.11 = (f32[64,128]{1,0:T(8,128)S(1)}, f32[64,128]{1,0:T(8,128)S(1)}, u32[]{:S(2)}, u32[]{:S(2)}) collective-permute-start(f32[64,128]{1,0:T(8,128)S(1)} %add_add_fusion._.mine), channel_id=1, source_target_pairs={{0,5},{1,4},{2,7},{3,6},{4,1},{5,0},{6,3},{7,2},{8,13},{9,12},{10,... | collective-permute-start | bytes 98312 | tf_op jit(solution)/shard_map/ppermute | solution.py:459
  27.8 0.5 %collective-permute-start.10 = (f32[64,128]{1,0:T(8,128)S(1)}, f32[64,128]{1,0:T(8,128)S(1)}, u32[]{:S(2)}, u32[]{:S(2)}) collective-permute-start(f32[64,128]{1,0:T(8,128)S(1)} %add_add_fusion._.mine), channel_id=1, source_target_pairs={{0,1},{1,0},{2,3},{3,2},{4,5},{5,4},{6,7},{7,6},{8,9},{9,8},{10,11... | collective-permute-start | bytes 98312 | tf_op jit(solution)/shard_map/ppermute | solution.py:549
  28.3 0.1 collective-permute-start.9
  28.4 0.0 collective-permute-done.8.far_core.refs_5_
  28.4 0.0 collective-permute-done.7.far_chip.refs_4_
  28.4 1.9 %shard_map.125 = (f32[1024,256]{1,0:T(8,128)S(1)}, f32[1024,256]{1,0:T(8,128)S(1)}) custom-call(f32[4,64,256]{2,1,0:T(8,128)S(1)} %collective-permute-done.from_chip, f32[2,64,256]{2,1,0:T(8,128)S(1)} %collective-permute-done.1.early_core, f32[2,64,256]{2,1,0:T(8,128)S(1)} %collective-permute-done.2.late_core, f32[4,128,256]{2,1,0:T(8,128)S(1)} %bitcast.9, ...), custom_call_target="tpu_custom_call" | custom-call | flops 1000000 | bytes 100000 | tf_op jit(solution)/shard_map/pallas_call | solution.py:437
  30.4 0.0 collective-permute-done.11.others_1_
  30.4 1.3 %collective-permute-done.10.others_0_ = f32[64,128]{1,0:T(8,128)S(1)} collective-permute-done((f32[64,128]{1,0:T(8,128)S(1)}, f32[64,128]{1,0:T(8,128)S(1)}, u32[]{:S(2)}, u32[]{:S(2)}) %collective-permute-start.10) | collective-permute-done | bytes 32800 | tf_op jit(solution)/shard_map/ppermute | solution.py:549
  31.7 0.5 %collective-permute-done.9.received = f32[64,128]{1,0:T(8,128)S(1)} collective-permute-done((f32[64,128]{1,0:T(8,128)S(1)}, f32[64,128]{1,0:T(8,128)S(1)}, u32[]{:S(2)}, u32[]{:S(2)}) %collective-permute-start.9) | collective-permute-done | bytes 32800 | tf_op jit(solution)/shard_map/ppermute | solution.py:454
  32.3 0.1 collective-permute-start.12
  32.3 1.2 %collective-permute-done.12.theirs = f32[72,128]{1,0:T(8,128)S(1)} collective-permute-done((f32[72,128]{1,0:T(8,128)S(1)}, f32[72,128]{1,0:T(8,128)S(1)}, u32[]{:S(2)}, u32[]{:S(2)}) %collective-permute-start.12) | collective-permute-done | bytes 36896 | tf_op jit(solution)/shard_map/ppermute | solution.py:454
  33.5 0.0 copy-done.4
  33.5 0.0 copy-done.5
  33.5 5.3 %shard_map.127 = (f32[4,128,256]{2,1,0:T(8,128)}, f32[128,128]{1,0:T(8,128)}) custom-call(f32[128,128]{1,0:T(8,128)S(1)} %bitcast.15, f32[128,128]{1,0:T(8,128)S(1)} %bitcast.17, f32[72,128]{1,0:T(8,128)S(1)} %shard_map.126.mine, f32[72,128]{1,0:T(8,128)S(1)} %collective-permute-done.12.theirs, f32[1024,256]{1,0:T(8,128)S(1)} %get-tuple-element.41.refs_0_, ...), custom_call_target="tpu_custom_call" | custom-call | flops 1000000 | bytes 100000 | tf_op jit(solution)/shard_map/pallas_call | solution.py:437
  (3 shorter events, 0.0 us)
Async XLA Ops:
  1.6 10.1 %collective-permute-start = (f32[4,64,256]{2,1,0:T(8,128)S(1)}, f32[4,64,256]{2,1,0:T(8,128)S(1)}, u32[]{:S(2)}, u32[]{:S(2)}) collective-permute-start(f32[4,64,256]{2,1,0:T(8,128)S(1)} %shard_map.122.refs_3_), channel_id=1, source_target_pairs={{0,30},{2,4},{4,2},{6,8},{8,6},{10,12},{12,10},{14,16},{16,14},{18... | collective-permute-start | bytes 786440 | tf_op jit(solution)/shard_map/ppermute | solution.py:450
  7.1 4.6 %copy-start = (bf16[768,1024]{1,0:T(8,128)(2,1)S(1)}, bf16[768,1024]{1,0:T(8,128)(2,1)}, u32[]{:S(2)}) copy-start(bf16[768,1024]{1,0:T(8,128)(2,1)} %constant.17.clone.refs_0_.refs_6_) | copy-start | bytes 4718596
  7.1 4.6 %copy-start.1 = (f32[1,4,128,256]{3,2,1,0:T(8,128)S(1)}, f32[1,4,128,256]{3,2,1,0:T(8,128)}, u32[]{:S(2)}) copy-start(f32[1,4,128,256]{3,2,1,0:T(8,128)} %param.11) | copy-start | bytes 1572868
  7.1 4.6 %copy-start.2 = (bf16[512,768]{1,0:T(8,128)(2,1)S(1)}, bf16[512,768]{1,0:T(8,128)(2,1)}, u32[]{:S(2)}) copy-start(bf16[512,768]{1,0:T(8,128)(2,1)} %constant.18.clone.refs_1_.refs_7_) | copy-start | bytes 2359300
  7.1 4.6 %copy-start.3 = (f32[1,4,128,256]{3,2,1,0:T(8,128)S(1)}, f32[1,4,128,256]{3,2,1,0:T(8,128)}, u32[]{:S(2)}) copy-start(f32[1,4,128,256]{3,2,1,0:T(8,128)} %param.12) | copy-start | bytes 1572868
  7.1 4.6 %copy-start.6 = (bf16[1536,768]{1,0:T(8,128)(2,1)S(1)}, bf16[1536,768]{1,0:T(8,128)(2,1)}, u32[]{:S(2)}) copy-start(bf16[1536,768]{1,0:T(8,128)(2,1)} %constant.19.clone.refs_2_) | copy-start | bytes 7077892
  7.1 4.6 %copy-start.7 = (bf16[656,864]{1,0:T(8,128)(2,1)S(1)}, bf16[656,864]{1,0:T(8,128)(2,1)}, u32[]{:S(2)}) copy-start(bf16[656,864]{1,0:T(8,128)(2,1)} %constant.20.clone.refs_3_) | copy-start | bytes 3400708
  9.9 1.4 %collective-permute-start.2 = (f32[2,64,256]{2,1,0:T(8,128)S(1)}, f32[2,64,256]{2,1,0:T(8,128)S(1)}, u32[]{:S(2)}, u32[]{:S(2)}) collective-permute-start(f32[2,64,256]{2,1,0:T(8,128)S(1)} %get-tuple-element.27), channel_id=1, source_target_pairs={{0,2},{2,0},{4,6},{6,4},{8,10},{10,8},{12,14},{14,12},{16,18},{18,... | collective-permute-start | bytes 393224 | tf_op jit(solution)/shard_map/ppermute | solution.py:454
  10.0 1.7 %collective-permute-start.1 = (f32[2,64,256]{2,1,0:T(8,128)S(1)}, f32[2,64,256]{2,1,0:T(8,128)S(1)}, u32[]{:S(2)}, u32[]{:S(2)}) collective-permute-start(f32[2,64,256]{2,1,0:T(8,128)S(1)} %get-tuple-element.25), channel_id=1, source_target_pairs={{0,2},{2,0},{4,6},{6,4},{8,10},{10,8},{12,14},{14,12},{16,18},{18,... | collective-permute-start | bytes 393224 | tf_op jit(solution)/shard_map/ppermute | solution.py:454
  10.5 18.0 %collective-permute-start.8 = (f32[8,64,256]{2,1,0:T(8,128)S(1)}, f32[8,64,256]{2,1,0:T(8,128)S(1)}, u32[]{:S(2)}, u32[]{:S(2)}) collective-permute-start(f32[8,64,256]{2,1,0:T(8,128)S(1)} %get-tuple-element.36), channel_id=1, source_target_pairs={{0,2},{2,0},{4,6},{6,4},{8,10},{10,8},{12,14},{14,12},{16,18},{18,... | collective-permute-start | bytes 1572872 | tf_op jit(solution)/shard_map/ppermute | solution.py:454
  11.3 17.1 %collective-permute-start.7 = (f32[8,64,256]{2,1,0:T(8,128)S(1)}, f32[8,64,256]{2,1,0:T(8,128)S(1)}, u32[]{:S(2)}, u32[]{:S(2)}) collective-permute-start(f32[8,64,256]{2,1,0:T(8,128)S(1)} %get-tuple-element.35), channel_id=1, source_target_pairs={{0,30},{2,4},{4,2},{6,8},{8,6},{10,12},{12,10},{14,16},{16,14},{18... | collective-permute-start | bytes 1572872 | tf_op jit(solution)/shard_map/ppermute | solution.py:450
  15.6 1.3 %collective-permute-start.3 = (f32[64,128]{1,0:T(8,128)S(1)}, f32[64,128]{1,0:T(8,128)S(1)}, u32[]{:S(2)}, u32[]{:S(2)}) collective-permute-start(f32[64,128]{1,0:T(8,128)S(1)} %get-tuple-element.34), channel_id=1, source_target_pairs={{0,2},{2,0},{4,6},{6,4},{8,10},{10,8},{12,14},{14,12},{16,18},{18,... | collective-permute-start | bytes 98312 | tf_op jit(solution)/shard_map/ppermute | solution.py:454
  16.9 5.5 %collective-permute-start.6 = (f32[64,128]{1,0:T(8,128)S(1)}, f32[64,128]{1,0:T(8,128)S(1)}, u32[]{:S(2)}, u32[]{:S(2)}) collective-permute-start(f32[64,128]{1,0:T(8,128)S(1)} %add.12), channel_id=1, source_target_pairs={{0,16},{2,18},{4,20},{6,22},{8,24},{10,26},{12,28},{14,30},{16,0},... | collective-permute-start | bytes 98312 | tf_op jit(solution)/shard_map/ppermute | solution.py:454
  19.1 5.7 %collective-permute-start.5 = (f32[64,128]{1,0:T(8,128)S(1)}, f32[64,128]{1,0:T(8,128)S(1)}, u32[]{:S(2)}, u32[]{:S(2)}) collective-permute-start(f32[64,128]{1,0:T(8,128)S(1)} %add.12), channel_id=1, source_target_pairs={{0,24},{2,26},{4,28},{6,30},{8,16},{10,18},{12,20},{14,22},{16,8},... | collective-permute-start | bytes 98312 | tf_op jit(solution)/shard_map/ppermute | solution.py:454
  20.4 4.4 %collective-permute-start.4 = (f32[64,128]{1,0:T(8,128)S(1)}, f32[64,128]{1,0:T(8,128)S(1)}, u32[]{:S(2)}, u32[]{:S(2)}) collective-permute-start(f32[64,128]{1,0:T(8,128)S(1)} %add.12), channel_id=1, source_target_pairs={{0,8},{2,10},{4,12},{6,14},{8,0},{10,2},{12,4},{14,6},{16,24},{18,... | collective-permute-start | bytes 98312 | tf_op jit(solution)/shard_map/ppermute | solution.py:454
  24.8 8.7 %copy-start.4 = (f32[1,128,128]{2,1,0:T(8,128)S(1)}, f32[1,128,128]{2,1,0:T(8,128)}, u32[]{:S(2)}) copy-start(f32[1,128,128]{2,1,0:T(8,128)} %param.13) | copy-start | bytes 196612
  24.8 8.7 %copy-start.5 = (f32[1,128,128]{2,1,0:T(8,128)S(1)}, f32[1,128,128]{2,1,0:T(8,128)}, u32[]{:S(2)}) copy-start(f32[1,128,128]{2,1,0:T(8,128)} %param.14) | copy-start | bytes 196612
  24.8 5.5 %collective-permute-start.11 = (f32[64,128]{1,0:T(8,128)S(1)}, f32[64,128]{1,0:T(8,128)S(1)}, u32[]{:S(2)}, u32[]{:S(2)}) collective-permute-start(f32[64,128]{1,0:T(8,128)S(1)} %add_add_fusion._.mine), channel_id=1, source_target_pairs={{0,5},{1,4},{2,7},{3,6},{4,1},{5,0},{6,3},{7,2},{8,13},{9,12},{10,... | collective-permute-start | bytes 98312 | tf_op jit(solution)/shard_map/ppermute | solution.py:459
  27.8 3.9 %collective-permute-start.10 = (f32[64,128]{1,0:T(8,128)S(1)}, f32[64,128]{1,0:T(8,128)S(1)}, u32[]{:S(2)}, u32[]{:S(2)}) collective-permute-start(f32[64,128]{1,0:T(8,128)S(1)} %add_add_fusion._.mine), channel_id=1, source_target_pairs={{0,1},{1,0},{2,3},{3,2},{4,5},{5,4},{6,7},{7,6},{8,9},{9,8},{10,11... | collective-permute-start | bytes 98312 | tf_op jit(solution)/shard_map/ppermute | solution.py:549
  28.3 3.9 %collective-permute-start.9 = (f32[64,128]{1,0:T(8,128)S(1)}, f32[64,128]{1,0:T(8,128)S(1)}, u32[]{:S(2)}, u32[]{:S(2)}) collective-permute-start(f32[64,128]{1,0:T(8,128)S(1)} %add_add_fusion._.mine), channel_id=1, source_target_pairs={{0,4},{2,6},{4,0},{6,2},{8,12},{10,14},{12,8},{14,10},{16,20},{18,... | collective-permute-start | bytes 98312 | tf_op jit(solution)/shard_map/ppermute | solution.py:454
  32.3 1.3 %collective-permute-start.12 = (f32[72,128]{1,0:T(8,128)S(1)}, f32[72,128]{1,0:T(8,128)S(1)}, u32[]{:S(2)}, u32[]{:S(2)}) collective-permute-start(f32[72,128]{1,0:T(8,128)S(1)} %shard_map.126.mine), channel_id=1, source_target_pairs={{0,2},{2,0},{4,6},{6,4},{8,10},{10,8},{12,14},{14,12},{16,18},{18,... | collective-permute-start | bytes 110600 | tf_op jit(solution)/shard_map/ppermute | solution.py:454
where the time goes:
time: 39 us; the launch traced here: 38.8 us
  Pallas kernels  14.8 us (38%)
  starting transfers between devices  14.1 us (36%)
  waiting for transfers between devices  9.04 us (23%)
  between operations  0.78 us (2%)
    pallas_call x6, Pallas kernels, call(): pl.pallas_call(kernel, out_shape=outs, in_specs=[pl.BlockSpec(memory_spac...  14.8 us
    ppermute x9, waiting for transfers between devices, exchange(): lax.ppermute(value, 'tile', [(i, i ^ step) for i in range(lax.axis_size('...  7.72 us
    ppermute x2, starting transfers between devices, to_next_chip(): lax.ppermute(value, 'tile', [(i, (i + 1 if i % 2 else i - 1) % count) for...  5.88 us
    ppermute x9, starting transfers between devices, exchange(): lax.ppermute(value, 'tile', [(i, i ^ step) for i in range(lax.axis_size('...  4.74 us
    ppermute x1, starting transfers between devices, across_depth_and_chip(): return lax.ppermute(value, ('tile', 'depth'), pairs)  2.96 us
    ppermute x1, waiting for transfers between devices, on_device(): lax.ppermute(half, 'depth', [(0, 1), (1, 0)])  1.32 us
  transfers between devices with their start and end apart: 13, of which 7 were waited for; matrix products, arithmetic and copies ran while one was open for 0% of the time, Pallas kernels for 22%

commit v1 on v0

--- a/solution.py
+++ b/solution.py
@@ -197,12 +197,15 @@
     return pupil, field, spectrum * norm, norm
 
 
-def forward(strips, row_matrix, const):
+def forward(strips, row_matrix, const, levels=None):
     sums, differences = [], []
-    for strip in strips:
+    for plane, strip in enumerate(strips):
         half = strip.shape[1] // 2
         first, second = strip[:, :half], strip[:, half:]
-        mixed = left_by(row_matrix, jnp.concatenate([first + second, first - second], 1))
+        both = first + second
+        if levels is not None:
+            both = both - 2.0 * levels[plane]
+        mixed = left_by(row_matrix, jnp.concatenate([both, first - second], 1))
         freqs = mixed.shape[0] // 2
         sums.append(jnp.concatenate([mixed[:freqs, :half], mixed[freqs:, :half]], 1))
         differences.append(jnp.concatenate([mixed[:freqs, half:], mixed[freqs:, half:]], 1))
@@ -280,9 +283,9 @@
     phase, amplitude, own, observed, *refs, at, places, arrays,
 ):
     psf_refs, outs = refs[:arrays], refs[arrays + 1 : arrays + 9]
-    pupil_out, field_out, spec_out, chip_out, core_out, early_out, late_out, token_out = outs
-    psf_outs, (phase_in, amplitude_in, sems) = refs[arrays + 9 : -3], refs[-3:]
-    planes, rows, _ = own.shape
+    pupil_out, field_out, spec_out, chip_out, core_out, early_out, late_out, means_out = outs
+    psf_outs, (phase_in, amplitude_in, own_in, sems) = refs[arrays + 9 : -4], refs[-4:]
+    planes, rows, cols = own.shape
     early = early_out.shape[0]
     objects_chip, objects_core = edge_rows(HALF, rows - 2 * HALF)
     observed_chip, observed_core = edge_rows(0, rows - HALF)
@@ -296,6 +299,7 @@
         (observed.at[:, pl.ds(observed_chip, HALF), :], chip_out.at[planes:]),
         (own.at[:, pl.ds(objects_core, HALF), :], core_out.at[:planes]),
         (observed.at[:, pl.ds(observed_core, HALF), :], core_out.at[planes:]),
+        (own, own_in),
     ]
     copies = [pltpu.make_async_copy(source, target, sems.at[i]) for i, (source, target) in enumerate(pairs)]
     for i in (0, 1, *(2 + places[name][0] for name in NEEDED_IN_ORDER), *range(2 + arrays, len(copies))):
@@ -311,9 +315,10 @@
     pupil_out[...] = pupil * root
     field_out[...] = field * root
     spec_out[...] = spectrum
-    token_out[...] = jnp.zeros_like(token_out)
     for copy in copies[2 + arrays :]:
         copy.wait()
+    for p in range(planes):
+        means_out[p] = jnp.broadcast_to(total(own_in[p]) * (1.0 / (rows * cols)), means_out.shape[1:])
 
 
 def halo_rows(chip, core):
@@ -322,7 +327,7 @@
 
 
 def gradient_kernel(
-    from_chip, early_core, late_core, own, observed, spec, pupil, field, _, *refs, at,
+    from_chip, early_core, late_core, own, observed, spec, pupil, field, means, *refs, at,
 ):
     planes, rows, cols = own.shape
     const = at(*refs[:-2])
@@ -333,9 +338,10 @@
     for p in range(planes):
         above, below = halo_rows(from_chip[p], early_core[p] if p < early else late_core[p - early])
         strips.append(jnp.concatenate([above, own[p], below], 0))
-    even, odd = forward(strips, const["row_forward"], const)
+    levels = [means[p][:1, :1] for p in range(planes)]
+    even, odd = forward(strips, const["row_forward"], const, levels)
     blurred = inverse(times(even, spec[:, :cols], False), times(odd, spec[:, cols:], False), freqs, const)
-    misfit = [1.0 - observed[p] / (blurred[p] + BACKGROUND) for p in range(planes)]
+    misfit = [1.0 - observed[p] / (blurred[p] + (levels[p] + BACKGROUND)) for p in range(planes)]
     weighted = misfit[0] * blurred[0]
     for p in range(1, planes):
         weighted = weighted + misfit[p] * blurred[p]
@@ -516,16 +522,17 @@
         near_kernel, [(planes, HALF, cols)], in_hbm[2:3], scratch=[pltpu.SemaphoreType.DMA(())], spaces={0: pltpu.HBM}
     )
     from_chip = to_next_chip(chip_rows)
-    pupil, field, spec, far_chip, far_core, early_rows, late_rows, token, *psf_arrays = call(
+    pupil, field, spec, far_chip, far_core, early_rows, late_rows, means, *psf_arrays = call(
         functools.partial(first_kernel, at=psf_const.at, places=psf_const.places, arrays=len(psf_arrays)),
         [(pup, 2 * pup), (2 * pad_rows, pad_cols), (length // 2, 2 * cols)]
         + [(2 * planes, HALF, cols)] * 2
-        + [(planes // 2, HALF, cols), (planes - planes // 2, HALF, cols), (8, 128)]
+        + [(planes // 2, HALF, cols), (planes - planes // 2, HALF, cols), (planes, 8, 128)]
         + psf_arrays,
         (*in_hbm, chip_rows),
         flops=3 * 10**9,
         spaces={**dict.fromkeys(range(len(in_hbm)), pltpu.HBM), len(in_hbm): pl.ANY},
-        scratch=[pltpu.VMEM(phase.shape, jnp.float32)] * 2 + [pltpu.SemaphoreType.DMA((8 + len(psf_arrays),))],
+        scratch=[pltpu.VMEM(value.shape, jnp.float32) for value in (phase, amplitude, picture)]
+        + [pltpu.SemaphoreType.DMA((9 + len(psf_arrays),))],
     )
     early_core, late_core, far_core = (exchange(value, 1) for value in (early_rows, late_rows, far_core))
     far_chip, late_core = lax.optimization_barrier((far_chip, late_core))
@@ -533,9 +540,8 @@
     keep, give = call(
         functools.partial(gradient_kernel, at=gradient_at),
         [(pup // 2, pup)] * 2,
-        (from_chip, early_core, late_core, picture, measured, spec, pupil, field, token, *block_arrays, *lag_arrays),
+        (from_chip, early_core, late_core, picture, measured, spec, pupil, field, means, *block_arrays, *lag_arrays),
         flops=4 * 10**10,
-        spaces={8: pl.ANY},
     )
     half = keep + exchange(give, 1)
     bits = list(range(2, count.bit_length() - 1))

time: 39 us -> 39 us (level)
  no operation moved by 1% of the time
where the time goes in v1:
time: 39 us; the launch traced here: 38.8 us
  Pallas kernels  15 us (38%)
  starting transfers between devices  14 us (36%)
  waiting for transfers between devices  9.04 us (23%)
  between operations  0.78 us (2%)
    pallas_call x6, Pallas kernels, call(): pl.pallas_call(kernel, out_shape=outs, in_specs=[pl.BlockSpec(memory_spac...  15 us
    ppermute x9, waiting for transfers between devices, exchange(): lax.ppermute(value, 'tile', [(i, i ^ step) for i in range(lax.axis_size('...  7.7 us
    ppermute x2, starting transfers between devices, to_next_chip(): lax.ppermute(value, 'tile', [(i, (i + 1 if i % 2 else i - 1) % count) for...  5.88 us
    ppermute x9, starting transfers between devices, exchange(): lax.ppermute(value, 'tile', [(i, i ^ step) for i in range(lax.axis_size('...  4.63 us
    ppermute x1, starting transfers between devices, across_depth_and_chip(): return lax.ppermute(value, ('tile', 'depth'), pairs)  2.97 us
    ppermute x1, waiting for transfers between devices, on_device(): lax.ppermute(half, 'depth', [(0, 1), (1, 0)])  1.32 us
  transfers between devices with their start and end apart: 13, of which 7 were waited for; matrix products, arithmetic and copies ran while one was open for 0% of the time, Pallas kernels for 22%

profile of v1, /device:TPU:0, one launch (start us, length us, event | category | flops | bytes accessed | tf_op | source)
XLA Modules:
  0.0 38.8 jit_solution(16534894830797268845)
XLA Ops:
  0.6 1.0 %shard_map.122.refs_3_ = f32[4,64,256]{2,1,0:T(8,128)S(1)} custom-call(f32[4,128,256]{2,1,0:T(8,128)} %bitcast.6), custom_call_target="tpu_custom_call" | custom-call | flops 1000000 | bytes 100000 | tf_op jit(solution)/shard_map/pallas_call | solution.py:443
  1.6 5.5 %collective-permute-start = (f32[4,64,256]{2,1,0:T(8,128)S(1)}, f32[4,64,256]{2,1,0:T(8,128)S(1)}, u32[]{:S(2)}, u32[]{:S(2)}) collective-permute-start(f32[4,64,256]{2,1,0:T(8,128)S(1)} %shard_map.122.refs_3_), channel_id=1, source_target_pairs={{0,30},{2,4},{4,2},{6,8},{8,6},{10,12},{12,10},{14,16},{16,14},{18... | collective-permute-start | bytes 786440 | tf_op jit(solution)/shard_map/ppermute | solution.py:456
  7.1 0.0 copy-start
  7.1 0.0 copy-start.1
  7.1 0.0 copy-start.2
  7.1 0.0 copy-start.3
  7.1 0.0 copy-start.6
  7.1 0.0 copy-start.7
  7.2 2.9 %shard_map.123 = (f32[128,256]{1,0:T(8,128)S(1)}, f32[288,256]{1,0:T(8,128)S(1)}, f32[128,512]{1,0:T(8,128)S(1)}, f32[8,64,256]{2,1,0:T(8,128)S(1)}, f32[8,64,25...) custom-call(f32[128,128]{1,0:T(8,128)} %bitcast.14, ...), custom_call_target="tpu_custom_call" | custom-call | flops 3000000000 | bytes 100000 | tf_op jit(solution)/shard_map/pallas_call | solution.py:443
  10.0 0.1 collective-permute-start.2
  10.1 0.5 %collective-permute-start.1 = (f32[2,64,256]{2,1,0:T(8,128)S(1)}, f32[2,64,256]{2,1,0:T(8,128)S(1)}, u32[]{:S(2)}, u32[]{:S(2)}) collective-permute-start(f32[2,64,256]{2,1,0:T(8,128)S(1)} %get-tuple-element.25), channel_id=1, source_target_pairs={{0,2},{2,0},{4,6},{6,4},{8,10},{10,8},{12,14},{14,12},{16,18},{18,... | collective-permute-start | bytes 393224 | tf_op jit(solution)/shard_map/ppermute | solution.py:460
  10.6 0.1 collective-permute-start.8
  10.7 0.8 %collective-permute-done.2.late_core = f32[2,64,256]{2,1,0:T(8,128)S(1)} collective-permute-done((f32[2,64,256]{2,1,0:T(8,128)S(1)}, f32[2,64,256]{2,1,0:T(8,128)S(1)}, u32[]{:S(2)}, u32[]{:S(2)}) %collective-permute-start.2) | collective-permute-done | bytes 131104 | tf_op jit(solution)/shard_map/ppermute | solution.py:460
  11.4 0.4 collective-permute-start.7
  11.8 0.0 collective-permute-done.1.early_core
  11.8 0.0 collective-permute-done.from_chip
  11.8 0.0 copy-done
  11.8 0.0 copy-done.1
  11.8 0.0 copy-done.2
  11.9 0.0 copy-done.3
  11.9 0.0 copy-done.6
  11.9 0.0 copy-done.7
  11.9 3.9 %shard_map.124 = (f32[64,128]{1,0:T(8,128)S(1)}, f32[64,128]{1,0:T(8,128)S(1)}) custom-call(f32[4,64,256]{2,1,0:T(8,128)S(1)} %collective-permute-done.from_chip, f32[2,64,256]{2,1,0:T(8,128)S(1)} %collective-permute-done.1.early_core, f32[2,64,256]{2,1,0:T(8,128)S(1)} %collective-permute-done.2.late_core, f32[4,128,256]{2,1,0:T(8,128)S(1)} %bitcast.8, ...), custom_call_target="tpu_custom_call" | custom-call | flops 40000000000 | bytes 100000 | tf_op jit(solution)/shard_map/pallas_call | solution.py:443
  15.8 0.2 collective-permute-start.3
  16.0 1.1 %collective-permute-done.3 = f32[64,128]{1,0:T(8,128)S(1)} collective-permute-done((f32[64,128]{1,0:T(8,128)S(1)}, f32[64,128]{1,0:T(8,128)S(1)}, u32[]{:S(2)}, u32[]{:S(2)}) %collective-permute-start.3) | collective-permute-done | bytes 32800 | tf_op jit(solution)/shard_map/ppermute | solution.py:460
  17.0 2.0 %collective-permute-start.6 = (f32[64,128]{1,0:T(8,128)S(1)}, f32[64,128]{1,0:T(8,128)S(1)}, u32[]{:S(2)}, u32[]{:S(2)}) collective-permute-start(f32[64,128]{1,0:T(8,128)S(1)} %add.12), channel_id=1, source_target_pairs={{0,16},{2,18},{4,20},{6,22},{8,24},{10,26},{12,28},{14,30},{16,0},... | collective-permute-start | bytes 98312 | tf_op jit(solution)/shard_map/ppermute | solution.py:460
  19.1 1.4 %collective-permute-start.5 = (f32[64,128]{1,0:T(8,128)S(1)}, f32[64,128]{1,0:T(8,128)S(1)}, u32[]{:S(2)}, u32[]{:S(2)}) collective-permute-start(f32[64,128]{1,0:T(8,128)S(1)} %add.12), channel_id=1, source_target_pairs={{0,24},{2,26},{4,28},{6,30},{8,16},{10,18},{12,20},{14,22},{16,8},... | collective-permute-start | bytes 98312 | tf_op jit(solution)/shard_map/ppermute | solution.py:460
  20.4 0.2 collective-permute-start.4
  20.7 1.7 %collective-permute-done.6 = f32[64,128]{1,0:T(8,128)S(1)} collective-permute-done((f32[64,128]{1,0:T(8,128)S(1)}, f32[64,128]{1,0:T(8,128)S(1)}, u32[]{:S(2)}, u32[]{:S(2)}) %collective-permute-start.6) | collective-permute-done | bytes 32800 | tf_op jit(solution)/shard_map/ppermute | solution.py:460
  22.4 2.4 %collective-permute-done.5 = f32[64,128]{1,0:T(8,128)S(1)} collective-permute-done((f32[64,128]{1,0:T(8,128)S(1)}, f32[64,128]{1,0:T(8,128)S(1)}, u32[]{:S(2)}, u32[]{:S(2)}) %collective-permute-start.5) | collective-permute-done | bytes 32800 | tf_op jit(solution)/shard_map/ppermute | solution.py:460
  24.8 0.0 collective-permute-done.4
  24.8 0.0 copy-start.4
  24.8 0.0 copy-start.5
  24.8 3.0 %collective-permute-start.11 = (f32[64,128]{1,0:T(8,128)S(1)}, f32[64,128]{1,0:T(8,128)S(1)}, u32[]{:S(2)}, u32[]{:S(2)}) collective-permute-start(f32[64,128]{1,0:T(8,128)S(1)} %add_add_fusion._.mine), channel_id=1, source_target_pairs={{0,5},{1,4},{2,7},{3,6},{4,1},{5,0},{6,3},{7,2},{8,13},{9,12},{10,... | collective-permute-start | bytes 98312 | tf_op jit(solution)/shard_map/ppermute | solution.py:465
  27.8 0.5 %collective-permute-start.10 = (f32[64,128]{1,0:T(8,128)S(1)}, f32[64,128]{1,0:T(8,128)S(1)}, u32[]{:S(2)}, u32[]{:S(2)}) collective-permute-start(f32[64,128]{1,0:T(8,128)S(1)} %add_add_fusion._.mine), channel_id=1, source_target_pairs={{0,1},{1,0},{2,3},{3,2},{4,5},{5,4},{6,7},{7,6},{8,9},{9,8},{10,11... | collective-permute-start | bytes 98312 | tf_op jit(solution)/shard_map/ppermute | solution.py:555
  28.3 0.1 collective-permute-start.9
  28.4 0.0 collective-permute-done.8.far_core.refs_5_
  28.4 0.0 collective-permute-done.7.far_chip.refs_4_
  28.4 1.9 %shard_map.125 = (f32[1024,256]{1,0:T(8,128)S(1)}, f32[1024,256]{1,0:T(8,128)S(1)}) custom-call(f32[4,64,256]{2,1,0:T(8,128)S(1)} %collective-permute-done.from_chip, f32[2,64,256]{2,1,0:T(8,128)S(1)} %collective-permute-done.1.early_core, f32[2,64,256]{2,1,0:T(8,128)S(1)} %collective-permute-done.2.late_core, f32[4,128,256]{2,1,0:T(8,128)S(1)} %bitcast.9, ...), custom_call_target="tpu_custom_call" | custom-call | flops 1000000 | bytes 100000 | tf_op jit(solution)/shard_map/pallas_call | solution.py:443
  30.4 0.0 collective-permute-done.11.others_1_
  30.4 1.3 %collective-permute-done.10.others_0_ = f32[64,128]{1,0:T(8,128)S(1)} collective-permute-done((f32[64,128]{1,0:T(8,128)S(1)}, f32[64,128]{1,0:T(8,128)S(1)}, u32[]{:S(2)}, u32[]{:S(2)}) %collective-permute-start.10) | collective-permute-done | bytes 32800 | tf_op jit(solution)/shard_map/ppermute | solution.py:555
  31.7 0.5 %collective-permute-done.9.received = f32[64,128]{1,0:T(8,128)S(1)} collective-permute-done((f32[64,128]{1,0:T(8,128)S(1)}, f32[64,128]{1,0:T(8,128)S(1)}, u32[]{:S(2)}, u32[]{:S(2)}) %collective-permute-start.9) | collective-permute-done | bytes 32800 | tf_op jit(solution)/shard_map/ppermute | solution.py:460
  32.3 0.1 collective-permute-start.12
  32.3 1.2 %collective-permute-done.12.theirs = f32[72,128]{1,0:T(8,128)S(1)} collective-permute-done((f32[72,128]{1,0:T(8,128)S(1)}, f32[72,128]{1,0:T(8,128)S(1)}, u32[]{:S(2)}, u32[]{:S(2)}) %collective-permute-start.12) | collective-permute-done | bytes 36896 | tf_op jit(solution)/shard_map/ppermute | solution.py:460
  33.5 0.0 copy-done.4
  33.5 0.0 copy-done.5
  33.5 5.3 %shard_map.127 = (f32[4,128,256]{2,1,0:T(8,128)}, f32[128,128]{1,0:T(8,128)}) custom-call(f32[128,128]{1,0:T(8,128)S(1)} %bitcast.15, f32[128,128]{1,0:T(8,128)S(1)} %bitcast.17, f32[72,128]{1,0:T(8,128)S(1)} %shard_map.126.mine, f32[72,128]{1,0:T(8,128)S(1)} %collective-permute-done.12.theirs, f32[1024,256]{1,0:T(8,128)S(1)} %get-tuple-element.41.refs_0_, ...), custom_call_target="tpu_custom_call" | custom-call | flops 1000000 | bytes 100000 | tf_op jit(solution)/shard_map/pallas_call | solution.py:443
  (3 shorter events, 0.0 us)
Async XLA Ops:
  1.6 10.2 %collective-permute-start = (f32[4,64,256]{2,1,0:T(8,128)S(1)}, f32[4,64,256]{2,1,0:T(8,128)S(1)}, u32[]{:S(2)}, u32[]{:S(2)}) collective-permute-start(f32[4,64,256]{2,1,0:T(8,128)S(1)} %shard_map.122.refs_3_), channel_id=1, source_target_pairs={{0,30},{2,4},{4,2},{6,8},{8,6},{10,12},{12,10},{14,16},{16,14},{18... | collective-permute-start | bytes 786440 | tf_op jit(solution)/shard_map/ppermute | solution.py:456
  7.1 4.7 %copy-start = (bf16[768,1024]{1,0:T(8,128)(2,1)S(1)}, bf16[768,1024]{1,0:T(8,128)(2,1)}, u32[]{:S(2)}) copy-start(bf16[768,1024]{1,0:T(8,128)(2,1)} %constant.17.clone.refs_0_.refs_6_) | copy-start | bytes 4718596
  7.1 4.7 %copy-start.1 = (f32[1,4,128,256]{3,2,1,0:T(8,128)S(1)}, f32[1,4,128,256]{3,2,1,0:T(8,128)}, u32[]{:S(2)}) copy-start(f32[1,4,128,256]{3,2,1,0:T(8,128)} %param.11) | copy-start | bytes 1572868
  7.1 4.7 %copy-start.2 = (bf16[512,768]{1,0:T(8,128)(2,1)S(1)}, bf16[512,768]{1,0:T(8,128)(2,1)}, u32[]{:S(2)}) copy-start(bf16[512,768]{1,0:T(8,128)(2,1)} %constant.18.clone.refs_1_.refs_7_) | copy-start | bytes 2359300
  7.1 4.7 %copy-start.3 = (f32[1,4,128,256]{3,2,1,0:T(8,128)S(1)}, f32[1,4,128,256]{3,2,1,0:T(8,128)}, u32[]{:S(2)}) copy-start(f32[1,4,128,256]{3,2,1,0:T(8,128)} %param.12) | copy-start | bytes 1572868
  7.1 4.7 %copy-start.6 = (bf16[1536,768]{1,0:T(8,128)(2,1)S(1)}, bf16[1536,768]{1,0:T(8,128)(2,1)}, u32[]{:S(2)}) copy-start(bf16[1536,768]{1,0:T(8,128)(2,1)} %constant.19.clone.refs_2_) | copy-start | bytes 7077892
  7.1 4.7 %copy-start.7 = (bf16[656,864]{1,0:T(8,128)(2,1)S(1)}, bf16[656,864]{1,0:T(8,128)(2,1)}, u32[]{:S(2)}) copy-start(bf16[656,864]{1,0:T(8,128)(2,1)} %constant.20.clone.refs_3_) | copy-start | bytes 3400708
  10.0 1.4 %collective-permute-start.2 = (f32[2,64,256]{2,1,0:T(8,128)S(1)}, f32[2,64,256]{2,1,0:T(8,128)S(1)}, u32[]{:S(2)}, u32[]{:S(2)}) collective-permute-start(f32[2,64,256]{2,1,0:T(8,128)S(1)} %get-tuple-element.27), channel_id=1, source_target_pairs={{0,2},{2,0},{4,6},{6,4},{8,10},{10,8},{12,14},{14,12},{16,18},{18,... | collective-permute-start | bytes 393224 | tf_op jit(solution)/shard_map/ppermute | solution.py:460
  10.1 1.7 %collective-permute-start.1 = (f32[2,64,256]{2,1,0:T(8,128)S(1)}, f32[2,64,256]{2,1,0:T(8,128)S(1)}, u32[]{:S(2)}, u32[]{:S(2)}) collective-permute-start(f32[2,64,256]{2,1,0:T(8,128)S(1)} %get-tuple-element.25), channel_id=1, source_target_pairs={{0,2},{2,0},{4,6},{6,4},{8,10},{10,8},{12,14},{14,12},{16,18},{18,... | collective-permute-start | bytes 393224 | tf_op jit(solution)/shard_map/ppermute | solution.py:460
  10.6 17.8 %collective-permute-start.8 = (f32[8,64,256]{2,1,0:T(8,128)S(1)}, f32[8,64,256]{2,1,0:T(8,128)S(1)}, u32[]{:S(2)}, u32[]{:S(2)}) collective-permute-start(f32[8,64,256]{2,1,0:T(8,128)S(1)} %get-tuple-element.36), channel_id=1, source_target_pairs={{0,2},{2,0},{4,6},{6,4},{8,10},{10,8},{12,14},{14,12},{16,18},{18,... | collective-permute-start | bytes 1572872 | tf_op jit(solution)/shard_map/ppermute | solution.py:460
  11.4 17.0 %collective-permute-start.7 = (f32[8,64,256]{2,1,0:T(8,128)S(1)}, f32[8,64,256]{2,1,0:T(8,128)S(1)}, u32[]{:S(2)}, u32[]{:S(2)}) collective-permute-start(f32[8,64,256]{2,1,0:T(8,128)S(1)} %get-tuple-element.35), channel_id=1, source_target_pairs={{0,30},{2,4},{4,2},{6,8},{8,6},{10,12},{12,10},{14,16},{16,14},{18... | collective-permute-start | bytes 1572872 | tf_op jit(solution)/shard_map/ppermute | solution.py:456
  15.8 1.3 %collective-permute-start.3 = (f32[64,128]{1,0:T(8,128)S(1)}, f32[64,128]{1,0:T(8,128)S(1)}, u32[]{:S(2)}, u32[]{:S(2)}) collective-permute-start(f32[64,128]{1,0:T(8,128)S(1)} %get-tuple-element.34), channel_id=1, source_target_pairs={{0,2},{2,0},{4,6},{6,4},{8,10},{10,8},{12,14},{14,12},{16,18},{18,... | collective-permute-start | bytes 98312 | tf_op jit(solution)/shard_map/ppermute | solution.py:460
  17.0 5.3 %collective-permute-start.6 = (f32[64,128]{1,0:T(8,128)S(1)}, f32[64,128]{1,0:T(8,128)S(1)}, u32[]{:S(2)}, u32[]{:S(2)}) collective-permute-start(f32[64,128]{1,0:T(8,128)S(1)} %add.12), channel_id=1, source_target_pairs={{0,16},{2,18},{4,20},{6,22},{8,24},{10,26},{12,28},{14,30},{16,0},... | collective-permute-start | bytes 98312 | tf_op jit(solution)/shard_map/ppermute | solution.py:460
  19.1 5.7 %collective-permute-start.5 = (f32[64,128]{1,0:T(8,128)S(1)}, f32[64,128]{1,0:T(8,128)S(1)}, u32[]{:S(2)}, u32[]{:S(2)}) collective-permute-start(f32[64,128]{1,0:T(8,128)S(1)} %add.12), channel_id=1, source_target_pairs={{0,24},{2,26},{4,28},{6,30},{8,16},{10,18},{12,20},{14,22},{16,8},... | collective-permute-start | bytes 98312 | tf_op jit(solution)/shard_map/ppermute | solution.py:460
  20.4 4.4 %collective-permute-start.4 = (f32[64,128]{1,0:T(8,128)S(1)}, f32[64,128]{1,0:T(8,128)S(1)}, u32[]{:S(2)}, u32[]{:S(2)}) collective-permute-start(f32[64,128]{1,0:T(8,128)S(1)} %add.12), channel_id=1, source_target_pairs={{0,8},{2,10},{4,12},{6,14},{8,0},{10,2},{12,4},{14,6},{16,24},{18,... | collective-permute-start | bytes 98312 | tf_op jit(solution)/shard_map/ppermute | solution.py:460
  24.8 8.7 %copy-start.4 = (f32[1,128,128]{2,1,0:T(8,128)S(1)}, f32[1,128,128]{2,1,0:T(8,128)}, u32[]{:S(2)}) copy-start(f32[1,128,128]{2,1,0:T(8,128)} %param.13) | copy-start | bytes 196612
  24.8 8.7 %copy-start.5 = (f32[1,128,128]{2,1,0:T(8,128)S(1)}, f32[1,128,128]{2,1,0:T(8,128)}, u32[]{:S(2)}) copy-start(f32[1,128,128]{2,1,0:T(8,128)} %param.14) | copy-start | bytes 196612
  24.8 5.5 %collective-permute-start.11 = (f32[64,128]{1,0:T(8,128)S(1)}, f32[64,128]{1,0:T(8,128)S(1)}, u32[]{:S(2)}, u32[]{:S(2)}) collective-permute-start(f32[64,128]{1,0:T(8,128)S(1)} %add_add_fusion._.mine), channel_id=1, source_target_pairs={{0,5},{1,4},{2,7},{3,6},{4,1},{5,0},{6,3},{7,2},{8,13},{9,12},{10,... | collective-permute-start | bytes 98312 | tf_op jit(solution)/shard_map/ppermute | solution.py:465
  27.8 3.9 %collective-permute-start.10 = (f32[64,128]{1,0:T(8,128)S(1)}, f32[64,128]{1,0:T(8,128)S(1)}, u32[]{:S(2)}, u32[]{:S(2)}) collective-permute-start(f32[64,128]{1,0:T(8,128)S(1)} %add_add_fusion._.mine), channel_id=1, source_target_pairs={{0,1},{1,0},{2,3},{3,2},{4,5},{5,4},{6,7},{7,6},{8,9},{9,8},{10,11... | collective-permute-start | bytes 98312 | tf_op jit(solution)/shard_map/ppermute | solution.py:555
  28.3 3.9 %collective-permute-start.9 = (f32[64,128]{1,0:T(8,128)S(1)}, f32[64,128]{1,0:T(8,128)S(1)}, u32[]{:S(2)}, u32[]{:S(2)}) collective-permute-start(f32[64,128]{1,0:T(8,128)S(1)} %add_add_fusion._.mine), channel_id=1, source_target_pairs={{0,4},{2,6},{4,0},{6,2},{8,12},{10,14},{12,8},{14,10},{16,20},{18,... | collective-permute-start | bytes 98312 | tf_op jit(solution)/shard_map/ppermute | solution.py:460
  32.3 1.3 %collective-permute-start.12 = (f32[72,128]{1,0:T(8,128)S(1)}, f32[72,128]{1,0:T(8,128)S(1)}, u32[]{:S(2)}, u32[]{:S(2)}) collective-permute-start(f32[72,128]{1,0:T(8,128)S(1)} %shard_map.126.mine), channel_id=1, source_target_pairs={{0,2},{2,0},{4,6},{6,4},{8,10},{10,8},{12,14},{14,12},{16,18},{18,... | collective-permute-start | bytes 110600 | tf_op jit(solution)/shard_map/ppermute | solution.py:460

commit v2 on v1

--- a/solution.py
+++ b/solution.py
@@ -406,15 +406,17 @@
     even, odd, own, observed, far_chip, far_core, *refs = refs
     planes, rows, cols = own.shape
     const = at(*refs[:arrays])
-    psf_const = psf_at(*refs[arrays:-2])
-    objects_out, phase_out = refs[-2:]
+    psf_const = psf_at(*refs[arrays:-5])
+    objects_out, phase_out, objects, new_phase, sems = refs[-5:]
+    writes = [pltpu.make_async_copy(new_phase, phase_out, sems.at[planes])]
     half = phase.shape[0] // 2
     first, second = halo_rows(mine[:half], theirs[:half])
     slope = jnp.concatenate([first, second], 0)
     summed = squares[...] if squares_apart else mine[half:] + theirs[half:]
     mean_square = total(summed) * (1.0 / cells)
     updated = phase[...] - STEP_SIZE * slope / jnp.sqrt(mean_square + EPSILON)
-    phase_out[...] = updated
+    new_phase[...] = updated
+    writes[0].start()
     _, _, spec, _ = point_spread(updated, amplitude[...], psf_const)
     spec_even, spec_odd = spec[:, :cols], spec[:, cols:]
     freqs = spec.shape[0]
@@ -432,10 +434,14 @@
     ratio_even, ratio_odd = forward(ratios, const["row_forward"], const)
     correction = inverse(times(ratio_even, spec_even, True), times(ratio_odd, spec_odd, True), freqs, const)
     for p in range(planes):
-        objects_out[p] = own[p] * correction[p]
-
-
-def call(kernel, out_shapes, args, flops=10**6, spaces=None, scratch=()):
+        objects[p] = own[p] * correction[p]
+        writes.append(pltpu.make_async_copy(objects.at[p], objects_out.at[p], sems.at[p]))
+        writes[-1].start()
+    for write in writes:
+        write.wait()
+
+
+def call(kernel, out_shapes, args, flops=10**6, spaces=None, scratch=(), out_space=pltpu.VMEM):
     outs = [
         jax.ShapeDtypeStruct(shape, jnp.float32) if isinstance(shape, tuple) else shape for shape in out_shapes
     ]
@@ -444,7 +450,7 @@
         kernel,
         out_shape=outs,
         in_specs=[pl.BlockSpec(memory_space=spaces.get(i, pltpu.VMEM)) for i in range(len(args))],
-        out_specs=[pl.BlockSpec(memory_space=pltpu.VMEM)] * len(outs),
+        out_specs=[pl.BlockSpec(memory_space=out_space)] * len(outs),
         scratch_shapes=scratch,
         compiler_params=pltpu.CompilerParams(vmem_limit_bytes=VMEM_LIMIT),
         cost_estimate=pl.CostEstimate(flops=flops, bytes_accessed=10**5, transcendentals=0),
@@ -579,6 +585,9 @@
             phase, amplitude, joined, other, *squares, even, odd, picture, measured,
             far_chip, far_core, *block_arrays, *psf_arrays,
         ),
+        scratch=[pltpu.VMEM(value.shape, jnp.float32) for value in (picture, phase)]
+        + [pltpu.SemaphoreType.DMA((planes + 1,))],
+        out_space=pltpu.HBM,
     )
     return new_objects[None], new_phase[None]
 

time: 39 us -> 38.9 us (level)
  no operation moved by 1% of the time
where the time goes in v2:
time: 38.9 us; the launch traced here: 38.8 us
  Pallas kernels  14.9 us (38%)
  starting transfers between devices  14 us (36%)
  waiting for transfers between devices  9.04 us (23%)
  between operations  0.78 us (2%)
    pallas_call x6, Pallas kernels, call(): pl.pallas_call(kernel, out_shape=outs, in_specs=[pl.BlockSpec(memory_spac...  14.9 us
    ppermute x9, waiting for transfers between devices, exchange(): lax.ppermute(value, 'tile', [(i, i ^ step) for i in range(lax.axis_size('...  7.7 us
    ppermute x2, starting transfers between devices, to_next_chip(): lax.ppermute(value, 'tile', [(i, (i + 1 if i % 2 else i - 1) % count) for...  5.88 us
    ppermute x9, starting transfers between devices, exchange(): lax.ppermute(value, 'tile', [(i, i ^ step) for i in range(lax.axis_size('...  4.63 us
    ppermute x1, starting transfers between devices, across_depth_and_chip(): return lax.ppermute(value, ('tile', 'depth'), pairs)  2.97 us
    ppermute x1, waiting for transfers between devices, on_device(): lax.ppermute(half, 'depth', [(0, 1), (1, 0)])  1.32 us
  transfers between devices with their start and end apart: 13, of which 7 were waited for; matrix products, arithmetic and copies ran while one was open for 0% of the time, Pallas kernels for 22%

profile of v2, /device:TPU:0, one launch (start us, length us, event | category | flops | bytes accessed | tf_op | source)
XLA Modules:
  0.0 38.8 jit_solution(263270933219447322)
XLA Ops:
  0.6 1.0 %shard_map.122.refs_3_ = f32[4,64,256]{2,1,0:T(8,128)S(1)} custom-call(f32[4,128,256]{2,1,0:T(8,128)} %bitcast.6), custom_call_target="tpu_custom_call" | custom-call | flops 1000000 | bytes 100000 | tf_op jit(solution)/shard_map/pallas_call | solution.py:449
  1.6 5.5 %collective-permute-start = (f32[4,64,256]{2,1,0:T(8,128)S(1)}, f32[4,64,256]{2,1,0:T(8,128)S(1)}, u32[]{:S(2)}, u32[]{:S(2)}) collective-permute-start(f32[4,64,256]{2,1,0:T(8,128)S(1)} %shard_map.122.refs_3_), channel_id=1, source_target_pairs={{0,30},{2,4},{4,2},{6,8},{8,6},{10,12},{12,10},{14,16},{16,14},{18... | collective-permute-start | bytes 786440 | tf_op jit(solution)/shard_map/ppermute | solution.py:462
  7.1 0.0 copy-start
  7.1 0.0 copy-start.1
  7.1 0.0 copy-start.2
  7.1 0.0 copy-start.3
  7.1 0.0 copy-start.6
  7.1 0.0 copy-start.7
  7.2 2.9 %shard_map.123 = (f32[128,256]{1,0:T(8,128)S(1)}, f32[288,256]{1,0:T(8,128)S(1)}, f32[128,512]{1,0:T(8,128)S(1)}, f32[8,64,256]{2,1,0:T(8,128)S(1)}, f32[8,64,25...) custom-call(f32[128,128]{1,0:T(8,128)} %bitcast.14, ...), custom_call_target="tpu_custom_call" | custom-call | flops 3000000000 | bytes 100000 | tf_op jit(solution)/shard_map/pallas_call | solution.py:449
  10.0 0.1 collective-permute-start.2
  10.1 0.5 %collective-permute-start.1 = (f32[2,64,256]{2,1,0:T(8,128)S(1)}, f32[2,64,256]{2,1,0:T(8,128)S(1)}, u32[]{:S(2)}, u32[]{:S(2)}) collective-permute-start(f32[2,64,256]{2,1,0:T(8,128)S(1)} %get-tuple-element.25), channel_id=1, source_target_pairs={{0,2},{2,0},{4,6},{6,4},{8,10},{10,8},{12,14},{14,12},{16,18},{18,... | collective-permute-start | bytes 393224 | tf_op jit(solution)/shard_map/ppermute | solution.py:466
  10.6 0.1 collective-permute-start.8
  10.7 0.8 %collective-permute-done.2.late_core = f32[2,64,256]{2,1,0:T(8,128)S(1)} collective-permute-done((f32[2,64,256]{2,1,0:T(8,128)S(1)}, f32[2,64,256]{2,1,0:T(8,128)S(1)}, u32[]{:S(2)}, u32[]{:S(2)}) %collective-permute-start.2) | collective-permute-done | bytes 131104 | tf_op jit(solution)/shard_map/ppermute | solution.py:466
  11.4 0.4 collective-permute-start.7
  11.8 0.0 collective-permute-done.1.early_core
  11.8 0.0 collective-permute-done.from_chip
  11.8 0.0 copy-done
  11.8 0.0 copy-done.1
  11.8 0.0 copy-done.2
  11.9 0.0 copy-done.3
  11.9 0.0 copy-done.6
  11.9 0.0 copy-done.7
  11.9 3.9 %shard_map.124 = (f32[64,128]{1,0:T(8,128)S(1)}, f32[64,128]{1,0:T(8,128)S(1)}) custom-call(f32[4,64,256]{2,1,0:T(8,128)S(1)} %collective-permute-done.from_chip, f32[2,64,256]{2,1,0:T(8,128)S(1)} %collective-permute-done.1.early_core, f32[2,64,256]{2,1,0:T(8,128)S(1)} %collective-permute-done.2.late_core, f32[4,128,256]{2,1,0:T(8,128)S(1)} %bitcast.8, ...), custom_call_target="tpu_custom_call" | custom-call | flops 40000000000 | bytes 100000 | tf_op jit(solution)/shard_map/pallas_call | solution.py:449
  15.8 0.2 collective-permute-start.3
  16.0 1.1 %collective-permute-done.3 = f32[64,128]{1,0:T(8,128)S(1)} collective-permute-done((f32[64,128]{1,0:T(8,128)S(1)}, f32[64,128]{1,0:T(8,128)S(1)}, u32[]{:S(2)}, u32[]{:S(2)}) %collective-permute-start.3) | collective-permute-done | bytes 32800 | tf_op jit(solution)/shard_map/ppermute | solution.py:466
  17.0 2.0 %collective-permute-start.6 = (f32[64,128]{1,0:T(8,128)S(1)}, f32[64,128]{1,0:T(8,128)S(1)}, u32[]{:S(2)}, u32[]{:S(2)}) collective-permute-start(f32[64,128]{1,0:T(8,128)S(1)} %add.12), channel_id=1, source_target_pairs={{0,16},{2,18},{4,20},{6,22},{8,24},{10,26},{12,28},{14,30},{16,0},... | collective-permute-start | bytes 98312 | tf_op jit(solution)/shard_map/ppermute | solution.py:466
  19.1 1.4 %collective-permute-start.5 = (f32[64,128]{1,0:T(8,128)S(1)}, f32[64,128]{1,0:T(8,128)S(1)}, u32[]{:S(2)}, u32[]{:S(2)}) collective-permute-start(f32[64,128]{1,0:T(8,128)S(1)} %add.12), channel_id=1, source_target_pairs={{0,24},{2,26},{4,28},{6,30},{8,16},{10,18},{12,20},{14,22},{16,8},... | collective-permute-start | bytes 98312 | tf_op jit(solution)/shard_map/ppermute | solution.py:466
  20.4 0.2 collective-permute-start.4
  20.7 1.7 %collective-permute-done.6 = f32[64,128]{1,0:T(8,128)S(1)} collective-permute-done((f32[64,128]{1,0:T(8,128)S(1)}, f32[64,128]{1,0:T(8,128)S(1)}, u32[]{:S(2)}, u32[]{:S(2)}) %collective-permute-start.6) | collective-permute-done | bytes 32800 | tf_op jit(solution)/shard_map/ppermute | solution.py:466
  22.4 2.4 %collective-permute-done.5 = f32[64,128]{1,0:T(8,128)S(1)} collective-permute-done((f32[64,128]{1,0:T(8,128)S(1)}, f32[64,128]{1,0:T(8,128)S(1)}, u32[]{:S(2)}, u32[]{:S(2)}) %collective-permute-start.5) | collective-permute-done | bytes 32800 | tf_op jit(solution)/shard_map/ppermute | solution.py:466
  24.8 0.0 collective-permute-done.4
  24.8 0.0 copy-start.4
  24.8 0.0 copy-start.5
  24.8 3.0 %collective-permute-start.11 = (f32[64,128]{1,0:T(8,128)S(1)}, f32[64,128]{1,0:T(8,128)S(1)}, u32[]{:S(2)}, u32[]{:S(2)}) collective-permute-start(f32[64,128]{1,0:T(8,128)S(1)} %add_add_fusion._.mine), channel_id=1, source_target_pairs={{0,5},{1,4},{2,7},{3,6},{4,1},{5,0},{6,3},{7,2},{8,13},{9,12},{10,... | collective-permute-start | bytes 98312 | tf_op jit(solution)/shard_map/ppermute | solution.py:471
  27.8 0.5 %collective-permute-start.10 = (f32[64,128]{1,0:T(8,128)S(1)}, f32[64,128]{1,0:T(8,128)S(1)}, u32[]{:S(2)}, u32[]{:S(2)}) collective-permute-start(f32[64,128]{1,0:T(8,128)S(1)} %add_add_fusion._.mine), channel_id=1, source_target_pairs={{0,1},{1,0},{2,3},{3,2},{4,5},{5,4},{6,7},{7,6},{8,9},{9,8},{10,11... | collective-permute-start | bytes 98312 | tf_op jit(solution)/shard_map/ppermute | solution.py:561
  28.3 0.1 collective-permute-start.9
  28.4 0.0 collective-permute-done.8.far_core.refs_5_
  28.4 0.0 collective-permute-done.7.far_chip.refs_4_
  28.4 1.9 %shard_map.125 = (f32[1024,256]{1,0:T(8,128)S(1)}, f32[1024,256]{1,0:T(8,128)S(1)}) custom-call(f32[4,64,256]{2,1,0:T(8,128)S(1)} %collective-permute-done.from_chip, f32[2,64,256]{2,1,0:T(8,128)S(1)} %collective-permute-done.1.early_core, f32[2,64,256]{2,1,0:T(8,128)S(1)} %collective-permute-done.2.late_core, f32[4,128,256]{2,1,0:T(8,128)S(1)} %bitcast.9, ...), custom_call_target="tpu_custom_call" | custom-call | flops 1000000 | bytes 100000 | tf_op jit(solution)/shard_map/pallas_call | solution.py:449
  30.4 0.0 collective-permute-done.11.others_1_
  30.4 1.3 %collective-permute-done.10.others_0_ = f32[64,128]{1,0:T(8,128)S(1)} collective-permute-done((f32[64,128]{1,0:T(8,128)S(1)}, f32[64,128]{1,0:T(8,128)S(1)}, u32[]{:S(2)}, u32[]{:S(2)}) %collective-permute-start.10) | collective-permute-done | bytes 32800 | tf_op jit(solution)/shard_map/ppermute | solution.py:561
  31.7 0.5 %collective-permute-done.9.received = f32[64,128]{1,0:T(8,128)S(1)} collective-permute-done((f32[64,128]{1,0:T(8,128)S(1)}, f32[64,128]{1,0:T(8,128)S(1)}, u32[]{:S(2)}, u32[]{:S(2)}) %collective-permute-start.9) | collective-permute-done | bytes 32800 | tf_op jit(solution)/shard_map/ppermute | solution.py:466
  32.3 0.1 collective-permute-start.12
  32.3 1.2 %collective-permute-done.12.theirs = f32[72,128]{1,0:T(8,128)S(1)} collective-permute-done((f32[72,128]{1,0:T(8,128)S(1)}, f32[72,128]{1,0:T(8,128)S(1)}, u32[]{:S(2)}, u32[]{:S(2)}) %collective-permute-start.12) | collective-permute-done | bytes 36896 | tf_op jit(solution)/shard_map/ppermute | solution.py:466
  33.5 0.0 copy-done.4
  33.5 0.0 copy-done.5
  33.5 5.3 %shard_map.127 = (f32[4,128,256]{2,1,0:T(8,128)}, f32[128,128]{1,0:T(8,128)}) custom-call(f32[128,128]{1,0:T(8,128)S(1)} %bitcast.15, f32[128,128]{1,0:T(8,128)S(1)} %bitcast.17, f32[72,128]{1,0:T(8,128)S(1)} %shard_map.126.mine, f32[72,128]{1,0:T(8,128)S(1)} %collective-permute-done.12.theirs, f32[1024,256]{1,0:T(8,128)S(1)} %get-tuple-element.41.refs_0_, ...), custom_call_target="tpu_custom_call" | custom-call | flops 1000000 | bytes 100000 | tf_op jit(solution)/shard_map/pallas_call | solution.py:449
  (3 shorter events, 0.0 us)
Async XLA Ops:
  1.6 10.2 %collective-permute-start = (f32[4,64,256]{2,1,0:T(8,128)S(1)}, f32[4,64,256]{2,1,0:T(8,128)S(1)}, u32[]{:S(2)}, u32[]{:S(2)}) collective-permute-start(f32[4,64,256]{2,1,0:T(8,128)S(1)} %shard_map.122.refs_3_), channel_id=1, source_target_pairs={{0,30},{2,4},{4,2},{6,8},{8,6},{10,12},{12,10},{14,16},{16,14},{18... | collective-permute-start | bytes 786440 | tf_op jit(solution)/shard_map/ppermute | solution.py:462
  7.1 4.7 %copy-start = (bf16[768,1024]{1,0:T(8,128)(2,1)S(1)}, bf16[768,1024]{1,0:T(8,128)(2,1)}, u32[]{:S(2)}) copy-start(bf16[768,1024]{1,0:T(8,128)(2,1)} %constant.17.clone.refs_0_.refs_6_) | copy-start | bytes 4718596
  7.1 4.7 %copy-start.1 = (f32[1,4,128,256]{3,2,1,0:T(8,128)S(1)}, f32[1,4,128,256]{3,2,1,0:T(8,128)}, u32[]{:S(2)}) copy-start(f32[1,4,128,256]{3,2,1,0:T(8,128)} %param.11) | copy-start | bytes 1572868
  7.1 4.7 %copy-start.2 = (bf16[512,768]{1,0:T(8,128)(2,1)S(1)}, bf16[512,768]{1,0:T(8,128)(2,1)}, u32[]{:S(2)}) copy-start(bf16[512,768]{1,0:T(8,128)(2,1)} %constant.18.clone.refs_1_.refs_7_) | copy-start | bytes 2359300
  7.1 4.7 %copy-start.3 = (f32[1,4,128,256]{3,2,1,0:T(8,128)S(1)}, f32[1,4,128,256]{3,2,1,0:T(8,128)}, u32[]{:S(2)}) copy-start(f32[1,4,128,256]{3,2,1,0:T(8,128)} %param.12) | copy-start | bytes 1572868
  7.1 4.7 %copy-start.6 = (bf16[1536,768]{1,0:T(8,128)(2,1)S(1)}, bf16[1536,768]{1,0:T(8,128)(2,1)}, u32[]{:S(2)}) copy-start(bf16[1536,768]{1,0:T(8,128)(2,1)} %constant.19.clone.refs_2_) | copy-start | bytes 7077892
  7.1 4.7 %copy-start.7 = (bf16[656,864]{1,0:T(8,128)(2,1)S(1)}, bf16[656,864]{1,0:T(8,128)(2,1)}, u32[]{:S(2)}) copy-start(bf16[656,864]{1,0:T(8,128)(2,1)} %constant.20.clone.refs_3_) | copy-start | bytes 3400708
  10.0 1.4 %collective-permute-start.2 = (f32[2,64,256]{2,1,0:T(8,128)S(1)}, f32[2,64,256]{2,1,0:T(8,128)S(1)}, u32[]{:S(2)}, u32[]{:S(2)}) collective-permute-start(f32[2,64,256]{2,1,0:T(8,128)S(1)} %get-tuple-element.27), channel_id=1, source_target_pairs={{0,2},{2,0},{4,6},{6,4},{8,10},{10,8},{12,14},{14,12},{16,18},{18,... | collective-permute-start | bytes 393224 | tf_op jit(solution)/shard_map/ppermute | solution.py:466
  10.1 1.7 %collective-permute-start.1 = (f32[2,64,256]{2,1,0:T(8,128)S(1)}, f32[2,64,256]{2,1,0:T(8,128)S(1)}, u32[]{:S(2)}, u32[]{:S(2)}) collective-permute-start(f32[2,64,256]{2,1,0:T(8,128)S(1)} %get-tuple-element.25), channel_id=1, source_target_pairs={{0,2},{2,0},{4,6},{6,4},{8,10},{10,8},{12,14},{14,12},{16,18},{18,... | collective-permute-start | bytes 393224 | tf_op jit(solution)/shard_map/ppermute | solution.py:466
  10.6 17.8 %collective-permute-start.8 = (f32[8,64,256]{2,1,0:T(8,128)S(1)}, f32[8,64,256]{2,1,0:T(8,128)S(1)}, u32[]{:S(2)}, u32[]{:S(2)}) collective-permute-start(f32[8,64,256]{2,1,0:T(8,128)S(1)} %get-tuple-element.36), channel_id=1, source_target_pairs={{0,2},{2,0},{4,6},{6,4},{8,10},{10,8},{12,14},{14,12},{16,18},{18,... | collective-permute-start | bytes 1572872 | tf_op jit(solution)/shard_map/ppermute | solution.py:466
  11.4 17.0 %collective-permute-start.7 = (f32[8,64,256]{2,1,0:T(8,128)S(1)}, f32[8,64,256]{2,1,0:T(8,128)S(1)}, u32[]{:S(2)}, u32[]{:S(2)}) collective-permute-start(f32[8,64,256]{2,1,0:T(8,128)S(1)} %get-tuple-element.35), channel_id=1, source_target_pairs={{0,30},{2,4},{4,2},{6,8},{8,6},{10,12},{12,10},{14,16},{16,14},{18... | collective-permute-start | bytes 1572872 | tf_op jit(solution)/shard_map/ppermute | solution.py:462
  15.8 1.3 %collective-permute-start.3 = (f32[64,128]{1,0:T(8,128)S(1)}, f32[64,128]{1,0:T(8,128)S(1)}, u32[]{:S(2)}, u32[]{:S(2)}) collective-permute-start(f32[64,128]{1,0:T(8,128)S(1)} %get-tuple-element.34), channel_id=1, source_target_pairs={{0,2},{2,0},{4,6},{6,4},{8,10},{10,8},{12,14},{14,12},{16,18},{18,... | collective-permute-start | bytes 98312 | tf_op jit(solution)/shard_map/ppermute | solution.py:466
  17.0 5.3 %collective-permute-start.6 = (f32[64,128]{1,0:T(8,128)S(1)}, f32[64,128]{1,0:T(8,128)S(1)}, u32[]{:S(2)}, u32[]{:S(2)}) collective-permute-start(f32[64,128]{1,0:T(8,128)S(1)} %add.12), channel_id=1, source_target_pairs={{0,16},{2,18},{4,20},{6,22},{8,24},{10,26},{12,28},{14,30},{16,0},... | collective-permute-start | bytes 98312 | tf_op jit(solution)/shard_map/ppermute | solution.py:466
  19.1 5.7 %collective-permute-start.5 = (f32[64,128]{1,0:T(8,128)S(1)}, f32[64,128]{1,0:T(8,128)S(1)}, u32[]{:S(2)}, u32[]{:S(2)}) collective-permute-start(f32[64,128]{1,0:T(8,128)S(1)} %add.12), channel_id=1, source_target_pairs={{0,24},{2,26},{4,28},{6,30},{8,16},{10,18},{12,20},{14,22},{16,8},... | collective-permute-start | bytes 98312 | tf_op jit(solution)/shard_map/ppermute | solution.py:466
  20.4 4.4 %collective-permute-start.4 = (f32[64,128]{1,0:T(8,128)S(1)}, f32[64,128]{1,0:T(8,128)S(1)}, u32[]{:S(2)}, u32[]{:S(2)}) collective-permute-start(f32[64,128]{1,0:T(8,128)S(1)} %add.12), channel_id=1, source_target_pairs={{0,8},{2,10},{4,12},{6,14},{8,0},{10,2},{12,4},{14,6},{16,24},{18,... | collective-permute-start | bytes 98312 | tf_op jit(solution)/shard_map/ppermute | solution.py:466
  24.8 8.7 %copy-start.4 = (f32[1,128,128]{2,1,0:T(8,128)S(1)}, f32[1,128,128]{2,1,0:T(8,128)}, u32[]{:S(2)}) copy-start(f32[1,128,128]{2,1,0:T(8,128)} %param.13) | copy-start | bytes 196612
  24.8 8.7 %copy-start.5 = (f32[1,128,128]{2,1,0:T(8,128)S(1)}, f32[1,128,128]{2,1,0:T(8,128)}, u32[]{:S(2)}) copy-start(f32[1,128,128]{2,1,0:T(8,128)} %param.14) | copy-start | bytes 196612
  24.8 5.5 %collective-permute-start.11 = (f32[64,128]{1,0:T(8,128)S(1)}, f32[64,128]{1,0:T(8,128)S(1)}, u32[]{:S(2)}, u32[]{:S(2)}) collective-permute-start(f32[64,128]{1,0:T(8,128)S(1)} %add_add_fusion._.mine), channel_id=1, source_target_pairs={{0,5},{1,4},{2,7},{3,6},{4,1},{5,0},{6,3},{7,2},{8,13},{9,12},{10,... | collective-permute-start | bytes 98312 | tf_op jit(solution)/shard_map/ppermute | solution.py:471
  27.8 3.9 %collective-permute-start.10 = (f32[64,128]{1,0:T(8,128)S(1)}, f32[64,128]{1,0:T(8,128)S(1)}, u32[]{:S(2)}, u32[]{:S(2)}) collective-permute-start(f32[64,128]{1,0:T(8,128)S(1)} %add_add_fusion._.mine), channel_id=1, source_target_pairs={{0,1},{1,0},{2,3},{3,2},{4,5},{5,4},{6,7},{7,6},{8,9},{9,8},{10,11... | collective-permute-start | bytes 98312 | tf_op jit(solution)/shard_map/ppermute | solution.py:561
  28.3 3.9 %collective-permute-start.9 = (f32[64,128]{1,0:T(8,128)S(1)}, f32[64,128]{1,0:T(8,128)S(1)}, u32[]{:S(2)}, u32[]{:S(2)}) collective-permute-start(f32[64,128]{1,0:T(8,128)S(1)} %add_add_fusion._.mine), channel_id=1, source_target_pairs={{0,4},{2,6},{4,0},{6,2},{8,12},{10,14},{12,8},{14,10},{16,20},{18,... | collective-permute-start | bytes 98312 | tf_op jit(solution)/shard_map/ppermute | solution.py:466
  32.3 1.3 %collective-permute-start.12 = (f32[72,128]{1,0:T(8,128)S(1)}, f32[72,128]{1,0:T(8,128)S(1)}, u32[]{:S(2)}, u32[]{:S(2)}) collective-permute-start(f32[72,128]{1,0:T(8,128)S(1)} %shard_map.126.mine), channel_id=1, source_target_pairs={{0,2},{2,0},{4,6},{6,4},{8,10},{10,8},{12,14},{14,12},{16,18},{18,... | collective-permute-start | bytes 110600 | tf_op jit(solution)/shard_map/ppermute | solution.py:466

commit v3 on v2

--- a/solution.py
+++ b/solution.py
@@ -197,21 +197,26 @@
     return pupil, field, spectrum * norm, norm
 
 
-def forward(strips, row_matrix, const, levels=None):
+def mixed_halves(strip, level=None):
+    half = strip.shape[1] // 2
+    first, second = strip[:, :half], strip[:, half:]
+    both = first + second if level is None else first + second - 2.0 * level
+    return jnp.concatenate([both, first - second], 1)
+
+
+def columns(mixed, const):
     sums, differences = [], []
-    for plane, strip in enumerate(strips):
-        half = strip.shape[1] // 2
-        first, second = strip[:, :half], strip[:, half:]
-        both = first + second
-        if levels is not None:
-            both = both - 2.0 * levels[plane]
-        mixed = left_by(row_matrix, jnp.concatenate([both, first - second], 1))
-        freqs = mixed.shape[0] // 2
-        sums.append(jnp.concatenate([mixed[:freqs, :half], mixed[freqs:, :half]], 1))
-        differences.append(jnp.concatenate([mixed[:freqs, half:], mixed[freqs:, half:]], 1))
+    for strip in mixed:
+        half, freqs = strip.shape[1] // 2, strip.shape[0] // 2
+        sums.append(jnp.concatenate([strip[:freqs, :half], strip[freqs:, :half]], 1))
+        differences.append(jnp.concatenate([strip[:freqs, half:], strip[freqs:, half:]], 1))
     even = [right_by(jnp.concatenate(sums[p : p + 2], 0), const["forward_even"]) for p in range(0, len(sums), 2)]
     odd = [right_by(jnp.concatenate(differences[p : p + 2], 0), const["forward_odd"]) for p in range(0, len(sums), 2)]
     return even, odd
+
+
+def forward(strips, row_matrix, const):
+    return columns([left_by(row_matrix, mixed_halves(strip)) for strip in strips], const)
 
 
 def inverse(even, odd, freqs, const):
@@ -326,20 +331,28 @@
     return jnp.where(even, chip, core), jnp.where(even, core, chip)
 
 
+def known_kernel(own, means, *refs, at):
+    const, known_out = at(*refs[:-1]), refs[-1]
+    for p in range(own.shape[0]):
+        known_out[p] = left_by(const["row_own"], mixed_halves(own[p], means[p][:1, :1]))
+
+
 def gradient_kernel(
-    from_chip, early_core, late_core, own, observed, spec, pupil, field, means, *refs, at,
+    from_chip, early_core, late_core, known, observed, spec, pupil, field, means, *refs, at,
 ):
-    planes, rows, cols = own.shape
+    planes = known.shape[0]
+    cols = known.shape[2]
     const = at(*refs[:-2])
     keep_out, give_out = refs[-2:]
     freqs = spec.shape[0]
     early = early_core.shape[0]
-    strips = []
+    levels = [means[p][:1, :1] for p in range(planes)]
+    mixed = []
     for p in range(planes):
-        above, below = halo_rows(from_chip[p], early_core[p] if p < early else late_core[p - early])
-        strips.append(jnp.concatenate([above, own[p], below], 0))
-    levels = [means[p][:1, :1] for p in range(planes)]
-    even, odd = forward(strips, const["row_forward"], const, levels)
+        edges = halo_rows(from_chip[p], early_core[p] if p < early else late_core[p - early])
+        edges = mixed_halves(jnp.concatenate(edges, 0), levels[p])
+        mixed.append(known[p] + left_by(const["row_edges"], edges))
+    even, odd = columns(mixed, const)
     blurred = inverse(times(even, spec[:, :cols], False), times(odd, spec[:, cols:], False), freqs, const)
     misfit = [1.0 - observed[p] / (blurred[p] + (levels[p] + BACKGROUND)) for p in range(planes)]
     weighted = misfit[0] * blurred[0]
@@ -506,19 +519,21 @@
     block_const = Joined(block_left, block_right)
     lag_const = Joined(
         {
-            "row_own": row_forward[:, HALF : HALF + rows],
+            "row_edges": np.concatenate([row_forward[:, :HALF], row_forward[:, HALF + rows :]], 1),
             "lag_left": kernel_rows.T * (2.0 / length),
             "adjoint_left": pupil_left.T,
         },
         {"lag_right": kernel_right.T / cols, "adjoint_right": pupil_right.T},
     )
-    psf_arrays, block_arrays, lag_arrays = (
-        [jnp.asarray(array) for array in const.arrays] for const in (psf_const, block_const, lag_const)
+    own_const = Joined({"row_own": row_forward[:, HALF : HALF + rows]}, {})
+    psf_arrays, block_arrays, lag_arrays, own_arrays = (
+        [jnp.asarray(array) for array in const.arrays] for const in (psf_const, block_const, lag_const, own_const)
     )
 
     def gradient_at(*refs):
         held = len(block_arrays)
-        return {**block_const.at(*refs[:held]), **lag_const.at(*refs[held:])}
+        end = held + len(lag_arrays)
+        return {**block_const.at(*refs[:held]), **lag_const.at(*refs[held:end]), **own_const.at(*refs[end:])}
 
     in_hbm = [
         pltpu.with_memory_space_constraint(value, pltpu.HBM)
@@ -541,12 +556,21 @@
         + [pltpu.SemaphoreType.DMA((9 + len(psf_arrays),))],
     )
     early_core, late_core, far_core = (exchange(value, 1) for value in (early_rows, late_rows, far_core))
-    far_chip, late_core = lax.optimization_barrier((far_chip, late_core))
+    (known,) = call(
+        functools.partial(known_kernel, at=own_const.at),
+        [(planes, length, cols)],
+        (picture, means, *own_arrays),
+        flops=10**3,
+    )
+    far_chip, late_core, known = lax.optimization_barrier((far_chip, late_core, known))
     far_chip = to_next_chip(far_chip)
     keep, give = call(
         functools.partial(gradient_kernel, at=gradient_at),
         [(pup // 2, pup)] * 2,
-        (from_chip, early_core, late_core, picture, measured, spec, pupil, field, means, *block_arrays, *lag_arrays),
+        (
+            from_chip, early_core, late_core, known, measured, spec, pupil, field, means, *block_arrays, *lag_arrays,
+            *own_arrays,
+        ),
         flops=4 * 10**10,
     )
     half = keep + exchange(give, 1)

time: 38.9 us -> 38.8 us (level)
  waiting for transfers between devices: 9.04 us -> 8.65 us
    pallas_call x6 -> x7, Pallas kernels: 14.9 us -> 15.2 us  [call(): pl.pallas_call(kernel, out_shape=outs, in_specs=[pl.BlockSpec(memory_spac...]
  transfers between devices with their start and end apart: 13 -> 13, of which waited for: 7 -> 7; matrix products, arithmetic and copies ran while one was open for 0% -> 0% of each run, Pallas kernels for 22% -> 23%
where the time goes in v3:
time: 38.8 us; the launch traced here: 38.6 us
  Pallas kernels  15.2 us (39%)
  starting transfers between devices  13.9 us (36%)
  waiting for transfers between devices  8.65 us (22%)
  between operations  0.78 us (2%)
    pallas_call x7, Pallas kernels, call(): pl.pallas_call(kernel, out_shape=outs, in_specs=[pl.BlockSpec(memory_spac...  15.2 us
    ppermute x9, waiting for transfers between devices, exchange(): lax.ppermute(value, 'tile', [(i, i ^ step) for i in range(lax.axis_size('...  7.32 us
    ppermute x2, starting transfers between devices, to_next_chip(): lax.ppermute(value, 'tile', [(i, (i + 1 if i % 2 else i - 1) % count) for...  5.98 us
    ppermute x9, starting transfers between devices, exchange(): lax.ppermute(value, 'tile', [(i, i ^ step) for i in range(lax.axis_size('...  4.4 us
    ppermute x1, starting transfers between devices, across_depth_and_chip(): return lax.ppermute(value, ('tile', 'depth'), pairs)  2.96 us
    ppermute x1, waiting for transfers between devices, on_device(): lax.ppermute(half, 'depth', [(0, 1), (1, 0)])  1.33 us
  transfers between devices with their start and end apart: 13, of which 7 were waited for; matrix products, arithmetic and copies ran while one was open for 0% of the time, Pallas kernels for 23%

profile of v3, /device:TPU:0, one launch (start us, length us, event | category | flops | bytes accessed | tf_op | source)
XLA Modules:
  0.0 38.6 jit_solution(4237002551760164899)
XLA Ops:
  0.6 1.0 %shard_map.131.refs_3_ = f32[4,64,256]{2,1,0:T(8,128)S(1)} custom-call(f32[4,128,256]{2,1,0:T(8,128)} %bitcast.6), custom_call_target="tpu_custom_call" | custom-call | flops 1000000 | bytes 100000 | tf_op jit(solution)/shard_map/pallas_call | solution.py:462
  1.6 5.5 %collective-permute-start = (f32[4,64,256]{2,1,0:T(8,128)S(1)}, f32[4,64,256]{2,1,0:T(8,128)S(1)}, u32[]{:S(2)}, u32[]{:S(2)}) collective-permute-start(f32[4,64,256]{2,1,0:T(8,128)S(1)} %shard_map.131.refs_3_), channel_id=1, source_target_pairs={{0,30},{2,4},{4,2},{6,8},{8,6},{10,12},{12,10},{14,16},{16,14},{18... | collective-permute-start | bytes 786440 | tf_op jit(solution)/shard_map/ppermute | solution.py:475
  7.1 0.0 copy-start
  7.1 0.0 copy-start.4
  7.1 0.0 copy-start.2
  7.1 0.0 copy-start.3
  7.1 0.0 copy-start.7
  7.1 0.0 copy-start.8
  7.2 2.9 %shard_map.132 = (f32[128,256]{1,0:T(8,128)S(1)}, f32[288,256]{1,0:T(8,128)S(1)}, f32[128,512]{1,0:T(8,128)S(1)}, f32[8,64,256]{2,1,0:T(8,128)S(1)}, f32[8,64,25...) custom-call(f32[128,128]{1,0:T(8,128)} %bitcast.14, ...), custom_call_target="tpu_custom_call" | custom-call | flops 3000000000 | bytes 100000 | tf_op jit(solution)/shard_map/pallas_call | solution.py:462
  10.0 0.0 copy-start.1
  10.0 0.1 collective-permute-start.2
  10.1 0.5 %collective-permute-start.1 = (f32[2,64,256]{2,1,0:T(8,128)S(1)}, f32[2,64,256]{2,1,0:T(8,128)S(1)}, u32[]{:S(2)}, u32[]{:S(2)}) collective-permute-start(f32[2,64,256]{2,1,0:T(8,128)S(1)} %get-tuple-element.26), channel_id=1, source_target_pairs={{0,2},{2,0},{4,6},{6,4},{8,10},{10,8},{12,14},{14,12},{16,18},{18,... | collective-permute-start | bytes 393224 | tf_op jit(solution)/shard_map/ppermute | solution.py:479
  10.6 0.1 collective-permute-start.8
  10.7 0.0 copy-done
  10.7 0.0 copy-done.4
  10.7 0.5 %shard_map.133.known = f32[4,256,256]{2,1,0:T(8,128)S(1)} custom-call(f32[4,128,256]{2,1,0:T(8,128)S(1)} %bitcast.8, f32[4,8,128]{2,1,0:T(8,128)S(1)} %get-tuple-element.29.means, bf16[256,384]{1,0:T(8,128)(2,1)S(1)} %copy-done.4), custom_call_target="tpu_custom_call" | custom-call | flops 1000 | bytes 100000 | tf_op jit(solution)/shard_map/pallas_call | solution.py:462
  11.2 0.3 collective-permute-done.2.late_core
  11.5 0.5 %collective-permute-start.7 = (f32[8,64,256]{2,1,0:T(8,128)S(1)}, f32[8,64,256]{2,1,0:T(8,128)S(1)}, u32[]{:S(2)}, u32[]{:S(2)}) collective-permute-start(f32[8,64,256]{2,1,0:T(8,128)S(1)} %get-tuple-element.37), channel_id=1, source_target_pairs={{0,30},{2,4},{4,2},{6,8},{8,6},{10,12},{12,10},{14,16},{16,14},{18... | collective-permute-start | bytes 1572872 | tf_op jit(solution)/shard_map/ppermute | solution.py:475
  11.9 0.0 collective-permute-done.1.early_core
  11.9 0.0 collective-permute-done.from_chip
  11.9 0.0 copy-done.2
  11.9 0.0 copy-done.3
  12.0 0.0 copy-done.7
  12.0 0.0 copy-done.8
  12.0 0.0 copy-done.1
  12.0 3.7 %shard_map.134 = (f32[64,128]{1,0:T(8,128)S(1)}, f32[64,128]{1,0:T(8,128)S(1)}) custom-call(f32[4,64,256]{2,1,0:T(8,128)S(1)} %collective-permute-done.from_chip, f32[2,64,256]{2,1,0:T(8,128)S(1)} %collective-permute-done.1.early_core, f32[2,64,256]{2,1,0:T(8,128)S(1)} %collective-permute-done.2.late_core, f32[4,256,256]{2,1,0:T(8,128)S(1)} %shard_map.133.known, ...), custom_call_target="tpu_custom_call" | custom-call | flops 40000000000 | bytes 100000 | tf_op jit(solution)/shard_map/pallas_call | solution.py:462
  15.7 0.1 collective-permute-start.3
  15.8 1.2 %collective-permute-done.3 = f32[64,128]{1,0:T(8,128)S(1)} collective-permute-done((f32[64,128]{1,0:T(8,128)S(1)}, f32[64,128]{1,0:T(8,128)S(1)}, u32[]{:S(2)}, u32[]{:S(2)}) %collective-permute-start.3) | collective-permute-done | bytes 32800 | tf_op jit(solution)/shard_map/ppermute | solution.py:479
  17.0 1.9 %collective-permute-start.6 = (f32[64,128]{1,0:T(8,128)S(1)}, f32[64,128]{1,0:T(8,128)S(1)}, u32[]{:S(2)}, u32[]{:S(2)}) collective-permute-start(f32[64,128]{1,0:T(8,128)S(1)} %add.12), channel_id=1, source_target_pairs={{0,16},{2,18},{4,20},{6,22},{8,24},{10,26},{12,28},{14,30},{16,0},... | collective-permute-start | bytes 98312 | tf_op jit(solution)/shard_map/ppermute | solution.py:479
  18.9 1.3 %collective-permute-start.5 = (f32[64,128]{1,0:T(8,128)S(1)}, f32[64,128]{1,0:T(8,128)S(1)}, u32[]{:S(2)}, u32[]{:S(2)}) collective-permute-start(f32[64,128]{1,0:T(8,128)S(1)} %add.12), channel_id=1, source_target_pairs={{0,24},{2,26},{4,28},{6,30},{8,16},{10,18},{12,20},{14,22},{16,8},... | collective-permute-start | bytes 98312 | tf_op jit(solution)/shard_map/ppermute | solution.py:479
  20.2 0.2 collective-permute-start.4
  20.4 1.7 %collective-permute-done.6 = f32[64,128]{1,0:T(8,128)S(1)} collective-permute-done((f32[64,128]{1,0:T(8,128)S(1)}, f32[64,128]{1,0:T(8,128)S(1)}, u32[]{:S(2)}, u32[]{:S(2)}) %collective-permute-start.6) | collective-permute-done | bytes 32800 | tf_op jit(solution)/shard_map/ppermute | solution.py:479
  22.2 2.4 %collective-permute-done.5 = f32[64,128]{1,0:T(8,128)S(1)} collective-permute-done((f32[64,128]{1,0:T(8,128)S(1)}, f32[64,128]{1,0:T(8,128)S(1)}, u32[]{:S(2)}, u32[]{:S(2)}) %collective-permute-start.5) | collective-permute-done | bytes 32800 | tf_op jit(solution)/shard_map/ppermute | solution.py:479
  24.6 0.0 collective-permute-done.4
  24.6 0.0 copy-start.5
  24.6 0.0 copy-start.6
  24.6 3.0 %collective-permute-start.11 = (f32[64,128]{1,0:T(8,128)S(1)}, f32[64,128]{1,0:T(8,128)S(1)}, u32[]{:S(2)}, u32[]{:S(2)}) collective-permute-start(f32[64,128]{1,0:T(8,128)S(1)} %add_add_fusion._.mine), channel_id=1, source_target_pairs={{0,5},{1,4},{2,7},{3,6},{4,1},{5,0},{6,3},{7,2},{8,13},{9,12},{10,... | collective-permute-start | bytes 98312 | tf_op jit(solution)/shard_map/ppermute | solution.py:484
  27.6 0.5 %collective-permute-start.10 = (f32[64,128]{1,0:T(8,128)S(1)}, f32[64,128]{1,0:T(8,128)S(1)}, u32[]{:S(2)}, u32[]{:S(2)}) collective-permute-start(f32[64,128]{1,0:T(8,128)S(1)} %add_add_fusion._.mine), channel_id=1, source_target_pairs={{0,1},{1,0},{2,3},{3,2},{4,5},{5,4},{6,7},{7,6},{8,9},{9,8},{10,11... | collective-permute-start | bytes 98312 | tf_op jit(solution)/shard_map/ppermute | solution.py:585
  28.1 0.1 collective-permute-start.9
  28.2 0.0 collective-permute-done.8.far_core.refs_5_
  28.2 0.0 collective-permute-done.7.far_chip.refs_4_
  28.2 1.9 %shard_map.135 = (f32[1024,256]{1,0:T(8,128)S(1)}, f32[1024,256]{1,0:T(8,128)S(1)}) custom-call(f32[4,64,256]{2,1,0:T(8,128)S(1)} %collective-permute-done.from_chip, f32[2,64,256]{2,1,0:T(8,128)S(1)} %collective-permute-done.1.early_core, f32[2,64,256]{2,1,0:T(8,128)S(1)} %collective-permute-done.2.late_core, f32[4,128,256]{2,1,0:T(8,128)S(1)} %bitcast.9, ...), custom_call_target="tpu_custom_call" | custom-call | flops 1000000 | bytes 100000 | tf_op jit(solution)/shard_map/pallas_call | solution.py:462
  30.2 0.0 collective-permute-done.11.others_1_
  30.2 1.3 %collective-permute-done.10.others_0_ = f32[64,128]{1,0:T(8,128)S(1)} collective-permute-done((f32[64,128]{1,0:T(8,128)S(1)}, f32[64,128]{1,0:T(8,128)S(1)}, u32[]{:S(2)}, u32[]{:S(2)}) %collective-permute-start.10) | collective-permute-done | bytes 32800 | tf_op jit(solution)/shard_map/ppermute | solution.py:585
  31.5 0.5 %collective-permute-done.9.received = f32[64,128]{1,0:T(8,128)S(1)} collective-permute-done((f32[64,128]{1,0:T(8,128)S(1)}, f32[64,128]{1,0:T(8,128)S(1)}, u32[]{:S(2)}, u32[]{:S(2)}) %collective-permute-start.9) | collective-permute-done | bytes 32800 | tf_op jit(solution)/shard_map/ppermute | solution.py:479
  32.1 0.1 collective-permute-start.12
  32.1 1.2 %collective-permute-done.12.theirs = f32[72,128]{1,0:T(8,128)S(1)} collective-permute-done((f32[72,128]{1,0:T(8,128)S(1)}, f32[72,128]{1,0:T(8,128)S(1)}, u32[]{:S(2)}, u32[]{:S(2)}) %collective-permute-start.12) | collective-permute-done | bytes 36896 | tf_op jit(solution)/shard_map/ppermute | solution.py:479
  33.3 0.0 copy-done.5
  33.3 0.0 copy-done.6
  33.3 5.2 %shard_map.137 = (f32[4,128,256]{2,1,0:T(8,128)}, f32[128,128]{1,0:T(8,128)}) custom-call(f32[128,128]{1,0:T(8,128)S(1)} %bitcast.15, f32[128,128]{1,0:T(8,128)S(1)} %bitcast.17, f32[72,128]{1,0:T(8,128)S(1)} %shard_map.136.mine, f32[72,128]{1,0:T(8,128)S(1)} %collective-permute-done.12.theirs, f32[1024,256]{1,0:T(8,128)S(1)} %get-tuple-element.43.refs_0_, ...), custom_call_target="tpu_custom_call" | custom-call | flops 1000000 | bytes 100000 | tf_op jit(solution)/shard_map/pallas_call | solution.py:462
  (3 shorter events, 0.0 us)
Async XLA Ops:
  1.6 10.3 %collective-permute-start = (f32[4,64,256]{2,1,0:T(8,128)S(1)}, f32[4,64,256]{2,1,0:T(8,128)S(1)}, u32[]{:S(2)}, u32[]{:S(2)}) collective-permute-start(f32[4,64,256]{2,1,0:T(8,128)S(1)} %shard_map.131.refs_3_), channel_id=1, source_target_pairs={{0,30},{2,4},{4,2},{6,8},{8,6},{10,12},{12,10},{14,16},{16,14},{18... | collective-permute-start | bytes 786440 | tf_op jit(solution)/shard_map/ppermute | solution.py:475
  7.1 3.6 %copy-start = (f32[1,4,128,256]{3,2,1,0:T(8,128)S(1)}, f32[1,4,128,256]{3,2,1,0:T(8,128)}, u32[]{:S(2)}) copy-start(f32[1,4,128,256]{3,2,1,0:T(8,128)} %param.12) | copy-start | bytes 1572868
  7.1 3.6 %copy-start.4 = (bf16[256,384]{1,0:T(8,128)(2,1)S(1)}, bf16[256,384]{1,0:T(8,128)(2,1)}, u32[]{:S(2)}) copy-start(bf16[256,384]{1,0:T(8,128)(2,1)} %constant.23.clone.refs_0_.refs_4_) | copy-start | bytes 589828
  7.1 4.8 %copy-start.2 = (bf16[512,768]{1,0:T(8,128)(2,1)S(1)}, bf16[512,768]{1,0:T(8,128)(2,1)}, u32[]{:S(2)}) copy-start(bf16[512,768]{1,0:T(8,128)(2,1)} %constant.20.clone.refs_1_.refs_7_) | copy-start | bytes 2359300
  7.1 4.8 %copy-start.3 = (f32[1,4,128,256]{3,2,1,0:T(8,128)S(1)}, f32[1,4,128,256]{3,2,1,0:T(8,128)}, u32[]{:S(2)}) copy-start(f32[1,4,128,256]{3,2,1,0:T(8,128)} %param.13) | copy-start | bytes 1572868
  7.1 4.8 %copy-start.7 = (bf16[1536,768]{1,0:T(8,128)(2,1)S(1)}, bf16[1536,768]{1,0:T(8,128)(2,1)}, u32[]{:S(2)}) copy-start(bf16[1536,768]{1,0:T(8,128)(2,1)} %constant.21.clone.refs_2_) | copy-start | bytes 7077892
  7.1 4.8 %copy-start.8 = (bf16[656,864]{1,0:T(8,128)(2,1)S(1)}, bf16[656,864]{1,0:T(8,128)(2,1)}, u32[]{:S(2)}) copy-start(bf16[656,864]{1,0:T(8,128)(2,1)} %constant.22.clone.refs_3_) | copy-start | bytes 3400708
  10.0 2.0 %copy-start.1 = (bf16[768,1024]{1,0:T(8,128)(2,1)S(1)}, bf16[768,1024]{1,0:T(8,128)(2,1)}, u32[]{:S(2)}) copy-start(bf16[768,1024]{1,0:T(8,128)(2,1)} %constant.19.clone.refs_0_.refs_6_) | copy-start | bytes 4718596
  10.0 1.4 %collective-permute-start.2 = (f32[2,64,256]{2,1,0:T(8,128)S(1)}, f32[2,64,256]{2,1,0:T(8,128)S(1)}, u32[]{:S(2)}, u32[]{:S(2)}) collective-permute-start(f32[2,64,256]{2,1,0:T(8,128)S(1)} %get-tuple-element.28), channel_id=1, source_target_pairs={{0,2},{2,0},{4,6},{6,4},{8,10},{10,8},{12,14},{14,12},{16,18},{18,... | collective-permute-start | bytes 393224 | tf_op jit(solution)/shard_map/ppermute | solution.py:479
  10.1 1.8 %collective-permute-start.1 = (f32[2,64,256]{2,1,0:T(8,128)S(1)}, f32[2,64,256]{2,1,0:T(8,128)S(1)}, u32[]{:S(2)}, u32[]{:S(2)}) collective-permute-start(f32[2,64,256]{2,1,0:T(8,128)S(1)} %get-tuple-element.26), channel_id=1, source_target_pairs={{0,2},{2,0},{4,6},{6,4},{8,10},{10,8},{12,14},{14,12},{16,18},{18,... | collective-permute-start | bytes 393224 | tf_op jit(solution)/shard_map/ppermute | solution.py:479
  10.6 17.6 %collective-permute-start.8 = (f32[8,64,256]{2,1,0:T(8,128)S(1)}, f32[8,64,256]{2,1,0:T(8,128)S(1)}, u32[]{:S(2)}, u32[]{:S(2)}) collective-permute-start(f32[8,64,256]{2,1,0:T(8,128)S(1)} %get-tuple-element.38), channel_id=1, source_target_pairs={{0,2},{2,0},{4,6},{6,4},{8,10},{10,8},{12,14},{14,12},{16,18},{18,... | collective-permute-start | bytes 1572872 | tf_op jit(solution)/shard_map/ppermute | solution.py:479
  11.5 16.8 %collective-permute-start.7 = (f32[8,64,256]{2,1,0:T(8,128)S(1)}, f32[8,64,256]{2,1,0:T(8,128)S(1)}, u32[]{:S(2)}, u32[]{:S(2)}) collective-permute-start(f32[8,64,256]{2,1,0:T(8,128)S(1)} %get-tuple-element.37), channel_id=1, source_target_pairs={{0,30},{2,4},{4,2},{6,8},{8,6},{10,12},{12,10},{14,16},{16,14},{18... | collective-permute-start | bytes 1572872 | tf_op jit(solution)/shard_map/ppermute | solution.py:475
  15.7 1.3 %collective-permute-start.3 = (f32[64,128]{1,0:T(8,128)S(1)}, f32[64,128]{1,0:T(8,128)S(1)}, u32[]{:S(2)}, u32[]{:S(2)}) collective-permute-start(f32[64,128]{1,0:T(8,128)S(1)} %get-tuple-element.36), channel_id=1, source_target_pairs={{0,2},{2,0},{4,6},{6,4},{8,10},{10,8},{12,14},{14,12},{16,18},{18,... | collective-permute-start | bytes 98312 | tf_op jit(solution)/shard_map/ppermute | solution.py:479
  17.0 5.2 %collective-permute-start.6 = (f32[64,128]{1,0:T(8,128)S(1)}, f32[64,128]{1,0:T(8,128)S(1)}, u32[]{:S(2)}, u32[]{:S(2)}) collective-permute-start(f32[64,128]{1,0:T(8,128)S(1)} %add.12), channel_id=1, source_target_pairs={{0,16},{2,18},{4,20},{6,22},{8,24},{10,26},{12,28},{14,30},{16,0},... | collective-permute-start | bytes 98312 | tf_op jit(solution)/shard_map/ppermute | solution.py:479
  18.9 5.7 %collective-permute-start.5 = (f32[64,128]{1,0:T(8,128)S(1)}, f32[64,128]{1,0:T(8,128)S(1)}, u32[]{:S(2)}, u32[]{:S(2)}) collective-permute-start(f32[64,128]{1,0:T(8,128)S(1)} %add.12), channel_id=1, source_target_pairs={{0,24},{2,26},{4,28},{6,30},{8,16},{10,18},{12,20},{14,22},{16,8},... | collective-permute-start | bytes 98312 | tf_op jit(solution)/shard_map/ppermute | solution.py:479
  20.2 4.4 %collective-permute-start.4 = (f32[64,128]{1,0:T(8,128)S(1)}, f32[64,128]{1,0:T(8,128)S(1)}, u32[]{:S(2)}, u32[]{:S(2)}) collective-permute-start(f32[64,128]{1,0:T(8,128)S(1)} %add.12), channel_id=1, source_target_pairs={{0,8},{2,10},{4,12},{6,14},{8,0},{10,2},{12,4},{14,6},{16,24},{18,... | collective-permute-start | bytes 98312 | tf_op jit(solution)/shard_map/ppermute | solution.py:479
  24.6 8.7 %copy-start.5 = (f32[1,128,128]{2,1,0:T(8,128)S(1)}, f32[1,128,128]{2,1,0:T(8,128)}, u32[]{:S(2)}) copy-start(f32[1,128,128]{2,1,0:T(8,128)} %param.14) | copy-start | bytes 196612
  24.6 8.7 %copy-start.6 = (f32[1,128,128]{2,1,0:T(8,128)S(1)}, f32[1,128,128]{2,1,0:T(8,128)}, u32[]{:S(2)}) copy-start(f32[1,128,128]{2,1,0:T(8,128)} %param.15) | copy-start | bytes 196612
  24.6 5.5 %collective-permute-start.11 = (f32[64,128]{1,0:T(8,128)S(1)}, f32[64,128]{1,0:T(8,128)S(1)}, u32[]{:S(2)}, u32[]{:S(2)}) collective-permute-start(f32[64,128]{1,0:T(8,128)S(1)} %add_add_fusion._.mine), channel_id=1, source_target_pairs={{0,5},{1,4},{2,7},{3,6},{4,1},{5,0},{6,3},{7,2},{8,13},{9,12},{10,... | collective-permute-start | bytes 98312 | tf_op jit(solution)/shard_map/ppermute | solution.py:484
  27.6 3.9 %collective-permute-start.10 = (f32[64,128]{1,0:T(8,128)S(1)}, f32[64,128]{1,0:T(8,128)S(1)}, u32[]{:S(2)}, u32[]{:S(2)}) collective-permute-start(f32[64,128]{1,0:T(8,128)S(1)} %add_add_fusion._.mine), channel_id=1, source_target_pairs={{0,1},{1,0},{2,3},{3,2},{4,5},{5,4},{6,7},{7,6},{8,9},{9,8},{10,11... | collective-permute-start | bytes 98312 | tf_op jit(solution)/shard_map/ppermute | solution.py:585
  28.1 3.9 %collective-permute-start.9 = (f32[64,128]{1,0:T(8,128)S(1)}, f32[64,128]{1,0:T(8,128)S(1)}, u32[]{:S(2)}, u32[]{:S(2)}) collective-permute-start(f32[64,128]{1,0:T(8,128)S(1)} %add_add_fusion._.mine), channel_id=1, source_target_pairs={{0,4},{2,6},{4,0},{6,2},{8,12},{10,14},{12,8},{14,10},{16,20},{18,... | collective-permute-start | bytes 98312 | tf_op jit(solution)/shard_map/ppermute | solution.py:479
  32.1 1.3 %collective-permute-start.12 = (f32[72,128]{1,0:T(8,128)S(1)}, f32[72,128]{1,0:T(8,128)S(1)}, u32[]{:S(2)}, u32[]{:S(2)}) collective-permute-start(f32[72,128]{1,0:T(8,128)S(1)} %shard_map.136.mine), channel_id=1, source_target_pairs={{0,2},{2,0},{4,6},{6,4},{8,10},{10,8},{12,14},{14,12},{16,18},{18,... | collective-permute-start | bytes 110600 | tf_op jit(solution)/shard_map/ppermute | solution.py:479

commit v4 on v3

--- a/solution.py
+++ b/solution.py
@@ -562,7 +562,7 @@
         (picture, means, *own_arrays),
         flops=10**3,
     )
-    far_chip, late_core, known = lax.optimization_barrier((far_chip, late_core, known))
+    far_chip, known = lax.optimization_barrier((far_chip, known))
     far_chip = to_next_chip(far_chip)
     keep, give = call(
         functools.partial(gradient_kernel, at=gradient_at),
@@ -576,7 +576,7 @@
     half = keep + exchange(give, 1)
     bits = list(range(2, count.bit_length() - 1))
     for low, high in zip(bits[::2], bits[1::2]):
-        half = half + ((exchange(half, 1 << low) + exchange(half, (1 << low) | (1 << high))) + exchange(half, 1 << high))
+        half = half + ((exchange(half, 1 << low) + exchange(half, 1 << high)) + exchange(half, (1 << low) | (1 << high)))
     if len(bits) % 2:
         half = half + exchange(half, 1 << bits[-1])
     last_round = [exchange(half, 2)]

time: 38.8 us -> 38.4 us (0.990)
  waiting for transfers between devices: 8.65 us -> 7.16 us
  starting transfers between devices: 13.9 us -> 15 us
    ppermute x9, starting transfers between devices: 4.4 us -> 5.75 us  [exchange(): lax.ppermute(value, 'tile', [(i, i ^ step) for i in range(lax.axis_size('...]
    ppermute x9, waiting for transfers between devices: 7.32 us -> 6.27 us  [exchange(): lax.ppermute(value, 'tile', [(i, i ^ step) for i in range(lax.axis_size('...]
    ppermute x1, starting transfers between devices: 2.96 us -> 2.47 us  [across_depth_and_chip(): return lax.ppermute(value, ('tile', 'depth'), pairs)]
    ppermute x1, waiting for transfers between devices: 1.33 us -> 0.89 us  [on_device(): lax.ppermute(half, 'depth', [(0, 1), (1, 0)])]
  transfers between devices with their start and end apart: 13 -> 13, of which waited for: 7 -> 6; matrix products, arithmetic and copies ran while one was open for 0% -> 0% of each run, Pallas kernels for 23% -> 23%
where the time goes in v4:
time: 38.4 us; the launch traced here: 38.2 us
  Pallas kernels  15.2 us (40%)
  starting transfers between devices  15 us (39%)
  waiting for transfers between devices  7.16 us (19%)
  between operations  0.79 us (2%)
    pallas_call x7, Pallas kernels, call(): pl.pallas_call(kernel, out_shape=outs, in_specs=[pl.BlockSpec(memory_spac...  15.2 us
    ppermute x9, waiting for transfers between devices, exchange(): lax.ppermute(value, 'tile', [(i, i ^ step) for i in range(lax.axis_size('...  6.27 us
    ppermute x2, starting transfers between devices, to_next_chip(): lax.ppermute(value, 'tile', [(i, (i + 1 if i % 2 else i - 1) % count) for...  6.23 us
    ppermute x9, starting transfers between devices, exchange(): lax.ppermute(value, 'tile', [(i, i ^ step) for i in range(lax.axis_size('...  5.75 us
    ppermute x1, starting transfers between devices, across_depth_and_chip(): return lax.ppermute(value, ('tile', 'depth'), pairs)  2.47 us
    ppermute x1, waiting for transfers between devices, on_device(): lax.ppermute(half, 'depth', [(0, 1), (1, 0)])  0.89 us
  transfers between devices with their start and end apart: 13, of which 6 were waited for; matrix products, arithmetic and copies ran while one was open for 0% of the time, Pallas kernels for 23%

profile of v4, /device:TPU:0, one launch (start us, length us, event | category | flops | bytes accessed | tf_op | source)
XLA Modules:
  0.0 38.2 jit_solution(17720127903373775801)
XLA Ops:
  0.6 1.0 %shard_map.131.refs_3_ = f32[4,64,256]{2,1,0:T(8,128)S(1)} custom-call(f32[4,128,256]{2,1,0:T(8,128)} %bitcast.6), custom_call_target="tpu_custom_call" | custom-call | flops 1000000 | bytes 100000 | tf_op jit(solution)/shard_map/pallas_call | solution.py:462
  1.6 5.5 %collective-permute-start = (f32[4,64,256]{2,1,0:T(8,128)S(1)}, f32[4,64,256]{2,1,0:T(8,128)S(1)}, u32[]{:S(2)}, u32[]{:S(2)}) collective-permute-start(f32[4,64,256]{2,1,0:T(8,128)S(1)} %shard_map.131.refs_3_), channel_id=1, source_target_pairs={{0,30},{2,4},{4,2},{6,8},{8,6},{10,12},{12,10},{14,16},{16,14},{18... | collective-permute-start | bytes 786440 | tf_op jit(solution)/shard_map/ppermute | solution.py:475
  7.1 0.0 copy-start
  7.1 0.0 copy-start.4
  7.1 0.0 copy-start.2
  7.1 0.0 copy-start.3
  7.1 0.0 copy-start.7
  7.1 0.0 copy-start.8
  7.2 2.9 %shard_map.132 = (f32[128,256]{1,0:T(8,128)S(1)}, f32[288,256]{1,0:T(8,128)S(1)}, f32[128,512]{1,0:T(8,128)S(1)}, f32[8,64,256]{2,1,0:T(8,128)S(1)}, f32[8,64,25...) custom-call(f32[128,128]{1,0:T(8,128)} %bitcast.14, ...), custom_call_target="tpu_custom_call" | custom-call | flops 3000000000 | bytes 100000 | tf_op jit(solution)/shard_map/pallas_call | solution.py:462
  10.0 0.0 copy-start.1
  10.0 0.1 collective-permute-start.1
  10.1 0.5 %collective-permute-start.2 = (f32[2,64,256]{2,1,0:T(8,128)S(1)}, f32[2,64,256]{2,1,0:T(8,128)S(1)}, u32[]{:S(2)}, u32[]{:S(2)}) collective-permute-start(f32[2,64,256]{2,1,0:T(8,128)S(1)} %get-tuple-element.26), channel_id=1, source_target_pairs={{0,2},{2,0},{4,6},{6,4},{8,10},{10,8},{12,14},{14,12},{16,18},{18,... | collective-permute-start | bytes 393224 | tf_op jit(solution)/shard_map/ppermute | solution.py:479
  10.6 0.1 collective-permute-start.8
  10.7 0.0 copy-done
  10.7 0.0 copy-done.4
  10.7 0.5 %shard_map.133.known = f32[4,256,256]{2,1,0:T(8,128)S(1)} custom-call(f32[4,128,256]{2,1,0:T(8,128)S(1)} %bitcast.8, f32[4,8,128]{2,1,0:T(8,128)S(1)} %get-tuple-element.28.means, bf16[256,384]{1,0:T(8,128)(2,1)S(1)} %copy-done.4), custom_call_target="tpu_custom_call" | custom-call | flops 1000 | bytes 100000 | tf_op jit(solution)/shard_map/pallas_call | solution.py:462
  11.2 0.7 %collective-permute-start.7 = (f32[8,64,256]{2,1,0:T(8,128)S(1)}, f32[8,64,256]{2,1,0:T(8,128)S(1)}, u32[]{:S(2)}, u32[]{:S(2)}) collective-permute-start(f32[8,64,256]{2,1,0:T(8,128)S(1)} %get-tuple-element.35), channel_id=1, source_target_pairs={{0,30},{2,4},{4,2},{6,8},{8,6},{10,12},{12,10},{14,16},{16,14},{18... | collective-permute-start | bytes 1572872 | tf_op jit(solution)/shard_map/ppermute | solution.py:475
  11.9 0.0 collective-permute-done.1.early_core
  11.9 0.0 collective-permute-done.2.late_core
  11.9 0.0 collective-permute-done.from_chip
  11.9 0.0 copy-done.2
  11.9 0.0 copy-done.3
  12.0 0.0 copy-done.7
  12.0 0.0 copy-done.8
  12.0 0.0 copy-done.1
  12.0 3.7 %shard_map.134 = (f32[64,128]{1,0:T(8,128)S(1)}, f32[64,128]{1,0:T(8,128)S(1)}) custom-call(f32[4,64,256]{2,1,0:T(8,128)S(1)} %collective-permute-done.from_chip, f32[2,64,256]{2,1,0:T(8,128)S(1)} %collective-permute-done.1.early_core, f32[2,64,256]{2,1,0:T(8,128)S(1)} %collective-permute-done.2.late_core, f32[4,256,256]{2,1,0:T(8,128)S(1)} %shard_map.133.known, ...), custom_call_target="tpu_custom_call" | custom-call | flops 40000000000 | bytes 100000 | tf_op jit(solution)/shard_map/pallas_call | solution.py:462
  15.7 0.1 collective-permute-start.3
  15.8 1.2 %collective-permute-done.3 = f32[64,128]{1,0:T(8,128)S(1)} collective-permute-done((f32[64,128]{1,0:T(8,128)S(1)}, f32[64,128]{1,0:T(8,128)S(1)}, u32[]{:S(2)}, u32[]{:S(2)}) %collective-permute-start.3) | collective-permute-done | bytes 32800 | tf_op jit(solution)/shard_map/ppermute | solution.py:479
  17.0 2.9 %collective-permute-start.6 = (f32[64,128]{1,0:T(8,128)S(1)}, f32[64,128]{1,0:T(8,128)S(1)}, u32[]{:S(2)}, u32[]{:S(2)}) collective-permute-start(f32[64,128]{1,0:T(8,128)S(1)} %add.12), channel_id=1, source_target_pairs={{0,24},{2,26},{4,28},{6,30},{8,16},{10,18},{12,20},{14,22},{16,8},... | collective-permute-start | bytes 98312 | tf_op jit(solution)/shard_map/ppermute | solution.py:479
  19.9 0.0 collective-permute-start.5
  19.9 1.5 %collective-permute-start.4 = (f32[64,128]{1,0:T(8,128)S(1)}, f32[64,128]{1,0:T(8,128)S(1)}, u32[]{:S(2)}, u32[]{:S(2)}) collective-permute-start(f32[64,128]{1,0:T(8,128)S(1)} %add.12), channel_id=1, source_target_pairs={{0,8},{2,10},{4,12},{6,14},{8,0},{10,2},{12,4},{14,6},{16,24},{18,... | collective-permute-start | bytes 98312 | tf_op jit(solution)/shard_map/ppermute | solution.py:479
  21.3 1.6 %collective-permute-done.6 = f32[64,128]{1,0:T(8,128)S(1)} collective-permute-done((f32[64,128]{1,0:T(8,128)S(1)}, f32[64,128]{1,0:T(8,128)S(1)}, u32[]{:S(2)}, u32[]{:S(2)}) %collective-permute-start.6) | collective-permute-done | bytes 32800 | tf_op jit(solution)/shard_map/ppermute | solution.py:479
  22.9 1.8 %collective-permute-done.5 = f32[64,128]{1,0:T(8,128)S(1)} collective-permute-done((f32[64,128]{1,0:T(8,128)S(1)}, f32[64,128]{1,0:T(8,128)S(1)}, u32[]{:S(2)}, u32[]{:S(2)}) %collective-permute-start.5) | collective-permute-done | bytes 32800 | tf_op jit(solution)/shard_map/ppermute | solution.py:479
  24.7 0.0 collective-permute-done.4
  24.7 0.0 copy-start.5
  24.7 0.0 copy-start.6
  24.7 2.5 %collective-permute-start.11 = (f32[64,128]{1,0:T(8,128)S(1)}, f32[64,128]{1,0:T(8,128)S(1)}, u32[]{:S(2)}, u32[]{:S(2)}) collective-permute-start(f32[64,128]{1,0:T(8,128)S(1)} %add_add_fusion._.mine), channel_id=1, source_target_pairs={{0,5},{1,4},{2,7},{3,6},{4,1},{5,0},{6,3},{7,2},{8,13},{9,12},{10,... | collective-permute-start | bytes 98312 | tf_op jit(solution)/shard_map/ppermute | solution.py:484
  27.2 0.5 %collective-permute-start.10 = (f32[64,128]{1,0:T(8,128)S(1)}, f32[64,128]{1,0:T(8,128)S(1)}, u32[]{:S(2)}, u32[]{:S(2)}) collective-permute-start(f32[64,128]{1,0:T(8,128)S(1)} %add_add_fusion._.mine), channel_id=1, source_target_pairs={{0,1},{1,0},{2,3},{3,2},{4,5},{5,4},{6,7},{7,6},{8,9},{9,8},{10,11... | collective-permute-start | bytes 98312 | tf_op jit(solution)/shard_map/ppermute | solution.py:585
  27.7 0.6 %collective-permute-start.9 = (f32[64,128]{1,0:T(8,128)S(1)}, f32[64,128]{1,0:T(8,128)S(1)}, u32[]{:S(2)}, u32[]{:S(2)}) collective-permute-start(f32[64,128]{1,0:T(8,128)S(1)} %add_add_fusion._.mine), channel_id=1, source_target_pairs={{0,4},{2,6},{4,0},{6,2},{8,12},{10,14},{12,8},{14,10},{16,20},{18,... | collective-permute-start | bytes 98312 | tf_op jit(solution)/shard_map/ppermute | solution.py:479
  28.3 0.0 collective-permute-done.8.far_core.refs_5_
  28.3 0.0 collective-permute-done.7.far_chip.refs_4_
  28.3 1.9 %shard_map.135 = (f32[1024,256]{1,0:T(8,128)S(1)}, f32[1024,256]{1,0:T(8,128)S(1)}) custom-call(f32[4,64,256]{2,1,0:T(8,128)S(1)} %collective-permute-done.from_chip, f32[2,64,256]{2,1,0:T(8,128)S(1)} %collective-permute-done.1.early_core, f32[2,64,256]{2,1,0:T(8,128)S(1)} %collective-permute-done.2.late_core, f32[4,128,256]{2,1,0:T(8,128)S(1)} %bitcast.9, ...), custom_call_target="tpu_custom_call" | custom-call | flops 1000000 | bytes 100000 | tf_op jit(solution)/shard_map/pallas_call | solution.py:462
  30.2 0.0 collective-permute-done.11.others_1_
  30.2 0.9 %collective-permute-done.10.others_0_ = f32[64,128]{1,0:T(8,128)S(1)} collective-permute-done((f32[64,128]{1,0:T(8,128)S(1)}, f32[64,128]{1,0:T(8,128)S(1)}, u32[]{:S(2)}, u32[]{:S(2)}) %collective-permute-start.10) | collective-permute-done | bytes 32800 | tf_op jit(solution)/shard_map/ppermute | solution.py:585
  31.1 0.5 %collective-permute-done.9.received = f32[64,128]{1,0:T(8,128)S(1)} collective-permute-done((f32[64,128]{1,0:T(8,128)S(1)}, f32[64,128]{1,0:T(8,128)S(1)}, u32[]{:S(2)}, u32[]{:S(2)}) %collective-permute-start.9) | collective-permute-done | bytes 32800 | tf_op jit(solution)/shard_map/ppermute | solution.py:479
  31.7 0.1 collective-permute-start.12
  31.8 1.2 %collective-permute-done.12.theirs = f32[72,128]{1,0:T(8,128)S(1)} collective-permute-done((f32[72,128]{1,0:T(8,128)S(1)}, f32[72,128]{1,0:T(8,128)S(1)}, u32[]{:S(2)}, u32[]{:S(2)}) %collective-permute-start.12) | collective-permute-done | bytes 36896 | tf_op jit(solution)/shard_map/ppermute | solution.py:479
  33.0 0.0 copy-done.5
  33.0 0.0 copy-done.6
  33.0 5.2 %shard_map.137 = (f32[4,128,256]{2,1,0:T(8,128)}, f32[128,128]{1,0:T(8,128)}) custom-call(f32[128,128]{1,0:T(8,128)S(1)} %bitcast.15, f32[128,128]{1,0:T(8,128)S(1)} %bitcast.17, f32[72,128]{1,0:T(8,128)S(1)} %shard_map.136.mine, f32[72,128]{1,0:T(8,128)S(1)} %collective-permute-done.12.theirs, f32[1024,256]{1,0:T(8,128)S(1)} %get-tuple-element.41.refs_0_, ...), custom_call_target="tpu_custom_call" | custom-call | flops 1000000 | bytes 100000 | tf_op jit(solution)/shard_map/pallas_call | solution.py:462
  (3 shorter events, 0.0 us)
Async XLA Ops:
  1.6 10.3 %collective-permute-start = (f32[4,64,256]{2,1,0:T(8,128)S(1)}, f32[4,64,256]{2,1,0:T(8,128)S(1)}, u32[]{:S(2)}, u32[]{:S(2)}) collective-permute-start(f32[4,64,256]{2,1,0:T(8,128)S(1)} %shard_map.131.refs_3_), channel_id=1, source_target_pairs={{0,30},{2,4},{4,2},{6,8},{8,6},{10,12},{12,10},{14,16},{16,14},{18... | collective-permute-start | bytes 786440 | tf_op jit(solution)/shard_map/ppermute | solution.py:475
  7.1 3.6 %copy-start = (f32[1,4,128,256]{3,2,1,0:T(8,128)S(1)}, f32[1,4,128,256]{3,2,1,0:T(8,128)}, u32[]{:S(2)}) copy-start(f32[1,4,128,256]{3,2,1,0:T(8,128)} %param.12) | copy-start | bytes 1572868
  7.1 3.6 %copy-start.4 = (bf16[256,384]{1,0:T(8,128)(2,1)S(1)}, bf16[256,384]{1,0:T(8,128)(2,1)}, u32[]{:S(2)}) copy-start(bf16[256,384]{1,0:T(8,128)(2,1)} %constant.23.clone.refs_0_.refs_4_) | copy-start | bytes 589828
  7.1 4.8 %copy-start.2 = (bf16[512,768]{1,0:T(8,128)(2,1)S(1)}, bf16[512,768]{1,0:T(8,128)(2,1)}, u32[]{:S(2)}) copy-start(bf16[512,768]{1,0:T(8,128)(2,1)} %constant.20.clone.refs_1_.refs_7_) | copy-start | bytes 2359300
  7.1 4.8 %copy-start.3 = (f32[1,4,128,256]{3,2,1,0:T(8,128)S(1)}, f32[1,4,128,256]{3,2,1,0:T(8,128)}, u32[]{:S(2)}) copy-start(f32[1,4,128,256]{3,2,1,0:T(8,128)} %param.13) | copy-start | bytes 1572868
  7.1 4.8 %copy-start.7 = (bf16[1536,768]{1,0:T(8,128)(2,1)S(1)}, bf16[1536,768]{1,0:T(8,128)(2,1)}, u32[]{:S(2)}) copy-start(bf16[1536,768]{1,0:T(8,128)(2,1)} %constant.21.clone.refs_2_) | copy-start | bytes 7077892
  7.1 4.8 %copy-start.8 = (bf16[656,864]{1,0:T(8,128)(2,1)S(1)}, bf16[656,864]{1,0:T(8,128)(2,1)}, u32[]{:S(2)}) copy-start(bf16[656,864]{1,0:T(8,128)(2,1)} %constant.22.clone.refs_3_) | copy-start | bytes 3400708
  10.0 2.0 %copy-start.1 = (bf16[768,1024]{1,0:T(8,128)(2,1)S(1)}, bf16[768,1024]{1,0:T(8,128)(2,1)}, u32[]{:S(2)}) copy-start(bf16[768,1024]{1,0:T(8,128)(2,1)} %constant.19.clone.refs_0_.refs_6_) | copy-start | bytes 4718596
  10.0 1.9 %collective-permute-start.1 = (f32[2,64,256]{2,1,0:T(8,128)S(1)}, f32[2,64,256]{2,1,0:T(8,128)S(1)}, u32[]{:S(2)}, u32[]{:S(2)}) collective-permute-start(f32[2,64,256]{2,1,0:T(8,128)S(1)} %get-tuple-element.25), channel_id=1, source_target_pairs={{0,2},{2,0},{4,6},{6,4},{8,10},{10,8},{12,14},{14,12},{16,18},{18,... | collective-permute-start | bytes 393224 | tf_op jit(solution)/shard_map/ppermute | solution.py:479
  10.1 1.8 %collective-permute-start.2 = (f32[2,64,256]{2,1,0:T(8,128)S(1)}, f32[2,64,256]{2,1,0:T(8,128)S(1)}, u32[]{:S(2)}, u32[]{:S(2)}) collective-permute-start(f32[2,64,256]{2,1,0:T(8,128)S(1)} %get-tuple-element.26), channel_id=1, source_target_pairs={{0,2},{2,0},{4,6},{6,4},{8,10},{10,8},{12,14},{14,12},{16,18},{18,... | collective-permute-start | bytes 393224 | tf_op jit(solution)/shard_map/ppermute | solution.py:479
  10.6 17.7 %collective-permute-start.8 = (f32[8,64,256]{2,1,0:T(8,128)S(1)}, f32[8,64,256]{2,1,0:T(8,128)S(1)}, u32[]{:S(2)}, u32[]{:S(2)}) collective-permute-start(f32[8,64,256]{2,1,0:T(8,128)S(1)} %get-tuple-element.36), channel_id=1, source_target_pairs={{0,2},{2,0},{4,6},{6,4},{8,10},{10,8},{12,14},{14,12},{16,18},{18,... | collective-permute-start | bytes 1572872 | tf_op jit(solution)/shard_map/ppermute | solution.py:479
  11.2 17.1 %collective-permute-start.7 = (f32[8,64,256]{2,1,0:T(8,128)S(1)}, f32[8,64,256]{2,1,0:T(8,128)S(1)}, u32[]{:S(2)}, u32[]{:S(2)}) collective-permute-start(f32[8,64,256]{2,1,0:T(8,128)S(1)} %get-tuple-element.35), channel_id=1, source_target_pairs={{0,30},{2,4},{4,2},{6,8},{8,6},{10,12},{12,10},{14,16},{16,14},{18... | collective-permute-start | bytes 1572872 | tf_op jit(solution)/shard_map/ppermute | solution.py:475
  15.7 1.3 %collective-permute-start.3 = (f32[64,128]{1,0:T(8,128)S(1)}, f32[64,128]{1,0:T(8,128)S(1)}, u32[]{:S(2)}, u32[]{:S(2)}) collective-permute-start(f32[64,128]{1,0:T(8,128)S(1)} %get-tuple-element.34), channel_id=1, source_target_pairs={{0,2},{2,0},{4,6},{6,4},{8,10},{10,8},{12,14},{14,12},{16,18},{18,... | collective-permute-start | bytes 98312 | tf_op jit(solution)/shard_map/ppermute | solution.py:479
  17.0 6.0 %collective-permute-start.6 = (f32[64,128]{1,0:T(8,128)S(1)}, f32[64,128]{1,0:T(8,128)S(1)}, u32[]{:S(2)}, u32[]{:S(2)}) collective-permute-start(f32[64,128]{1,0:T(8,128)S(1)} %add.12), channel_id=1, source_target_pairs={{0,24},{2,26},{4,28},{6,30},{8,16},{10,18},{12,20},{14,22},{16,8},... | collective-permute-start | bytes 98312 | tf_op jit(solution)/shard_map/ppermute | solution.py:479
  19.9 4.8 %collective-permute-start.5 = (f32[64,128]{1,0:T(8,128)S(1)}, f32[64,128]{1,0:T(8,128)S(1)}, u32[]{:S(2)}, u32[]{:S(2)}) collective-permute-start(f32[64,128]{1,0:T(8,128)S(1)} %add.12), channel_id=1, source_target_pairs={{0,16},{2,18},{4,20},{6,22},{8,24},{10,26},{12,28},{14,30},{16,0},... | collective-permute-start | bytes 98312 | tf_op jit(solution)/shard_map/ppermute | solution.py:479
  19.9 4.8 %collective-permute-start.4 = (f32[64,128]{1,0:T(8,128)S(1)}, f32[64,128]{1,0:T(8,128)S(1)}, u32[]{:S(2)}, u32[]{:S(2)}) collective-permute-start(f32[64,128]{1,0:T(8,128)S(1)} %add.12), channel_id=1, source_target_pairs={{0,8},{2,10},{4,12},{6,14},{8,0},{10,2},{12,4},{14,6},{16,24},{18,... | collective-permute-start | bytes 98312 | tf_op jit(solution)/shard_map/ppermute | solution.py:479
  24.7 8.2 %copy-start.5 = (f32[1,128,128]{2,1,0:T(8,128)S(1)}, f32[1,128,128]{2,1,0:T(8,128)}, u32[]{:S(2)}) copy-start(f32[1,128,128]{2,1,0:T(8,128)} %param.14) | copy-start | bytes 196612
  24.7 8.2 %copy-start.6 = (f32[1,128,128]{2,1,0:T(8,128)S(1)}, f32[1,128,128]{2,1,0:T(8,128)}, u32[]{:S(2)}) copy-start(f32[1,128,128]{2,1,0:T(8,128)} %param.15) | copy-start | bytes 196612
  24.7 5.5 %collective-permute-start.11 = (f32[64,128]{1,0:T(8,128)S(1)}, f32[64,128]{1,0:T(8,128)S(1)}, u32[]{:S(2)}, u32[]{:S(2)}) collective-permute-start(f32[64,128]{1,0:T(8,128)S(1)} %add_add_fusion._.mine), channel_id=1, source_target_pairs={{0,5},{1,4},{2,7},{3,6},{4,1},{5,0},{6,3},{7,2},{8,13},{9,12},{10,... | collective-permute-start | bytes 98312 | tf_op jit(solution)/shard_map/ppermute | solution.py:484
  27.2 3.9 %collective-permute-start.10 = (f32[64,128]{1,0:T(8,128)S(1)}, f32[64,128]{1,0:T(8,128)S(1)}, u32[]{:S(2)}, u32[]{:S(2)}) collective-permute-start(f32[64,128]{1,0:T(8,128)S(1)} %add_add_fusion._.mine), channel_id=1, source_target_pairs={{0,1},{1,0},{2,3},{3,2},{4,5},{5,4},{6,7},{7,6},{8,9},{9,8},{10,11... | collective-permute-start | bytes 98312 | tf_op jit(solution)/shard_map/ppermute | solution.py:585
  27.7 3.9 %collective-permute-start.9 = (f32[64,128]{1,0:T(8,128)S(1)}, f32[64,128]{1,0:T(8,128)S(1)}, u32[]{:S(2)}, u32[]{:S(2)}) collective-permute-start(f32[64,128]{1,0:T(8,128)S(1)} %add_add_fusion._.mine), channel_id=1, source_target_pairs={{0,4},{2,6},{4,0},{6,2},{8,12},{10,14},{12,8},{14,10},{16,20},{18,... | collective-permute-start | bytes 98312 | tf_op jit(solution)/shard_map/ppermute | solution.py:479
  31.7 1.3 %collective-permute-start.12 = (f32[72,128]{1,0:T(8,128)S(1)}, f32[72,128]{1,0:T(8,128)S(1)}, u32[]{:S(2)}, u32[]{:S(2)}) collective-permute-start(f32[72,128]{1,0:T(8,128)S(1)} %shard_map.136.mine), channel_id=1, source_target_pairs={{0,2},{2,0},{4,6},{6,4},{8,10},{10,8},{12,14},{14,12},{16,18},{18,... | collective-permute-start | bytes 110600 | tf_op jit(solution)/shard_map/ppermute | solution.py:479

commit v5 on v4

--- a/solution.py
+++ b/solution.py
@@ -210,8 +210,10 @@
         half, freqs = strip.shape[1] // 2, strip.shape[0] // 2
         sums.append(jnp.concatenate([strip[:freqs, :half], strip[freqs:, :half]], 1))
         differences.append(jnp.concatenate([strip[:freqs, half:], strip[freqs:, half:]], 1))
-    even = [right_by(jnp.concatenate(sums[p : p + 2], 0), const["forward_even"]) for p in range(0, len(sums), 2)]
-    odd = [right_by(jnp.concatenate(differences[p : p + 2], 0), const["forward_odd"]) for p in range(0, len(sums), 2)]
+    even, odd = [], []
+    for p in range(0, len(sums), 2):
+        even.append(right_by(jnp.concatenate(sums[p : p + 2], 0), const["forward_even"]))
+        odd.append(right_by(jnp.concatenate(differences[p : p + 2], 0), const["forward_odd"]))
     return even, odd
 
 
@@ -220,10 +222,12 @@
 
 
 def inverse(even, odd, freqs, const):
-    even = [right_by(spectrum, const["inverse_even"]) for spectrum in even]
-    odd = [right_by(spectrum, const["inverse_odd"]) for spectrum in odd]
+    pairs = [
+        (right_by(sums, const["inverse_even"]), right_by(differences, const["inverse_odd"]))
+        for sums, differences in zip(even, odd)
+    ]
     strips = []
-    for sums, differences in zip(even, odd):
+    for sums, differences in pairs:
         half = sums.shape[1] // 2
         for top in range(0, sums.shape[0], freqs):
             rows = slice(top, top + freqs)

time: 38.4 us -> 38.3 us (level)
  no operation moved by 1% of the time
where the time goes in v5:
time: 38.3 us; the launch traced here: 38.1 us
  Pallas kernels  15.1 us (39%)
  starting transfers between devices  15 us (39%)
  waiting for transfers between devices  7.17 us (19%)
  between operations  0.79 us (2%)
    pallas_call x7, Pallas kernels, call(): pl.pallas_call(kernel, out_shape=outs, in_specs=[pl.BlockSpec(memory_spac...  15.1 us
    ppermute x9, waiting for transfers between devices, exchange(): lax.ppermute(value, 'tile', [(i, i ^ step) for i in range(lax.axis_size('...  6.27 us
    ppermute x2, starting transfers between devices, to_next_chip(): lax.ppermute(value, 'tile', [(i, (i + 1 if i % 2 else i - 1) % count) for...  6.23 us
    ppermute x9, starting transfers between devices, exchange(): lax.ppermute(value, 'tile', [(i, i ^ step) for i in range(lax.axis_size('...  5.75 us
    ppermute x1, starting transfers between devices, across_depth_and_chip(): return lax.ppermute(value, ('tile', 'depth'), pairs)  2.47 us
    ppermute x1, waiting for transfers between devices, on_device(): lax.ppermute(half, 'depth', [(0, 1), (1, 0)])  0.89 us
  transfers between devices with their start and end apart: 13, of which 6 were waited for; matrix products, arithmetic and copies ran while one was open for 0% of the time, Pallas kernels for 23%

profile of v5, /device:TPU:0, one launch (start us, length us, event | category | flops | bytes accessed | tf_op | source)
XLA Modules:
  0.0 38.1 jit_solution(6669919412694710552)
XLA Ops:
  0.6 1.0 %shard_map.131.refs_3_ = f32[4,64,256]{2,1,0:T(8,128)S(1)} custom-call(f32[4,128,256]{2,1,0:T(8,128)} %bitcast.6), custom_call_target="tpu_custom_call" | custom-call | flops 1000000 | bytes 100000 | tf_op jit(solution)/shard_map/pallas_call | solution.py:466
  1.6 5.5 %collective-permute-start = (f32[4,64,256]{2,1,0:T(8,128)S(1)}, f32[4,64,256]{2,1,0:T(8,128)S(1)}, u32[]{:S(2)}, u32[]{:S(2)}) collective-permute-start(f32[4,64,256]{2,1,0:T(8,128)S(1)} %shard_map.131.refs_3_), channel_id=1, source_target_pairs={{0,30},{2,4},{4,2},{6,8},{8,6},{10,12},{12,10},{14,16},{16,14},{18... | collective-permute-start | bytes 786440 | tf_op jit(solution)/shard_map/ppermute | solution.py:479
  7.1 0.0 copy-start
  7.1 0.0 copy-start.4
  7.1 0.0 copy-start.2
  7.1 0.0 copy-start.3
  7.1 0.0 copy-start.7
  7.1 0.0 copy-start.8
  7.2 2.9 %shard_map.132 = (f32[128,256]{1,0:T(8,128)S(1)}, f32[288,256]{1,0:T(8,128)S(1)}, f32[128,512]{1,0:T(8,128)S(1)}, f32[8,64,256]{2,1,0:T(8,128)S(1)}, f32[8,64,25...) custom-call(f32[128,128]{1,0:T(8,128)} %bitcast.14, ...), custom_call_target="tpu_custom_call" | custom-call | flops 3000000000 | bytes 100000 | tf_op jit(solution)/shard_map/pallas_call | solution.py:466
  10.0 0.0 copy-start.1
  10.0 0.1 collective-permute-start.1
  10.1 0.5 %collective-permute-start.2 = (f32[2,64,256]{2,1,0:T(8,128)S(1)}, f32[2,64,256]{2,1,0:T(8,128)S(1)}, u32[]{:S(2)}, u32[]{:S(2)}) collective-permute-start(f32[2,64,256]{2,1,0:T(8,128)S(1)} %get-tuple-element.26), channel_id=1, source_target_pairs={{0,2},{2,0},{4,6},{6,4},{8,10},{10,8},{12,14},{14,12},{16,18},{18,... | collective-permute-start | bytes 393224 | tf_op jit(solution)/shard_map/ppermute | solution.py:483
  10.6 0.1 collective-permute-start.8
  10.7 0.0 copy-done
  10.7 0.0 copy-done.4
  10.7 0.5 %shard_map.133.known = f32[4,256,256]{2,1,0:T(8,128)S(1)} custom-call(f32[4,128,256]{2,1,0:T(8,128)S(1)} %bitcast.8, f32[4,8,128]{2,1,0:T(8,128)S(1)} %get-tuple-element.28.means, bf16[256,384]{1,0:T(8,128)(2,1)S(1)} %copy-done.4), custom_call_target="tpu_custom_call" | custom-call | flops 1000 | bytes 100000 | tf_op jit(solution)/shard_map/pallas_call | solution.py:466
  11.2 0.7 %collective-permute-start.7 = (f32[8,64,256]{2,1,0:T(8,128)S(1)}, f32[8,64,256]{2,1,0:T(8,128)S(1)}, u32[]{:S(2)}, u32[]{:S(2)}) collective-permute-start(f32[8,64,256]{2,1,0:T(8,128)S(1)} %get-tuple-element.35), channel_id=1, source_target_pairs={{0,30},{2,4},{4,2},{6,8},{8,6},{10,12},{12,10},{14,16},{16,14},{18... | collective-permute-start | bytes 1572872 | tf_op jit(solution)/shard_map/ppermute | solution.py:479
  11.9 0.0 collective-permute-done.1.early_core
  11.9 0.0 collective-permute-done.2.late_core
  11.9 0.0 collective-permute-done.from_chip
  11.9 0.0 copy-done.2
  11.9 0.0 copy-done.3
  12.0 0.0 copy-done.7
  12.0 0.0 copy-done.8
  12.0 0.0 copy-done.1
  12.0 3.6 %shard_map.134 = (f32[64,128]{1,0:T(8,128)S(1)}, f32[64,128]{1,0:T(8,128)S(1)}) custom-call(f32[4,64,256]{2,1,0:T(8,128)S(1)} %collective-permute-done.from_chip, f32[2,64,256]{2,1,0:T(8,128)S(1)} %collective-permute-done.1.early_core, f32[2,64,256]{2,1,0:T(8,128)S(1)} %collective-permute-done.2.late_core, f32[4,256,256]{2,1,0:T(8,128)S(1)} %shard_map.133.known, ...), custom_call_target="tpu_custom_call" | custom-call | flops 40000000000 | bytes 100000 | tf_op jit(solution)/shard_map/pallas_call | solution.py:466
  15.6 0.1 collective-permute-start.3
  15.7 1.2 %collective-permute-done.3 = f32[64,128]{1,0:T(8,128)S(1)} collective-permute-done((f32[64,128]{1,0:T(8,128)S(1)}, f32[64,128]{1,0:T(8,128)S(1)}, u32[]{:S(2)}, u32[]{:S(2)}) %collective-permute-start.3) | collective-permute-done | bytes 32800 | tf_op jit(solution)/shard_map/ppermute | solution.py:483
  16.9 2.9 %collective-permute-start.6 = (f32[64,128]{1,0:T(8,128)S(1)}, f32[64,128]{1,0:T(8,128)S(1)}, u32[]{:S(2)}, u32[]{:S(2)}) collective-permute-start(f32[64,128]{1,0:T(8,128)S(1)} %add.12), channel_id=1, source_target_pairs={{0,24},{2,26},{4,28},{6,30},{8,16},{10,18},{12,20},{14,22},{16,8},... | collective-permute-start | bytes 98312 | tf_op jit(solution)/shard_map/ppermute | solution.py:483
  19.8 0.0 collective-permute-start.5
  19.8 1.5 %collective-permute-start.4 = (f32[64,128]{1,0:T(8,128)S(1)}, f32[64,128]{1,0:T(8,128)S(1)}, u32[]{:S(2)}, u32[]{:S(2)}) collective-permute-start(f32[64,128]{1,0:T(8,128)S(1)} %add.12), channel_id=1, source_target_pairs={{0,8},{2,10},{4,12},{6,14},{8,0},{10,2},{12,4},{14,6},{16,24},{18,... | collective-permute-start | bytes 98312 | tf_op jit(solution)/shard_map/ppermute | solution.py:483
  21.3 1.6 %collective-permute-done.6 = f32[64,128]{1,0:T(8,128)S(1)} collective-permute-done((f32[64,128]{1,0:T(8,128)S(1)}, f32[64,128]{1,0:T(8,128)S(1)}, u32[]{:S(2)}, u32[]{:S(2)}) %collective-permute-start.6) | collective-permute-done | bytes 32800 | tf_op jit(solution)/shard_map/ppermute | solution.py:483
  22.8 1.8 %collective-permute-done.5 = f32[64,128]{1,0:T(8,128)S(1)} collective-permute-done((f32[64,128]{1,0:T(8,128)S(1)}, f32[64,128]{1,0:T(8,128)S(1)}, u32[]{:S(2)}, u32[]{:S(2)}) %collective-permute-start.5) | collective-permute-done | bytes 32800 | tf_op jit(solution)/shard_map/ppermute | solution.py:483
  24.6 0.0 collective-permute-done.4
  24.6 0.0 copy-start.5
  24.6 0.0 copy-start.6
  24.6 2.5 %collective-permute-start.11 = (f32[64,128]{1,0:T(8,128)S(1)}, f32[64,128]{1,0:T(8,128)S(1)}, u32[]{:S(2)}, u32[]{:S(2)}) collective-permute-start(f32[64,128]{1,0:T(8,128)S(1)} %add_add_fusion._.mine), channel_id=1, source_target_pairs={{0,5},{1,4},{2,7},{3,6},{4,1},{5,0},{6,3},{7,2},{8,13},{9,12},{10,... | collective-permute-start | bytes 98312 | tf_op jit(solution)/shard_map/ppermute | solution.py:488
  27.1 0.5 %collective-permute-start.10 = (f32[64,128]{1,0:T(8,128)S(1)}, f32[64,128]{1,0:T(8,128)S(1)}, u32[]{:S(2)}, u32[]{:S(2)}) collective-permute-start(f32[64,128]{1,0:T(8,128)S(1)} %add_add_fusion._.mine), channel_id=1, source_target_pairs={{0,1},{1,0},{2,3},{3,2},{4,5},{5,4},{6,7},{7,6},{8,9},{9,8},{10,11... | collective-permute-start | bytes 98312 | tf_op jit(solution)/shard_map/ppermute | solution.py:589
  27.7 0.6 %collective-permute-start.9 = (f32[64,128]{1,0:T(8,128)S(1)}, f32[64,128]{1,0:T(8,128)S(1)}, u32[]{:S(2)}, u32[]{:S(2)}) collective-permute-start(f32[64,128]{1,0:T(8,128)S(1)} %add_add_fusion._.mine), channel_id=1, source_target_pairs={{0,4},{2,6},{4,0},{6,2},{8,12},{10,14},{12,8},{14,10},{16,20},{18,... | collective-permute-start | bytes 98312 | tf_op jit(solution)/shard_map/ppermute | solution.py:483
  28.2 0.0 collective-permute-done.8.far_core.refs_5_
  28.2 0.0 collective-permute-done.7.far_chip.refs_4_
  28.2 1.9 %shard_map.135 = (f32[1024,256]{1,0:T(8,128)S(1)}, f32[1024,256]{1,0:T(8,128)S(1)}) custom-call(f32[4,64,256]{2,1,0:T(8,128)S(1)} %collective-permute-done.from_chip, f32[2,64,256]{2,1,0:T(8,128)S(1)} %collective-permute-done.1.early_core, f32[2,64,256]{2,1,0:T(8,128)S(1)} %collective-permute-done.2.late_core, f32[4,128,256]{2,1,0:T(8,128)S(1)} %bitcast.9, ...), custom_call_target="tpu_custom_call" | custom-call | flops 1000000 | bytes 100000 | tf_op jit(solution)/shard_map/pallas_call | solution.py:466
  30.1 0.0 collective-permute-done.11.others_1_
  30.1 0.9 %collective-permute-done.10.others_0_ = f32[64,128]{1,0:T(8,128)S(1)} collective-permute-done((f32[64,128]{1,0:T(8,128)S(1)}, f32[64,128]{1,0:T(8,128)S(1)}, u32[]{:S(2)}, u32[]{:S(2)}) %collective-permute-start.10) | collective-permute-done | bytes 32800 | tf_op jit(solution)/shard_map/ppermute | solution.py:589
  31.0 0.5 %collective-permute-done.9.received = f32[64,128]{1,0:T(8,128)S(1)} collective-permute-done((f32[64,128]{1,0:T(8,128)S(1)}, f32[64,128]{1,0:T(8,128)S(1)}, u32[]{:S(2)}, u32[]{:S(2)}) %collective-permute-start.9) | collective-permute-done | bytes 32800 | tf_op jit(solution)/shard_map/ppermute | solution.py:483
  31.6 0.1 collective-permute-start.12
  31.7 1.2 %collective-permute-done.12.theirs = f32[72,128]{1,0:T(8,128)S(1)} collective-permute-done((f32[72,128]{1,0:T(8,128)S(1)}, f32[72,128]{1,0:T(8,128)S(1)}, u32[]{:S(2)}, u32[]{:S(2)}) %collective-permute-start.12) | collective-permute-done | bytes 36896 | tf_op jit(solution)/shard_map/ppermute | solution.py:483
  32.9 0.0 copy-done.5
  32.9 0.0 copy-done.6
  32.9 5.2 %shard_map.137 = (f32[4,128,256]{2,1,0:T(8,128)}, f32[128,128]{1,0:T(8,128)}) custom-call(f32[128,128]{1,0:T(8,128)S(1)} %bitcast.15, f32[128,128]{1,0:T(8,128)S(1)} %bitcast.17, f32[72,128]{1,0:T(8,128)S(1)} %shard_map.136.mine, f32[72,128]{1,0:T(8,128)S(1)} %collective-permute-done.12.theirs, f32[1024,256]{1,0:T(8,128)S(1)} %get-tuple-element.41.refs_0_, ...), custom_call_target="tpu_custom_call" | custom-call | flops 1000000 | bytes 100000 | tf_op jit(solution)/shard_map/pallas_call | solution.py:466
  (3 shorter events, 0.0 us)
Async XLA Ops:
  1.6 10.3 %collective-permute-start = (f32[4,64,256]{2,1,0:T(8,128)S(1)}, f32[4,64,256]{2,1,0:T(8,128)S(1)}, u32[]{:S(2)}, u32[]{:S(2)}) collective-permute-start(f32[4,64,256]{2,1,0:T(8,128)S(1)} %shard_map.131.refs_3_), channel_id=1, source_target_pairs={{0,30},{2,4},{4,2},{6,8},{8,6},{10,12},{12,10},{14,16},{16,14},{18... | collective-permute-start | bytes 786440 | tf_op jit(solution)/shard_map/ppermute | solution.py:479
  7.1 3.6 %copy-start = (f32[1,4,128,256]{3,2,1,0:T(8,128)S(1)}, f32[1,4,128,256]{3,2,1,0:T(8,128)}, u32[]{:S(2)}) copy-start(f32[1,4,128,256]{3,2,1,0:T(8,128)} %param.12) | copy-start | bytes 1572868
  7.1 3.6 %copy-start.4 = (bf16[256,384]{1,0:T(8,128)(2,1)S(1)}, bf16[256,384]{1,0:T(8,128)(2,1)}, u32[]{:S(2)}) copy-start(bf16[256,384]{1,0:T(8,128)(2,1)} %constant.23.clone.refs_0_.refs_4_) | copy-start | bytes 589828
  7.1 4.8 %copy-start.2 = (bf16[512,768]{1,0:T(8,128)(2,1)S(1)}, bf16[512,768]{1,0:T(8,128)(2,1)}, u32[]{:S(2)}) copy-start(bf16[512,768]{1,0:T(8,128)(2,1)} %constant.20.clone.refs_1_.refs_7_) | copy-start | bytes 2359300
  7.1 4.8 %copy-start.3 = (f32[1,4,128,256]{3,2,1,0:T(8,128)S(1)}, f32[1,4,128,256]{3,2,1,0:T(8,128)}, u32[]{:S(2)}) copy-start(f32[1,4,128,256]{3,2,1,0:T(8,128)} %param.13) | copy-start | bytes 1572868
  7.1 4.8 %copy-start.7 = (bf16[1536,768]{1,0:T(8,128)(2,1)S(1)}, bf16[1536,768]{1,0:T(8,128)(2,1)}, u32[]{:S(2)}) copy-start(bf16[1536,768]{1,0:T(8,128)(2,1)} %constant.21.clone.refs_2_) | copy-start | bytes 7077892
  7.1 4.8 %copy-start.8 = (bf16[656,864]{1,0:T(8,128)(2,1)S(1)}, bf16[656,864]{1,0:T(8,128)(2,1)}, u32[]{:S(2)}) copy-start(bf16[656,864]{1,0:T(8,128)(2,1)} %constant.22.clone.refs_3_) | copy-start | bytes 3400708
  10.0 2.0 %copy-start.1 = (bf16[768,1024]{1,0:T(8,128)(2,1)S(1)}, bf16[768,1024]{1,0:T(8,128)(2,1)}, u32[]{:S(2)}) copy-start(bf16[768,1024]{1,0:T(8,128)(2,1)} %constant.19.clone.refs_0_.refs_6_) | copy-start | bytes 4718596
  10.0 1.9 %collective-permute-start.1 = (f32[2,64,256]{2,1,0:T(8,128)S(1)}, f32[2,64,256]{2,1,0:T(8,128)S(1)}, u32[]{:S(2)}, u32[]{:S(2)}) collective-permute-start(f32[2,64,256]{2,1,0:T(8,128)S(1)} %get-tuple-element.25), channel_id=1, source_target_pairs={{0,2},{2,0},{4,6},{6,4},{8,10},{10,8},{12,14},{14,12},{16,18},{18,... | collective-permute-start | bytes 393224 | tf_op jit(solution)/shard_map/ppermute | solution.py:483
  10.1 1.8 %collective-permute-start.2 = (f32[2,64,256]{2,1,0:T(8,128)S(1)}, f32[2,64,256]{2,1,0:T(8,128)S(1)}, u32[]{:S(2)}, u32[]{:S(2)}) collective-permute-start(f32[2,64,256]{2,1,0:T(8,128)S(1)} %get-tuple-element.26), channel_id=1, source_target_pairs={{0,2},{2,0},{4,6},{6,4},{8,10},{10,8},{12,14},{14,12},{16,18},{18,... | collective-permute-start | bytes 393224 | tf_op jit(solution)/shard_map/ppermute | solution.py:483
  10.6 17.6 %collective-permute-start.8 = (f32[8,64,256]{2,1,0:T(8,128)S(1)}, f32[8,64,256]{2,1,0:T(8,128)S(1)}, u32[]{:S(2)}, u32[]{:S(2)}) collective-permute-start(f32[8,64,256]{2,1,0:T(8,128)S(1)} %get-tuple-element.36), channel_id=1, source_target_pairs={{0,2},{2,0},{4,6},{6,4},{8,10},{10,8},{12,14},{14,12},{16,18},{18,... | collective-permute-start | bytes 1572872 | tf_op jit(solution)/shard_map/ppermute | solution.py:483
  11.2 17.0 %collective-permute-start.7 = (f32[8,64,256]{2,1,0:T(8,128)S(1)}, f32[8,64,256]{2,1,0:T(8,128)S(1)}, u32[]{:S(2)}, u32[]{:S(2)}) collective-permute-start(f32[8,64,256]{2,1,0:T(8,128)S(1)} %get-tuple-element.35), channel_id=1, source_target_pairs={{0,30},{2,4},{4,2},{6,8},{8,6},{10,12},{12,10},{14,16},{16,14},{18... | collective-permute-start | bytes 1572872 | tf_op jit(solution)/shard_map/ppermute | solution.py:479
  15.6 1.3 %collective-permute-start.3 = (f32[64,128]{1,0:T(8,128)S(1)}, f32[64,128]{1,0:T(8,128)S(1)}, u32[]{:S(2)}, u32[]{:S(2)}) collective-permute-start(f32[64,128]{1,0:T(8,128)S(1)} %get-tuple-element.34), channel_id=1, source_target_pairs={{0,2},{2,0},{4,6},{6,4},{8,10},{10,8},{12,14},{14,12},{16,18},{18,... | collective-permute-start | bytes 98312 | tf_op jit(solution)/shard_map/ppermute | solution.py:483
  16.9 6.0 %collective-permute-start.6 = (f32[64,128]{1,0:T(8,128)S(1)}, f32[64,128]{1,0:T(8,128)S(1)}, u32[]{:S(2)}, u32[]{:S(2)}) collective-permute-start(f32[64,128]{1,0:T(8,128)S(1)} %add.12), channel_id=1, source_target_pairs={{0,24},{2,26},{4,28},{6,30},{8,16},{10,18},{12,20},{14,22},{16,8},... | collective-permute-start | bytes 98312 | tf_op jit(solution)/shard_map/ppermute | solution.py:483
  19.8 4.8 %collective-permute-start.5 = (f32[64,128]{1,0:T(8,128)S(1)}, f32[64,128]{1,0:T(8,128)S(1)}, u32[]{:S(2)}, u32[]{:S(2)}) collective-permute-start(f32[64,128]{1,0:T(8,128)S(1)} %add.12), channel_id=1, source_target_pairs={{0,16},{2,18},{4,20},{6,22},{8,24},{10,26},{12,28},{14,30},{16,0},... | collective-permute-start | bytes 98312 | tf_op jit(solution)/shard_map/ppermute | solution.py:483
  19.8 4.8 %collective-permute-start.4 = (f32[64,128]{1,0:T(8,128)S(1)}, f32[64,128]{1,0:T(8,128)S(1)}, u32[]{:S(2)}, u32[]{:S(2)}) collective-permute-start(f32[64,128]{1,0:T(8,128)S(1)} %add.12), channel_id=1, source_target_pairs={{0,8},{2,10},{4,12},{6,14},{8,0},{10,2},{12,4},{14,6},{16,24},{18,... | collective-permute-start | bytes 98312 | tf_op jit(solution)/shard_map/ppermute | solution.py:483
  24.6 8.2 %copy-start.5 = (f32[1,128,128]{2,1,0:T(8,128)S(1)}, f32[1,128,128]{2,1,0:T(8,128)}, u32[]{:S(2)}) copy-start(f32[1,128,128]{2,1,0:T(8,128)} %param.14) | copy-start | bytes 196612
  24.6 8.2 %copy-start.6 = (f32[1,128,128]{2,1,0:T(8,128)S(1)}, f32[1,128,128]{2,1,0:T(8,128)}, u32[]{:S(2)}) copy-start(f32[1,128,128]{2,1,0:T(8,128)} %param.15) | copy-start | bytes 196612
  24.6 5.5 %collective-permute-start.11 = (f32[64,128]{1,0:T(8,128)S(1)}, f32[64,128]{1,0:T(8,128)S(1)}, u32[]{:S(2)}, u32[]{:S(2)}) collective-permute-start(f32[64,128]{1,0:T(8,128)S(1)} %add_add_fusion._.mine), channel_id=1, source_target_pairs={{0,5},{1,4},{2,7},{3,6},{4,1},{5,0},{6,3},{7,2},{8,13},{9,12},{10,... | collective-permute-start | bytes 98312 | tf_op jit(solution)/shard_map/ppermute | solution.py:488
  27.1 3.9 %collective-permute-start.10 = (f32[64,128]{1,0:T(8,128)S(1)}, f32[64,128]{1,0:T(8,128)S(1)}, u32[]{:S(2)}, u32[]{:S(2)}) collective-permute-start(f32[64,128]{1,0:T(8,128)S(1)} %add_add_fusion._.mine), channel_id=1, source_target_pairs={{0,1},{1,0},{2,3},{3,2},{4,5},{5,4},{6,7},{7,6},{8,9},{9,8},{10,11... | collective-permute-start | bytes 98312 | tf_op jit(solution)/shard_map/ppermute | solution.py:589
  27.7 3.9 %collective-permute-start.9 = (f32[64,128]{1,0:T(8,128)S(1)}, f32[64,128]{1,0:T(8,128)S(1)}, u32[]{:S(2)}, u32[]{:S(2)}) collective-permute-start(f32[64,128]{1,0:T(8,128)S(1)} %add_add_fusion._.mine), channel_id=1, source_target_pairs={{0,4},{2,6},{4,0},{6,2},{8,12},{10,14},{12,8},{14,10},{16,20},{18,... | collective-permute-start | bytes 98312 | tf_op jit(solution)/shard_map/ppermute | solution.py:483
  31.6 1.3 %collective-permute-start.12 = (f32[72,128]{1,0:T(8,128)S(1)}, f32[72,128]{1,0:T(8,128)S(1)}, u32[]{:S(2)}, u32[]{:S(2)}) collective-permute-start(f32[72,128]{1,0:T(8,128)S(1)} %shard_map.136.mine), channel_id=1, source_target_pairs={{0,2},{2,0},{4,6},{6,4},{8,10},{10,8},{12,14},{14,12},{16,18},{18,... | collective-permute-start | bytes 110600 | tf_op jit(solution)/shard_map/ppermute | solution.py:483

commit v6 on v4

--- a/solution.py
+++ b/solution.py
@@ -287,10 +287,10 @@
 def first_kernel(
     phase, amplitude, own, observed, *refs, at, places, arrays,
 ):
-    psf_refs, outs = refs[:arrays], refs[arrays + 1 : arrays + 9]
-    pupil_out, field_out, spec_out, chip_out, core_out, early_out, late_out, means_out = outs
-    psf_outs, (phase_in, amplitude_in, own_in, sems) = refs[arrays + 9 : -4], refs[-4:]
-    planes, rows, cols = own.shape
+    psf_refs, outs = refs[:arrays], refs[arrays + 1 : arrays + 8]
+    pupil_out, field_out, spec_out, chip_out, core_out, early_out, late_out = outs
+    psf_outs, (phase_in, amplitude_in, sems) = refs[arrays + 8 : -3], refs[-3:]
+    planes, rows, _ = own.shape
     early = early_out.shape[0]
     objects_chip, objects_core = edge_rows(HALF, rows - 2 * HALF)
     observed_chip, observed_core = edge_rows(0, rows - HALF)
@@ -304,7 +304,6 @@
         (observed.at[:, pl.ds(observed_chip, HALF), :], chip_out.at[planes:]),
         (own.at[:, pl.ds(objects_core, HALF), :], core_out.at[:planes]),
         (observed.at[:, pl.ds(observed_core, HALF), :], core_out.at[planes:]),
-        (own, own_in),
     ]
     copies = [pltpu.make_async_copy(source, target, sems.at[i]) for i, (source, target) in enumerate(pairs)]
     for i in (0, 1, *(2 + places[name][0] for name in NEEDED_IN_ORDER), *range(2 + arrays, len(copies))):
@@ -322,8 +321,6 @@
     spec_out[...] = spectrum
     for copy in copies[2 + arrays :]:
         copy.wait()
-    for p in range(planes):
-        means_out[p] = jnp.broadcast_to(total(own_in[p]) * (1.0 / (rows * cols)), means_out.shape[1:])
 
 
 def halo_rows(chip, core):
@@ -331,10 +328,13 @@
     return jnp.where(even, chip, core), jnp.where(even, core, chip)
 
 
-def known_kernel(own, means, *refs, at):
-    const, known_out = at(*refs[:-1]), refs[-1]
-    for p in range(own.shape[0]):
-        known_out[p] = left_by(const["row_own"], mixed_halves(own[p], means[p][:1, :1]))
+def known_kernel(own, *refs, at):
+    const, (known_out, means_out) = at(*refs[:-2]), refs[-2:]
+    planes, rows, cols = own.shape
+    for p in range(planes):
+        mean = total(own[p]) * (1.0 / (rows * cols))
+        known_out[p] = left_by(const["row_own"], mixed_halves(own[p], mean))
+        means_out[p] = jnp.broadcast_to(mean, means_out.shape[1:])
 
 
 def gradient_kernel(
@@ -543,23 +543,23 @@
         near_kernel, [(planes, HALF, cols)], in_hbm[2:3], scratch=[pltpu.SemaphoreType.DMA(())], spaces={0: pltpu.HBM}
     )
     from_chip = to_next_chip(chip_rows)
-    pupil, field, spec, far_chip, far_core, early_rows, late_rows, means, *psf_arrays = call(
+    pupil, field, spec, far_chip, far_core, early_rows, late_rows, *psf_arrays = call(
         functools.partial(first_kernel, at=psf_const.at, places=psf_const.places, arrays=len(psf_arrays)),
         [(pup, 2 * pup), (2 * pad_rows, pad_cols), (length // 2, 2 * cols)]
         + [(2 * planes, HALF, cols)] * 2
-        + [(planes // 2, HALF, cols), (planes - planes // 2, HALF, cols), (planes, 8, 128)]
+        + [(planes // 2, HALF, cols), (planes - planes // 2, HALF, cols)]
         + psf_arrays,
         (*in_hbm, chip_rows),
         flops=3 * 10**9,
         spaces={**dict.fromkeys(range(len(in_hbm)), pltpu.HBM), len(in_hbm): pl.ANY},
-        scratch=[pltpu.VMEM(value.shape, jnp.float32) for value in (phase, amplitude, picture)]
-        + [pltpu.SemaphoreType.DMA((9 + len(psf_arrays),))],
+        scratch=[pltpu.VMEM(value.shape, jnp.float32) for value in (phase, amplitude)]
+        + [pltpu.SemaphoreType.DMA((8 + len(psf_arrays),))],
     )
     early_core, late_core, far_core = (exchange(value, 1) for value in (early_rows, late_rows, far_core))
-    (known,) = call(
+    known, means = call(
         functools.partial(known_kernel, at=own_const.at),
-        [(planes, length, cols)],
-        (picture, means, *own_arrays),
+        [(planes, length, cols), (planes, 8, 128)],
+        (picture, *own_arrays),
         flops=10**3,
     )
     far_chip, known = lax.optimization_barrier((far_chip, known))

time: 38.4 us -> 38.5 us (level)
  transfers between devices with their start and end apart: 13 -> 13, of which waited for: 6 -> 7; matrix products, arithmetic and copies ran while one was open for 0% -> 0% of each run, Pallas kernels for 23% -> 23%
where the time goes in v6:
time: 38.5 us; the launch traced here: 38.4 us
  Pallas kernels  15.1 us (39%)
  starting transfers between devices  14.9 us (39%)
  waiting for transfers between devices  7.5 us (19%)
  between operations  0.77 us (2%)
    pallas_call x7, Pallas kernels, call(): pl.pallas_call(kernel, out_shape=outs, in_specs=[pl.BlockSpec(memory_spac...  15.1 us
    ppermute x9, waiting for transfers between devices, exchange(): lax.ppermute(value, 'tile', [(i, i ^ step) for i in range(lax.axis_size('...  6.42 us
    ppermute x2, starting transfers between devices, to_next_chip(): lax.ppermute(value, 'tile', [(i, (i + 1 if i % 2 else i - 1) % count) for...  5.87 us
    ppermute x9, starting transfers between devices, exchange(): lax.ppermute(value, 'tile', [(i, i ^ step) for i in range(lax.axis_size('...  5.84 us
    ppermute x1, starting transfers between devices, across_depth_and_chip(): return lax.ppermute(value, ('tile', 'depth'), pairs)  2.66 us
    ppermute x1, waiting for transfers between devices, on_device(): lax.ppermute(half, 'depth', [(0, 1), (1, 0)])  1.07 us
  transfers between devices with their start and end apart: 13, of which 7 were waited for; matrix products, arithmetic and copies ran while one was open for 0% of the time, Pallas kernels for 23%

profile of v6, /device:TPU:0, one launch (start us, length us, event | category | flops | bytes accessed | tf_op | source)
XLA Modules:
  0.0 38.4 jit_solution(6557455052141186265)
XLA Ops:
  0.6 1.0 %shard_map.131.refs_3_ = f32[4,64,256]{2,1,0:T(8,128)S(1)} custom-call(f32[4,128,256]{2,1,0:T(8,128)} %bitcast.6), custom_call_target="tpu_custom_call" | custom-call | flops 1000000 | bytes 100000 | tf_op jit(solution)/shard_map/pallas_call | solution.py:462
  1.6 5.5 %collective-permute-start = (f32[4,64,256]{2,1,0:T(8,128)S(1)}, f32[4,64,256]{2,1,0:T(8,128)S(1)}, u32[]{:S(2)}, u32[]{:S(2)}) collective-permute-start(f32[4,64,256]{2,1,0:T(8,128)S(1)} %shard_map.131.refs_3_), channel_id=1, source_target_pairs={{0,30},{2,4},{4,2},{6,8},{8,6},{10,12},{12,10},{14,16},{16,14},{18... | collective-permute-start | bytes 786440 | tf_op jit(solution)/shard_map/ppermute | solution.py:475
  7.1 0.0 copy-start
  7.1 0.0 copy-start.4
  7.1 0.0 copy-start.1
  7.1 0.0 copy-start.2
  7.1 0.0 copy-start.3
  7.1 0.0 copy-start.7
  7.2 0.0 copy-start.8
  7.2 2.7 %shard_map.132 = (f32[128,256]{1,0:T(8,128)S(1)}, f32[288,256]{1,0:T(8,128)S(1)}, f32[128,512]{1,0:T(8,128)S(1)}, f32[8,64,256]{2,1,0:T(8,128)S(1)}, f32[8,64,25...) custom-call(f32[128,128]{1,0:T(8,128)} %bitcast.14, ...), custom_call_target="tpu_custom_call" | custom-call | flops 3000000000 | bytes 100000 | tf_op jit(solution)/shard_map/pallas_call | solution.py:462
  9.9 0.1 collective-permute-start.1
  10.0 0.5 %collective-permute-start.2 = (f32[2,64,256]{2,1,0:T(8,128)S(1)}, f32[2,64,256]{2,1,0:T(8,128)S(1)}, u32[]{:S(2)}, u32[]{:S(2)}) collective-permute-start(f32[2,64,256]{2,1,0:T(8,128)S(1)} %get-tuple-element.27), channel_id=1, source_target_pairs={{0,2},{2,0},{4,6},{6,4},{8,10},{10,8},{12,14},{14,12},{16,18},{18,... | collective-permute-start | bytes 393224 | tf_op jit(solution)/shard_map/ppermute | solution.py:479
  10.5 0.0 copy-done
  10.5 0.0 copy-done.4
  10.5 0.5 %shard_map.133 = (f32[4,256,256]{2,1,0:T(8,128)S(1)}, f32[4,8,128]{2,1,0:T(8,128)S(1)}) custom-call(f32[4,128,256]{2,1,0:T(8,128)S(1)} %bitcast.8, bf16[256,384]{1,0:T(8,128)(2,1)S(1)} %copy-done.4), custom_call_target="tpu_custom_call" | custom-call | flops 1000 | bytes 100000 | tf_op jit(solution)/shard_map/pallas_call | solution.py:462
  11.0 0.4 collective-permute-start.7
  11.4 0.0 collective-permute-start.8
  11.4 0.0 collective-permute-done.1.early_core
  11.4 0.1 collective-permute-done.2.late_core
  11.5 0.0 collective-permute-done.from_chip
  11.5 0.0 copy-done.1
  11.5 0.0 copy-done.2
  11.5 0.0 copy-done.3
  11.5 0.0 copy-done.7
  11.6 0.0 copy-done.8
  11.6 3.7 %shard_map.134 = (f32[64,128]{1,0:T(8,128)S(1)}, f32[64,128]{1,0:T(8,128)S(1)}) custom-call(f32[4,64,256]{2,1,0:T(8,128)S(1)} %collective-permute-done.from_chip, f32[2,64,256]{2,1,0:T(8,128)S(1)} %collective-permute-done.1.early_core, f32[2,64,256]{2,1,0:T(8,128)S(1)} %collective-permute-done.2.late_core, f32[4,256,256]{2,1,0:T(8,128)S(1)} %get-tuple-element.30.known, ...), custom_call_target="tpu_custom_call" | custom-call | flops 40000000000 | bytes 100000 | tf_op jit(solution)/shard_map/pallas_call | solution.py:462
  15.3 0.5 %collective-permute-start.3 = (f32[64,128]{1,0:T(8,128)S(1)}, f32[64,128]{1,0:T(8,128)S(1)}, u32[]{:S(2)}, u32[]{:S(2)}) collective-permute-start(f32[64,128]{1,0:T(8,128)S(1)} %get-tuple-element.36), channel_id=1, source_target_pairs={{0,2},{2,0},{4,6},{6,4},{8,10},{10,8},{12,14},{14,12},{16,18},{18,... | collective-permute-start | bytes 98312 | tf_op jit(solution)/shard_map/ppermute | solution.py:479
  15.7 0.9 %collective-permute-done.3 = f32[64,128]{1,0:T(8,128)S(1)} collective-permute-done((f32[64,128]{1,0:T(8,128)S(1)}, f32[64,128]{1,0:T(8,128)S(1)}, u32[]{:S(2)}, u32[]{:S(2)}) %collective-permute-start.3) | collective-permute-done | bytes 32800 | tf_op jit(solution)/shard_map/ppermute | solution.py:479
  16.6 3.3 %collective-permute-start.6 = (f32[64,128]{1,0:T(8,128)S(1)}, f32[64,128]{1,0:T(8,128)S(1)}, u32[]{:S(2)}, u32[]{:S(2)}) collective-permute-start(f32[64,128]{1,0:T(8,128)S(1)} %add.12), channel_id=1, source_target_pairs={{0,24},{2,26},{4,28},{6,30},{8,16},{10,18},{12,20},{14,22},{16,8},... | collective-permute-start | bytes 98312 | tf_op jit(solution)/shard_map/ppermute | solution.py:479
  19.9 0.0 collective-permute-start.5
  19.9 1.1 %collective-permute-start.4 = (f32[64,128]{1,0:T(8,128)S(1)}, f32[64,128]{1,0:T(8,128)S(1)}, u32[]{:S(2)}, u32[]{:S(2)}) collective-permute-start(f32[64,128]{1,0:T(8,128)S(1)} %add.12), channel_id=1, source_target_pairs={{0,8},{2,10},{4,12},{6,14},{8,0},{10,2},{12,4},{14,6},{16,24},{18,... | collective-permute-start | bytes 98312 | tf_op jit(solution)/shard_map/ppermute | solution.py:479
  21.0 1.3 %collective-permute-done.6 = f32[64,128]{1,0:T(8,128)S(1)} collective-permute-done((f32[64,128]{1,0:T(8,128)S(1)}, f32[64,128]{1,0:T(8,128)S(1)}, u32[]{:S(2)}, u32[]{:S(2)}) %collective-permute-start.6) | collective-permute-done | bytes 32800 | tf_op jit(solution)/shard_map/ppermute | solution.py:479
  22.3 2.4 %collective-permute-done.5 = f32[64,128]{1,0:T(8,128)S(1)} collective-permute-done((f32[64,128]{1,0:T(8,128)S(1)}, f32[64,128]{1,0:T(8,128)S(1)}, u32[]{:S(2)}, u32[]{:S(2)}) %collective-permute-start.5) | collective-permute-done | bytes 32800 | tf_op jit(solution)/shard_map/ppermute | solution.py:479
  24.7 0.0 collective-permute-done.4
  24.7 0.0 copy-start.5
  24.7 0.0 copy-start.6
  24.7 2.7 %collective-permute-start.11 = (f32[64,128]{1,0:T(8,128)S(1)}, f32[64,128]{1,0:T(8,128)S(1)}, u32[]{:S(2)}, u32[]{:S(2)}) collective-permute-start(f32[64,128]{1,0:T(8,128)S(1)} %add_add_fusion._.mine), channel_id=1, source_target_pairs={{0,5},{1,4},{2,7},{3,6},{4,1},{5,0},{6,3},{7,2},{8,13},{9,12},{10,... | collective-permute-start | bytes 98312 | tf_op jit(solution)/shard_map/ppermute | solution.py:484
  27.4 0.5 %collective-permute-start.10 = (f32[64,128]{1,0:T(8,128)S(1)}, f32[64,128]{1,0:T(8,128)S(1)}, u32[]{:S(2)}, u32[]{:S(2)}) collective-permute-start(f32[64,128]{1,0:T(8,128)S(1)} %add_add_fusion._.mine), channel_id=1, source_target_pairs={{0,1},{1,0},{2,3},{3,2},{4,5},{5,4},{6,7},{7,6},{8,9},{9,8},{10,11... | collective-permute-start | bytes 98312 | tf_op jit(solution)/shard_map/ppermute | solution.py:585
  27.9 0.4 collective-permute-start.9
  28.3 0.0 collective-permute-done.7.far_chip.refs_4_
  28.3 0.0 collective-permute-done.8.far_core.refs_5_
  28.3 1.9 %shard_map.135 = (f32[1024,256]{1,0:T(8,128)S(1)}, f32[1024,256]{1,0:T(8,128)S(1)}) custom-call(f32[4,64,256]{2,1,0:T(8,128)S(1)} %collective-permute-done.from_chip, f32[2,64,256]{2,1,0:T(8,128)S(1)} %collective-permute-done.1.early_core, f32[2,64,256]{2,1,0:T(8,128)S(1)} %collective-permute-done.2.late_core, f32[4,128,256]{2,1,0:T(8,128)S(1)} %bitcast.9, ...), custom_call_target="tpu_custom_call" | custom-call | flops 1000000 | bytes 100000 | tf_op jit(solution)/shard_map/pallas_call | solution.py:462
  30.2 0.0 collective-permute-done.11.others_1_
  30.2 1.1 %collective-permute-done.10.others_0_ = f32[64,128]{1,0:T(8,128)S(1)} collective-permute-done((f32[64,128]{1,0:T(8,128)S(1)}, f32[64,128]{1,0:T(8,128)S(1)}, u32[]{:S(2)}, u32[]{:S(2)}) %collective-permute-start.10) | collective-permute-done | bytes 32800 | tf_op jit(solution)/shard_map/ppermute | solution.py:585
  31.3 0.5 %collective-permute-done.9.received = f32[64,128]{1,0:T(8,128)S(1)} collective-permute-done((f32[64,128]{1,0:T(8,128)S(1)}, f32[64,128]{1,0:T(8,128)S(1)}, u32[]{:S(2)}, u32[]{:S(2)}) %collective-permute-start.9) | collective-permute-done | bytes 32800 | tf_op jit(solution)/shard_map/ppermute | solution.py:479
  31.9 0.1 collective-permute-start.12
  31.9 1.2 %collective-permute-done.12.theirs = f32[72,128]{1,0:T(8,128)S(1)} collective-permute-done((f32[72,128]{1,0:T(8,128)S(1)}, f32[72,128]{1,0:T(8,128)S(1)}, u32[]{:S(2)}, u32[]{:S(2)}) %collective-permute-start.12) | collective-permute-done | bytes 36896 | tf_op jit(solution)/shard_map/ppermute | solution.py:479
  33.1 0.0 copy-done.5
  33.1 0.0 copy-done.6
  33.1 5.2 %shard_map.137 = (f32[4,128,256]{2,1,0:T(8,128)}, f32[128,128]{1,0:T(8,128)}) custom-call(f32[128,128]{1,0:T(8,128)S(1)} %bitcast.15, f32[128,128]{1,0:T(8,128)S(1)} %bitcast.17, f32[72,128]{1,0:T(8,128)S(1)} %shard_map.136.mine, f32[72,128]{1,0:T(8,128)S(1)} %collective-permute-done.12.theirs, f32[1024,256]{1,0:T(8,128)S(1)} %get-tuple-element.43.refs_0_, ...), custom_call_target="tpu_custom_call" | custom-call | flops 1000000 | bytes 100000 | tf_op jit(solution)/shard_map/pallas_call | solution.py:462
  (3 shorter events, 0.0 us)
Async XLA Ops:
  1.6 9.9 %collective-permute-start = (f32[4,64,256]{2,1,0:T(8,128)S(1)}, f32[4,64,256]{2,1,0:T(8,128)S(1)}, u32[]{:S(2)}, u32[]{:S(2)}) collective-permute-start(f32[4,64,256]{2,1,0:T(8,128)S(1)} %shard_map.131.refs_3_), channel_id=1, source_target_pairs={{0,30},{2,4},{4,2},{6,8},{8,6},{10,12},{12,10},{14,16},{16,14},{18... | collective-permute-start | bytes 786440 | tf_op jit(solution)/shard_map/ppermute | solution.py:475
  7.1 3.4 %copy-start = (f32[1,4,128,256]{3,2,1,0:T(8,128)S(1)}, f32[1,4,128,256]{3,2,1,0:T(8,128)}, u32[]{:S(2)}) copy-start(f32[1,4,128,256]{3,2,1,0:T(8,128)} %param.12) | copy-start | bytes 1572868
  7.1 3.4 %copy-start.4 = (bf16[256,384]{1,0:T(8,128)(2,1)S(1)}, bf16[256,384]{1,0:T(8,128)(2,1)}, u32[]{:S(2)}) copy-start(bf16[256,384]{1,0:T(8,128)(2,1)} %constant.23.clone.refs_0_.refs_4_) | copy-start | bytes 589828
  7.1 4.4 %copy-start.1 = (bf16[768,1024]{1,0:T(8,128)(2,1)S(1)}, bf16[768,1024]{1,0:T(8,128)(2,1)}, u32[]{:S(2)}) copy-start(bf16[768,1024]{1,0:T(8,128)(2,1)} %constant.19.clone.refs_0_.refs_6_) | copy-start | bytes 4718596
  7.1 4.4 %copy-start.2 = (bf16[512,768]{1,0:T(8,128)(2,1)S(1)}, bf16[512,768]{1,0:T(8,128)(2,1)}, u32[]{:S(2)}) copy-start(bf16[512,768]{1,0:T(8,128)(2,1)} %constant.20.clone.refs_1_.refs_7_) | copy-start | bytes 2359300
  7.1 4.4 %copy-start.3 = (f32[1,4,128,256]{3,2,1,0:T(8,128)S(1)}, f32[1,4,128,256]{3,2,1,0:T(8,128)}, u32[]{:S(2)}) copy-start(f32[1,4,128,256]{3,2,1,0:T(8,128)} %param.13) | copy-start | bytes 1572868
  7.1 4.4 %copy-start.7 = (bf16[1536,768]{1,0:T(8,128)(2,1)S(1)}, bf16[1536,768]{1,0:T(8,128)(2,1)}, u32[]{:S(2)}) copy-start(bf16[1536,768]{1,0:T(8,128)(2,1)} %constant.21.clone.refs_2_) | copy-start | bytes 7077892
  7.2 4.4 %copy-start.8 = (bf16[656,864]{1,0:T(8,128)(2,1)S(1)}, bf16[656,864]{1,0:T(8,128)(2,1)}, u32[]{:S(2)}) copy-start(bf16[656,864]{1,0:T(8,128)(2,1)} %constant.22.clone.refs_3_) | copy-start | bytes 3400708
  9.9 1.5 %collective-permute-start.1 = (f32[2,64,256]{2,1,0:T(8,128)S(1)}, f32[2,64,256]{2,1,0:T(8,128)S(1)}, u32[]{:S(2)}, u32[]{:S(2)}) collective-permute-start(f32[2,64,256]{2,1,0:T(8,128)S(1)} %get-tuple-element.26), channel_id=1, source_target_pairs={{0,2},{2,0},{4,6},{6,4},{8,10},{10,8},{12,14},{14,12},{16,18},{18,... | collective-permute-start | bytes 393224 | tf_op jit(solution)/shard_map/ppermute | solution.py:479
  10.0 1.5 %collective-permute-start.2 = (f32[2,64,256]{2,1,0:T(8,128)S(1)}, f32[2,64,256]{2,1,0:T(8,128)S(1)}, u32[]{:S(2)}, u32[]{:S(2)}) collective-permute-start(f32[2,64,256]{2,1,0:T(8,128)S(1)} %get-tuple-element.27), channel_id=1, source_target_pairs={{0,2},{2,0},{4,6},{6,4},{8,10},{10,8},{12,14},{14,12},{16,18},{18,... | collective-permute-start | bytes 393224 | tf_op jit(solution)/shard_map/ppermute | solution.py:479
  11.0 17.2 %collective-permute-start.7 = (f32[8,64,256]{2,1,0:T(8,128)S(1)}, f32[8,64,256]{2,1,0:T(8,128)S(1)}, u32[]{:S(2)}, u32[]{:S(2)}) collective-permute-start(f32[8,64,256]{2,1,0:T(8,128)S(1)} %get-tuple-element.37), channel_id=1, source_target_pairs={{0,30},{2,4},{4,2},{6,8},{8,6},{10,12},{12,10},{14,16},{16,14},{18... | collective-permute-start | bytes 1572872 | tf_op jit(solution)/shard_map/ppermute | solution.py:475
  11.4 16.9 %collective-permute-start.8 = (f32[8,64,256]{2,1,0:T(8,128)S(1)}, f32[8,64,256]{2,1,0:T(8,128)S(1)}, u32[]{:S(2)}, u32[]{:S(2)}) collective-permute-start(f32[8,64,256]{2,1,0:T(8,128)S(1)} %get-tuple-element.38), channel_id=1, source_target_pairs={{0,2},{2,0},{4,6},{6,4},{8,10},{10,8},{12,14},{14,12},{16,18},{18,... | collective-permute-start | bytes 1572872 | tf_op jit(solution)/shard_map/ppermute | solution.py:479
  15.3 1.3 %collective-permute-start.3 = (f32[64,128]{1,0:T(8,128)S(1)}, f32[64,128]{1,0:T(8,128)S(1)}, u32[]{:S(2)}, u32[]{:S(2)}) collective-permute-start(f32[64,128]{1,0:T(8,128)S(1)} %get-tuple-element.36), channel_id=1, source_target_pairs={{0,2},{2,0},{4,6},{6,4},{8,10},{10,8},{12,14},{14,12},{16,18},{18,... | collective-permute-start | bytes 98312 | tf_op jit(solution)/shard_map/ppermute | solution.py:479
  16.6 5.7 %collective-permute-start.6 = (f32[64,128]{1,0:T(8,128)S(1)}, f32[64,128]{1,0:T(8,128)S(1)}, u32[]{:S(2)}, u32[]{:S(2)}) collective-permute-start(f32[64,128]{1,0:T(8,128)S(1)} %add.12), channel_id=1, source_target_pairs={{0,24},{2,26},{4,28},{6,30},{8,16},{10,18},{12,20},{14,22},{16,8},... | collective-permute-start | bytes 98312 | tf_op jit(solution)/shard_map/ppermute | solution.py:479
  19.9 4.8 %collective-permute-start.5 = (f32[64,128]{1,0:T(8,128)S(1)}, f32[64,128]{1,0:T(8,128)S(1)}, u32[]{:S(2)}, u32[]{:S(2)}) collective-permute-start(f32[64,128]{1,0:T(8,128)S(1)} %add.12), channel_id=1, source_target_pairs={{0,16},{2,18},{4,20},{6,22},{8,24},{10,26},{12,28},{14,30},{16,0},... | collective-permute-start | bytes 98312 | tf_op jit(solution)/shard_map/ppermute | solution.py:479
  19.9 4.8 %collective-permute-start.4 = (f32[64,128]{1,0:T(8,128)S(1)}, f32[64,128]{1,0:T(8,128)S(1)}, u32[]{:S(2)}, u32[]{:S(2)}) collective-permute-start(f32[64,128]{1,0:T(8,128)S(1)} %add.12), channel_id=1, source_target_pairs={{0,8},{2,10},{4,12},{6,14},{8,0},{10,2},{12,4},{14,6},{16,24},{18,... | collective-permute-start | bytes 98312 | tf_op jit(solution)/shard_map/ppermute | solution.py:479
  24.7 8.4 %copy-start.5 = (f32[1,128,128]{2,1,0:T(8,128)S(1)}, f32[1,128,128]{2,1,0:T(8,128)}, u32[]{:S(2)}) copy-start(f32[1,128,128]{2,1,0:T(8,128)} %param.14) | copy-start | bytes 196612
  24.7 8.4 %copy-start.6 = (f32[1,128,128]{2,1,0:T(8,128)S(1)}, f32[1,128,128]{2,1,0:T(8,128)}, u32[]{:S(2)}) copy-start(f32[1,128,128]{2,1,0:T(8,128)} %param.15) | copy-start | bytes 196612
  24.7 5.5 %collective-permute-start.11 = (f32[64,128]{1,0:T(8,128)S(1)}, f32[64,128]{1,0:T(8,128)S(1)}, u32[]{:S(2)}, u32[]{:S(2)}) collective-permute-start(f32[64,128]{1,0:T(8,128)S(1)} %add_add_fusion._.mine), channel_id=1, source_target_pairs={{0,5},{1,4},{2,7},{3,6},{4,1},{5,0},{6,3},{7,2},{8,13},{9,12},{10,... | collective-permute-start | bytes 98312 | tf_op jit(solution)/shard_map/ppermute | solution.py:484
  27.4 3.9 %collective-permute-start.10 = (f32[64,128]{1,0:T(8,128)S(1)}, f32[64,128]{1,0:T(8,128)S(1)}, u32[]{:S(2)}, u32[]{:S(2)}) collective-permute-start(f32[64,128]{1,0:T(8,128)S(1)} %add_add_fusion._.mine), channel_id=1, source_target_pairs={{0,1},{1,0},{2,3},{3,2},{4,5},{5,4},{6,7},{7,6},{8,9},{9,8},{10,11... | collective-permute-start | bytes 98312 | tf_op jit(solution)/shard_map/ppermute | solution.py:585
  27.9 3.9 %collective-permute-start.9 = (f32[64,128]{1,0:T(8,128)S(1)}, f32[64,128]{1,0:T(8,128)S(1)}, u32[]{:S(2)}, u32[]{:S(2)}) collective-permute-start(f32[64,128]{1,0:T(8,128)S(1)} %add_add_fusion._.mine), channel_id=1, source_target_pairs={{0,4},{2,6},{4,0},{6,2},{8,12},{10,14},{12,8},{14,10},{16,20},{18,... | collective-permute-start | bytes 98312 | tf_op jit(solution)/shard_map/ppermute | solution.py:479
  31.9 1.3 %collective-permute-start.12 = (f32[72,128]{1,0:T(8,128)S(1)}, f32[72,128]{1,0:T(8,128)S(1)}, u32[]{:S(2)}, u32[]{:S(2)}) collective-permute-start(f32[72,128]{1,0:T(8,128)S(1)} %shard_map.136.mine), channel_id=1, source_target_pairs={{0,2},{2,0},{4,6},{6,4},{8,10},{10,8},{12,14},{14,12},{16,18},{18,... | collective-permute-start | bytes 110600 | tf_op jit(solution)/shard_map/ppermute | solution.py:479
